TPU v7x, 512 devices: a whole 4x4x16 slice. The times are simulated.
512 devices in a mesh: gx: 16 (over y_hi, x, core), gy: 32 (over y_lo, z).
Axes of the slice: x: 4, y: 4 (y_hi: 2, y_lo: 2; y = y_hi * 2 + y_lo), z: 16, core: 2. Of those that a mesh axis runs over, the one named last changes fastest.
Arguments:
- weights: float32 [16, 32, 2048, 128], P('gx', 'gy'), may hold values from -1.8 to 1.8
- angles: bfloat16 [4, 16, 32, 2048, 128], P(None, 'gx', 'gy'), may hold values from -3.140625 to 3.140625
Outputs:
- transformed: float32 [16, 32, 2048, 128], P('gx', 'gy')
All inputs are finite; a program needn't handle non-finite values.
Results may differ from a plain program's by a relative error of at most 0.0003.
Values sent between devices are 32-bit elements; how exact they have to be, the bound alone decides.
No kernel may reach another device: no remote copies, remote signals or barrier semaphores. Data moves between devices by JAX's collectives and lax.ppermute only.
A program may use at most 128 MiB of HBM per device.

v0:
```python
import jax
import jax.numpy as jnp
import numpy as np
from jax import lax
from jax.sharding import PartitionSpec as P

P_SIZE = 8
LEVELS = 4


def from_partner(block, axis, bit):
    count = lax.axis_size(axis)
    route = []
    for low in range(count):
        high = low | 1 << bit
        if high != low and high < count:
            route += [(low, high), (high, low)]
    return lax.ppermute(block, axis, route)


def child_tables(degree_count):
    cheb_nodes = np.cos((2.0 * np.arange(degree_count) + 1.0) * np.pi / (2.0 * degree_count))
    lagrange = np.ones((2, degree_count, degree_count))
    for parity in range(2):
        points = (cheb_nodes + (2.0 * parity - 1.0)) / 2.0
        for target in range(degree_count):
            for source in range(degree_count):
                for others in range(degree_count):
                    if others != source:
                        lagrange[parity, target, source] *= (
                            points[target] - cheb_nodes[others]
                        ) / (cheb_nodes[source] - cheb_nodes[others])
    return lagrange


def level_plan(count_x, count_y):
    bits_x = count_x.bit_length() - 1
    bits_y = count_y.bit_length() - 1
    return [(0, bits_x - 1), (1, bits_y - 1), (0, bits_x - 2), (1, bits_y - 2)]


def spread_table(lagrange, grid_axis):
    square = P_SIZE * P_SIZE
    columns = []
    for parity in range(2):
        if grid_axis == 0:
            inner = np.kron(lagrange[parity].T, np.eye(P_SIZE))
        else:
            inner = np.kron(np.eye(P_SIZE), lagrange[parity].T)
        plain = np.kron(np.eye(2), inner)
        columns.append(plain)
        columns.append(np.roll(plain, square, axis=1))
    return jnp.asarray(np.concatenate(columns, axis=1), jnp.float32)


def angle_table():
    square = P_SIZE * P_SIZE
    select = np.zeros((2 * square, 4 * square))
    for child in range(2):
        for place in range(square):
            select[child * square + place, child * 2 * square + place] = 1.0
            select[child * square + place, child * 2 * square + square + place] = 1.0
    return jnp.asarray(select, jnp.float32)


def spread_rows(blocks, table):
    spread = jnp.dot(
        blocks, table, precision=lax.Precision.HIGHEST, preferred_element_type=jnp.float32
    )
    return spread.reshape(2 * blocks.shape[0], table.shape[1] // 2)


def rotate(pair, cosine, sine_part):
    width = cosine.shape[-1]
    return pair[:, :width] * cosine + pair[:, width:] * sine_part


def partner_rows(payload, grid_axis, bit_num):
    if grid_axis == 0:
        return from_partner(payload, "gx", bit_num)
    return from_partner(payload, "gy", bit_num)


def shards(weights, angles):
    weights_now = weights[0, 0]
    box_rows = weights_now.shape[0]
    half_rows = box_rows // 2
    square = P_SIZE * P_SIZE
    width = 2 * square
    lagrange = child_tables(P_SIZE)
    tables = [spread_table(lagrange, 0), spread_table(lagrange, 1)]
    select = angle_table()
    signs = jnp.concatenate([-jnp.ones((square,), jnp.float32), jnp.ones((square,), jnp.float32)])
    plan = level_plan(lax.axis_size("gx"), lax.axis_size("gy"))
    index_x = lax.axis_index("gx")
    index_y = lax.axis_index("gy")
    for level_num in range(LEVELS):
        grid_axis, bit_num = plan[level_num]
        table = tables[grid_axis]
        own_index = index_x if grid_axis == 0 else index_y
        upper_side = own_index >> bit_num & 1 == 1
        kept_rows = jnp.where(upper_side, weights_now[half_rows:], weights_now[:half_rows])
        given_rows = jnp.where(upper_side, weights_now[:half_rows], weights_now[half_rows:])
        doubled = jnp.dot(
            angles[level_num, 0, 0].astype(jnp.float32),
            select,
            precision=lax.Precision.HIGHEST,
            preferred_element_type=jnp.float32,
        )
        cos_all = jnp.cos(doubled)
        sin_all = jnp.sin(doubled)
        near_cos = jnp.where(upper_side, cos_all[:, width:], cos_all[:, :width])
        near_sin = jnp.where(upper_side, sin_all[:, width:], sin_all[:, :width]) * signs
        far_cos = jnp.where(upper_side, cos_all[:, :width], cos_all[:, width:])
        far_sin = jnp.where(upper_side, sin_all[:, :width], sin_all[:, width:]) * signs
        arrived = partner_rows(given_rows, grid_axis, bit_num)
        local_term = rotate(spread_rows(kept_rows, table), near_cos, near_sin)
        incoming = rotate(spread_rows(arrived, table), far_cos, far_sin)
        weights_now = local_term + incoming
    return weights_now.reshape(1, 1, box_rows, width)


def solution(mesh):
    return jax.shard_map(
        shards,
        mesh=mesh,
        in_specs=(P("gx", "gy", None, None), P(None, "gx", "gy", None, None)),
        out_specs=P("gx", "gy", None, None),
        check_vma=False,
    )
```

profile of v0, /device:TPU:38, one launch (start us, length us, event | category | flops | bytes accessed | tf_op | source)
XLA Modules:
  0.0 240.4 jit_solution(7913512959996992225)
XLA Ops:
  2.1 5.2 %collective-permute-start = (f32[1024,128]{1,0:T(8,128)}, f32[1024,128]{1,0:T(8,128)}, u32[]{:S(2)}, u32[]{:S(2)}) collective-permute-start(f32[1024,128]{1,0:T(8,128)} %select_bitcast_fusion), channel_id=1, source_target_pairs={{0,256},{256,0},{32,288},{288,32},{64,320},{320,64},{96,352},{352,... | collective-permute-start | bytes 1572872 | tf_op jit(solution)/shard_map/ppermute | solution.py:18
  7.3 10.9 %cosine_bitcast_fusion.3 = (f32[2048,256]{0,1:T(8,128)}, f32[2048,256]{0,1:T(8,128)}) fusion(f32[128,256]{1,0:T(8,128)} %constant.28.clone, bf16[4,1,1,2048,128]{4,3,2,1,0:T(8,128)(2,1)} %param.6), kind=kOutput, calls=%fused_computation.7 | convolution fusion | flops 805306368 | bytes 4849664 | tf_op jit(solution)/shard_map/dot_general | solution.py:104
  18.2 11.0 %cosine_bitcast_fusion.2 = (f32[2048,256]{0,1:T(8,128)}, f32[2048,256]{0,1:T(8,128)}) fusion(f32[128,256]{1,0:T(8,128)S(1)} %copy-done.5, bf16[4,1,1,2048,128]{4,3,2,1,0:T(8,128)(2,1)} %param.6), kind=kOutput, calls=%fused_computation.5 | convolution fusion | flops 805306368 | bytes 4849664 | tf_op jit(solution)/shard_map/dot_general | solution.py:104
  29.1 3.1 %fusion.8 = f32[1024,512]{1,0:T(8,128)} fusion(f32[128,512]{1,0:T(8,128)S(1)} %copy-done.2, f32[1,1,2048,128]{3,2,1,0:T(8,128)S(1)} %copy-done.4, pred[]{:T(512)S(6)} %eq.15), kind=kOutput, calls=%fused_computation.20 | convolution fusion | flops 805437440 | bytes 3407873 | tf_op jit(solution)/shard_map/dot_general | solution.py:67
  38.5 10.8 %cosine_bitcast_fusion.1 = (f32[2048,256]{0,1:T(8,128)}, f32[2048,256]{0,1:T(8,128)}) fusion(f32[128,256]{1,0:T(8,128)S(1)} %copy-done.5, bf16[4,1,1,2048,128]{4,3,2,1,0:T(8,128)(2,1)} %param.6), kind=kOutput, calls=%fused_computation.3 | convolution fusion | flops 805306368 | bytes 4849664 | tf_op jit(solution)/shard_map/dot_general | solution.py:104
  49.3 10.6 %cosine_bitcast_fusion = (f32[2048,256]{0,1:T(8,128)S(1)}, f32[2048,256]{0,1:T(8,128)}) fusion(f32[128,256]{1,0:T(8,128)S(1)} %copy-done.5, bf16[4,1,1,2048,128]{4,3,2,1,0:T(8,128)(2,1)} %param.6), kind=kOutput, calls=%fused_computation.1 | convolution fusion | flops 805306368 | bytes 4849664 | tf_op jit(solution)/shard_map/dot_general | solution.py:104
  59.9 4.1 %fusion.49 = f32[1024,512]{1,0:T(8,128)} fusion(f32[1024,128]{1,0:T(8,128)} %collective-permute-done, f32[128,512]{1,0:T(8,128)S(1)} %copy-done.2), kind=kOutput, calls=%fused_computation.57 | convolution fusion | flops 805306368 | bytes 2883584 | tf_op jit(solution)/shard_map/dot_general | solution.py:67
  74.9 4.1 %add_add_fusion.2 = f32[2048,128]{0,1:T(8,128)S(1)} fusion(f32[2048,128]{0,1:T(8,128)} %copy.29, f32[2048,128]{0,1:T(8,128)} %copy.28, f32[2048,128]{0,1:T(8,128)} %copy.27, f32[2048,256]{0,1:T(8,128)} %get-tuple-element.24, f32[2048,128]{0,1:T(8,128)S(1)} %copy.26, f32[2048,256]{0,1:T(8,128)} %get-tuple-element.23, f32[128]{0:T(128)S(1)} %copy-done.6, ...), kind=kLoop, calls=%fused_computation.11 | loop fusion | flops 3407872 | bytes 9437697 | tf_op jit(solution)/shard_map/add | solution.py:119
  82.4 3.2 %fusion.17 = f32[1024,512]{1,0:T(8,128)} fusion(f32[128,512]{1,0:T(8,128)S(1)} %copy-done.1, f32[2048,128]{0,1:T(8,128)S(1)} %add_add_fusion.2, pred[]{:T(512)S(6)} %eq.14), kind=kOutput, calls=%fused_computation.29 | convolution fusion | flops 805437440 | bytes 3407873 | tf_op jit(solution)/shard_map/dot_general | solution.py:67
  88.3 3.1 %fusion.37 = (f32[2048,128]{1,0:T(8,128)}, f32[2048,128]{1,0:T(8,128)}) fusion(f32[2048,256]{1,0:T(8,128)} %reshape.35), kind=kLoop, calls=%fused_computation.53 | loop fusion | bytes 4194304 | tf_op jit(solution)/shard_map/slice | solution.py:75
  95.5 4.2 %fusion.50 = f32[1024,512]{1,0:T(8,128)} fusion(f32[1024,128]{0,1:T(8,128)} %collective-permute-done.1, f32[128,512]{1,0:T(8,128)S(1)} %copy-done.1), kind=kOutput, calls=%fused_computation.58 | convolution fusion | flops 805306368 | bytes 2883584 | tf_op jit(solution)/shard_map/dot_general | solution.py:67
  110.5 4.1 %add_add_fusion.1 = f32[2048,128]{0,1:T(8,128)S(1)} fusion(f32[2048,128]{0,1:T(8,128)} %copy.33, f32[2048,128]{0,1:T(8,128)} %copy.32, f32[2048,128]{0,1:T(8,128)} %copy.31, f32[2048,256]{0,1:T(8,128)} %get-tuple-element.18, f32[2048,128]{0,1:T(8,128)S(1)} %copy.30, f32[2048,256]{0,1:T(8,128)} %get-tuple-element.17, f32[128]{0:T(128)S(1)} %copy-done.6, ...), kind=kLoop, calls=%fused_computation.10 | loop fusion | flops 3407872 | bytes 9437697 | tf_op jit(solution)/shard_map/add | solution.py:119
  115.5 3.2 %fusion.14 = f32[1024,512]{1,0:T(8,128)} fusion(f32[128,512]{1,0:T(8,128)S(1)} %copy-done.3, f32[2048,128]{0,1:T(8,128)S(1)} %add_add_fusion.1, pred[]{:T(512)S(6)} %eq.13), kind=kOutput, calls=%fused_computation.26 | convolution fusion | flops 805437440 | bytes 3407873 | tf_op jit(solution)/shard_map/dot_general | solution.py:67
  118.7 3.3 %collective-permute-start.2 = (f32[1024,128]{0,1:T(8,128)}, f32[1024,128]{0,1:T(8,128)}, u32[]{:S(2)}, u32[]{:S(2)}) collective-permute-start(f32[1024,128]{0,1:T(8,128)} %slice_select_fusion.1), channel_id=1, source_target_pairs={{0,128},{128,0},{32,160},{160,32},{64,192},{192,64},{96,224},{224,... | collective-permute-start | bytes 1572872 | tf_op jit(solution)/shard_map/ppermute | solution.py:18
  122.0 3.0 %reshape.37 = f32[2048,256]{1,0:T(8,128)} reshape(f32[1024,512]{1,0:T(8,128)} %fusion.14) | data formatting | bytes 4194304 | tf_op jit(solution)/shard_map/reshape | solution.py:70
  132.2 3.4 %collective-permute-done.2 = f32[1024,128]{0,1:T(8,128)} collective-permute-done((f32[1024,128]{0,1:T(8,128)}, f32[1024,128]{0,1:T(8,128)}, u32[]{:S(2)}, u32[]{:S(2)}) %collective-permute-start.2) | collective-permute-done | bytes 524320 | tf_op jit(solution)/shard_map/ppermute | solution.py:18
  135.5 4.3 %fusion.51 = f32[1024,512]{1,0:T(8,128)} fusion(f32[1024,128]{0,1:T(8,128)} %collective-permute-done.2, f32[128,512]{1,0:T(8,128)} %constant.26.clone), kind=kOutput, calls=%fused_computation.59 | convolution fusion | flops 805306368 | bytes 2883584 | tf_op jit(solution)/shard_map/dot_general | solution.py:67
  142.6 3.1 %fusion.36 = (f32[2048,128]{1,0:T(8,128)}, f32[2048,128]{1,0:T(8,128)}) fusion(f32[2048,256]{1,0:T(8,128)} %reshape.38), kind=kLoop, calls=%fused_computation.52 | loop fusion | bytes 4194304 | tf_op jit(solution)/shard_map/slice | solution.py:75
  150.8 4.1 %add_add_fusion = f32[2048,128]{0,1:T(8,128)S(1)} fusion(f32[2048,128]{0,1:T(8,128)} %copy.37, f32[2048,128]{0,1:T(8,128)} %copy.36, f32[2048,128]{0,1:T(8,128)} %copy.35, f32[2048,256]{0,1:T(8,128)} %get-tuple-element.12, f32[2048,128]{0,1:T(8,128)S(1)} %copy.34, f32[2048,256]{0,1:T(8,128)} %get-tuple-element.11, f32[128]{0:T(128)S(1)} %copy-done.6, pred[]{:T(512)S(6)} %eq.13), kind=kLoop, calls=%fused_computation.9 | loop fusion | flops 3407872 | bytes 9437697 | tf_op jit(solution)/shard_map/add | solution.py:119
  155.7 3.1 %fusion.11 = f32[1024,512]{1,0:T(8,128)} fusion(f32[128,512]{1,0:T(8,128)S(1)} %copy-done.1, f32[2048,128]{0,1:T(8,128)S(1)} %add_add_fusion, pred[]{:T(512)S(6)} %eq.12), kind=kOutput, calls=%fused_computation.23 | convolution fusion | flops 805437440 | bytes 3407873 | tf_op jit(solution)/shard_map/dot_general | solution.py:67
  158.8 14.8 %collective-permute-start.3 = (f32[1024,128]{0,1:T(8,128)}, f32[1024,128]{0,1:T(8,128)}, u32[]{:S(2)}, u32[]{:S(2)}) collective-permute-start(f32[1024,128]{0,1:T(8,128)} %slice_select_fusion), channel_id=1, source_target_pairs={{0,8},{8,0},{1,9},{9,1},{2,10},{10,2},{3,11},{11,3},{4,12},{12,4},... | collective-permute-start | bytes 1572872 | tf_op jit(solution)/shard_map/ppermute | solution.py:18
  183.5 34.9 %collective-permute-done.3 = f32[1024,128]{0,1:T(8,128)} collective-permute-done((f32[1024,128]{0,1:T(8,128)}, f32[1024,128]{0,1:T(8,128)}, u32[]{:S(2)}, u32[]{:S(2)}) %collective-permute-start.3) | collective-permute-done | bytes 524320 | tf_op jit(solution)/shard_map/ppermute | solution.py:18
  218.4 4.2 %fusion.52 = f32[1024,512]{1,0:T(8,128)} fusion(f32[1024,128]{0,1:T(8,128)} %collective-permute-done.3, f32[128,512]{1,0:T(8,128)S(1)} %copy-done.1), kind=kOutput, calls=%fused_computation.60 | convolution fusion | flops 805306368 | bytes 2883584 | tf_op jit(solution)/shard_map/dot_general | solution.py:67
  233.4 4.4 %add_bitcast_fusion = f32[1,1,2048,128]{2,3,1,0:T(8,128)} fusion(f32[2048,128]{0,1:T(8,128)} %copy.41, f32[2048,128]{0,1:T(8,128)} %copy.40, f32[2048,128]{0,1:T(8,128)} %copy.39, f32[2048,256]{0,1:T(8,128)} %get-tuple-element.6, f32[2048,128]{0,1:T(8,128)S(1)} %copy.38, f32[2048,256]{0,1:T(8,128)S(1)} %get-tuple-element.5, f32[128]{0:T(128)S(1)} %copy-done.6, ...), kind=kLoop, calls=%fused_computation.8 | loop fusion | flops 3407872 | bytes 9437697 | tf_op jit(solution)/shard_map/reshape | solution.py:120
  (51 shorter events, 80.0 us)
Async XLA Ops:
  2.1 16.1 %copy-start.5 = (f32[128,256]{1,0:T(8,128)S(1)}, f32[128,256]{1,0:T(8,128)}, u32[]{:S(2)}) copy-start(f32[128,256]{1,0:T(8,128)} %constant.28.clone) | copy-start | bytes 393220
  2.1 57.9 %collective-permute-start = (f32[1024,128]{1,0:T(8,128)}, f32[1024,128]{1,0:T(8,128)}, u32[]{:S(2)}, u32[]{:S(2)}) collective-permute-start(f32[1024,128]{1,0:T(8,128)} %select_bitcast_fusion), channel_id=1, source_target_pairs={{0,256},{256,0},{32,288},{288,32},{64,320},{320,64},{96,352},{352,... | collective-permute-start | bytes 1572872 | tf_op jit(solution)/shard_map/ppermute | solution.py:18
  18.2 11.0 %copy-start.2 = (f32[128,512]{1,0:T(8,128)S(1)}, f32[128,512]{1,0:T(8,128)}, u32[]{:S(2)}) copy-start(f32[128,512]{1,0:T(8,128)} %constant.26.clone) | copy-start | bytes 786436
  18.2 11.0 %copy-start.4 = (f32[1,1,2048,128]{3,2,1,0:T(8,128)S(1)}, f32[1,1,2048,128]{3,2,1,0:T(8,128)}, u32[]{:S(2)}) copy-start(f32[1,1,2048,128]{3,2,1,0:T(8,128)} %param.5) | copy-start | bytes 3145732
  35.5 1.7 copy-start
  69.8 5.1 %copy-start.6 = (f32[128]{0:T(128)S(1)}, f32[128]{0:T(128)}, u32[]{:S(2)}) copy-start(f32[128]{0:T(128)} %constant.25.clone.1) | copy-start | bytes 1540
  74.9 7.5 %copy-start.1 = (f32[128,512]{1,0:T(8,128)S(1)}, f32[128,512]{1,0:T(8,128)}, u32[]{:S(2)}) copy-start(f32[128,512]{1,0:T(8,128)} %constant.27.clone) | copy-start | bytes 786436
  79.8 15.7 %collective-permute-start.1 = (f32[1024,128]{0,1:T(8,128)}, f32[1024,128]{0,1:T(8,128)}, u32[]{:S(2)}, u32[]{:S(2)}) collective-permute-start(f32[1024,128]{0,1:T(8,128)} %slice_select_fusion.2), channel_id=1, source_target_pairs={{0,16},{16,0},{1,17},{17,1},{2,18},{18,2},{3,19},{19,3},{4,20},{20... | collective-permute-start | bytes 1572872 | tf_op jit(solution)/shard_map/ppermute | solution.py:18
  110.5 5.0 %copy-start.3 = (f32[128,512]{1,0:T(8,128)S(1)}, f32[128,512]{1,0:T(8,128)}, u32[]{:S(2)}) copy-start(f32[128,512]{1,0:T(8,128)} %constant.26.clone) | copy-start | bytes 786436
  118.7 16.8 %collective-permute-start.2 = (f32[1024,128]{0,1:T(8,128)}, f32[1024,128]{0,1:T(8,128)}, u32[]{:S(2)}, u32[]{:S(2)}) collective-permute-start(f32[1024,128]{0,1:T(8,128)} %slice_select_fusion.1), channel_id=1, source_target_pairs={{0,128},{128,0},{32,160},{160,32},{64,192},{192,64},{96,224},{224,... | collective-permute-start | bytes 1572872 | tf_op jit(solution)/shard_map/ppermute | solution.py:18
  158.8 59.6 %collective-permute-start.3 = (f32[1024,128]{0,1:T(8,128)}, f32[1024,128]{0,1:T(8,128)}, u32[]{:S(2)}, u32[]{:S(2)}) collective-permute-start(f32[1024,128]{0,1:T(8,128)} %slice_select_fusion), channel_id=1, source_target_pairs={{0,8},{8,0},{1,9},{9,1},{2,10},{10,2},{3,11},{11,3},{4,12},{12,4},... | collective-permute-start | bytes 1572872 | tf_op jit(solution)/shard_map/ppermute | solution.py:18
where the time goes:
time: 242 us; the launch traced here: 240 us
  local copies, waits for them, and re-layouts  82 us (34%)
  matrix products  72.8 us (30%)
  waiting for transfers between devices  38.3 us (16%)
  starting transfers between devices  25.9 us (11%)
  other arithmetic  21.3 us (9%)
    dot_general x4, matrix products, shards(): jnp.dot(angles[level_num, 0, 0].astype(jnp.float32), select, precision=la...  43.3 us
    ppermute x4, waiting for transfers between devices, from_partner(): return lax.ppermute(block, axis, route)  38.3 us
    unnamed x30, local copies, waits for them, and re-layouts  35.6 us
    dot_general x8, matrix products, spread_rows(): jnp.dot(blocks, table, precision=lax.Precision.HIGHEST, preferred_element...  29.5 us
    ppermute x4, starting transfers between devices, from_partner(): return lax.ppermute(block, axis, route)  25.9 us
    slice x8, local copies, waits for them, and re-layouts, rotate(): return pair[:, :width] * cosine + pair[:, width:] * sine_part  22.6 us
    reshape x8, local copies, waits for them, and re-layouts, spread_rows(): return spread.reshape(2 * blocks.shape[0], table.shape[1] // 2)  21.3 us
    add x3, other arithmetic, shards(): weights_now = local_term + incoming  12.3 us
  transfers between devices with their start and end apart: 4, of which 2 were waited for; matrix products, arithmetic and copies ran while one was open for 36% of the time, Pallas kernels for 0%

commit v1 on v0

v1 whole, which is shorter than its diff:
```python
import functools

import jax
import jax.numpy as jnp
import ml_dtypes
import numpy as np
from jax import lax
from jax.experimental import pallas as pl
from jax.experimental.pallas import tpu as pltpu
from jax.sharding import PartitionSpec as P

P_SIZE = 8
SQUARE = P_SIZE * P_SIZE
CH = 2 * SQUARE

def half_angle_polys():
    nodes = np.cos((2 * np.arange(64) + 1) * np.pi / 128)
    top = 3.15**2
    u = (nodes + 1) / 2 * top
    x = np.sqrt(u)
    fit = np.polynomial.chebyshev.Chebyshev.fit
    power = np.polynomial.Polynomial
    sine = fit(u, np.sin(x / 2) / x, 5, domain=[0, top]).convert(kind=power)
    cosine = fit(u, 2 * np.cos(x / 2), 6, domain=[0, top]).convert(kind=power)
    return [float(v) for v in sine.coef], [float(v) for v in cosine.coef]


SINE, COSINE = half_angle_polys()


def horner(coef, u):
    total = jnp.full_like(u, coef[-1])
    for c in coef[-2::-1]:
        total = total * u + c
    return total


def cos_sin(x):
    u = x * x
    s = x * horner(SINE, u)
    c2 = horner(COSINE, u)
    return 1.0 - 2.0 * (s * s), s * c2


def child_tables(degree_count):
    cheb_nodes = np.cos((2.0 * np.arange(degree_count) + 1.0) * np.pi / (2.0 * degree_count))
    lagrange = np.ones((2, degree_count, degree_count))
    for parity in range(2):
        points = (cheb_nodes + (2.0 * parity - 1.0)) / 2.0
        for target in range(degree_count):
            for source in range(degree_count):
                for others in range(degree_count):
                    if others != source:
                        lagrange[parity, target, source] *= (
                            points[target] - cheb_nodes[others]
                        ) / (cheb_nodes[source] - cheb_nodes[others])
    return lagrange


def spread_tables(grid_axis):
    lagrange = child_tables(P_SIZE).astype(np.float32)
    table = np.zeros((2, 2, 2, SQUARE, 2, 2, 2, SQUARE), np.float32)
    for a in range(2):
        if grid_axis == 0:
            inner = np.kron(lagrange[a].T, np.eye(P_SIZE, dtype=np.float32))
        else:
            inner = np.kron(np.eye(P_SIZE, dtype=np.float32), lagrange[a].T)
        for h in range(2):
            for slot in range(2):
                for part in range(2):
                    table[h, slot, part, :, a, part, slot ^ h, :] = inner
    table = table.reshape(2, 2 * CH, 4 * CH)
    high = table.astype(ml_dtypes.bfloat16)
    low = (table - high.astype(np.float32)).astype(ml_dtypes.bfloat16)
    return high, low


def level_kernel(tile, scal, own, arr, ang, high, low, out, scratch):
    rows = own.shape[0]
    lane = lax.broadcasted_iota(jnp.int32, (tile, CH), 1)
    left = lane < SQUARE

    def one(i):
        base = i * tile
        x = jnp.concatenate([own[pl.ds(base, tile), :], arr[pl.ds(base, tile), :]], axis=1)
        x_hi = x.astype(jnp.bfloat16)
        x_lo = (x - x_hi.astype(jnp.float32)).astype(jnp.bfloat16)
        dot = functools.partial(jnp.dot, preferred_element_type=jnp.float32)
        y = dot(x_hi, high[...]) + (dot(x_lo, high[...]) + dot(x_hi, low[...]))
        scratch[...] = ang[pl.ds(2 * base, 2 * tile), :].astype(jnp.float32)
        for a in range(2):
            c, s = cos_sin(scratch[pl.ds(a, tile, stride=2), :])
            re = y[:, 2 * a * CH : (2 * a + 1) * CH]
            im = y[:, (2 * a + 1) * CH : (2 * a + 2) * CH]
            u = c * re - s * im
            v = s * re + c * im
            mixed = jnp.where(left, u, v) + pltpu.roll(jnp.where(left, v, u), SQUARE, 1)
            out[pl.ds(2 * base + a, tile, stride=2), :] = mixed

    if rows == tile:
        one(0)
    else:
        pl.loop(0, rows // tile)(lambda i: one(pl.multiple_of(i, 1)))


def level_call(scal, own, own_spec, arr, arr_spec, ang, ang_spec, tables, out_shape, out_spec, grid):
    rows = own_spec[0][-2]
    tile = min(rows, 128)
    side = lambda g, sc: (sc[0], 0, 0)
    total = 1
    for n in out_shape:
        total *= n
    return pl.pallas_call(
        functools.partial(level_kernel, tile),
        out_shape=jax.ShapeDtypeStruct(out_shape, jnp.float32),
        grid_spec=pltpu.PrefetchScalarGridSpec(
            num_scalar_prefetch=1,
            grid=(grid,),
            in_specs=[
                pl.BlockSpec(*own_spec),
                pl.BlockSpec(*arr_spec),
                pl.BlockSpec(*ang_spec),
                pl.BlockSpec((None, 2 * CH, 4 * CH), side),
                pl.BlockSpec((None, 2 * CH, 4 * CH), side),
            ],
            out_specs=pl.BlockSpec(*out_spec),
            scratch_shapes=[pltpu.VMEM((2 * tile, CH), jnp.float32)],
        ),
        compiler_params=pltpu.CompilerParams(vmem_limit_bytes=16 * 1024 * 1024),
        cost_estimate=pl.CostEstimate(
            flops=total * 4 * CH * 2 * 3, bytes_accessed=total * 4 * 3, transcendentals=0
        ),
    )(scal, own, arr, ang, *tables)


def from_partner(block, axis, bit):
    count = lax.axis_size(axis)
    route = [(low, low ^ (1 << bit)) for low in range(count)]
    return lax.ppermute(block, axis, route)


def shards(weights, angles):
    count_x, count_y = lax.axis_size("gx"), lax.axis_size("gy")
    bits_x, bits_y = count_x.bit_length() - 1, count_y.bit_length() - 1
    boxes = weights.shape[2]
    base = boxes // 16
    index_x, index_y = lax.axis_index("gx"), lax.axis_index("gy")
    h0 = index_x >> (bits_x - 1) & 1
    h1 = index_y >> (bits_y - 1) & 1
    h2 = index_x >> (bits_x - 2) & 1
    h3 = index_y >> (bits_y - 2) & 1
    tab_x = [jnp.asarray(t) for t in spread_tables(0)]
    tab_y = [jnp.asarray(t) for t in spread_tables(1)]
    w6 = weights.reshape(2, 2, 2, 2, base, CH)
    ang0 = angles.reshape(4, 2, 2, 2, 2 * base, CH)
    ang1 = angles.reshape(4, 2, 2, 4 * base, CH)
    ang2 = angles.reshape(4, 2, 8 * base, CH)
    ang3 = angles.reshape(4, 16 * base, CH)

    def pack(*values):
        return jnp.stack([jnp.asarray(v, jnp.int32) for v in values])

    def first(chunk, sel):
        at, n = chunk
        z = jnp.int32(0)
        taken = lax.dynamic_slice(
            w6, (1 - h0, z, z, sel, jnp.int32(at), z), (1, 2, 2, 1, n, CH)
        )
        return from_partner(taken.reshape(2, 2, n, CH), "gx", bits_x - 1)

    def level0(chunk, sel, arr, t1):
        at, n = chunk
        k = at // n
        return level_call(
            pack(h0, t1, sel), w6,
            ((None, None, None, None, n, CH), lambda g, sc: (sc[0], sc[1], g, sc[2], k, 0)),
            arr, ((None, None, n, CH), lambda g, sc: (sc[1], g, 0, 0)),
            ang0, ((None, None, None, None, 2 * n, CH), lambda g, sc: (0, sc[1], g, sc[2], k, 0)),
            tab_x, (2, 2 * n, CH), ((None, 2 * n, CH), lambda g, sc: (g, 0, 0)), 2,
        )

    def level1(chunk, sel, own, arr, t2):
        at, n = chunk
        k = at // n
        return level_call(
            pack(h1, t2, sel), own, ((None, n, CH), lambda g, sc: (sc[1], g, 0)),
            arr, ((None, n, CH), lambda g, sc: (sc[1], g, 0)),
            ang1, ((None, None, None, 2 * n, CH), lambda g, sc: (1, sc[1], sc[2], 2 * k + g, 0)),
            tab_y, (4 * n, CH), ((2 * n, CH), lambda g, sc: (g, 0)), 2,
        )

    def level2(chunk, sel, own, arr):
        at, n = chunk
        k = at // n
        return level_call(
            pack(h2, sel), own, ((n, CH), lambda g, sc: (g, 0)),
            arr, ((n, CH), lambda g, sc: (g, 0)),
            ang2, ((None, None, 2 * n, CH), lambda g, sc: (2, sc[1], 4 * k + g, 0)),
            tab_x, (8 * n, CH), ((2 * n, CH), lambda g, sc: (g, 0)), 4,
        )

    def level3(own, arrs, n):
        arr = jnp.concatenate(arrs, axis=0)
        rows = own.shape[0]
        return level_call(
            pack(h3), own, ((n, CH), lambda g, sc: (g, 0)),
            arr, ((n, CH), lambda g, sc: (g, 0)),
            ang3, ((None, 2 * n, CH), lambda g, sc: (3, g, 0)),
            tab_y, (2 * rows, CH), ((2 * n, CH), lambda g, sc: (g, 0)), rows // n,
        )

    def through(chunk, sel):
        arr = first(chunk, sel)
        send = level0(chunk, sel, arr, 1 - h1)
        arr1 = from_partner(send, "gy", bits_y - 1)
        keep = level0(chunk, sel, arr, h1)
        send = level1(chunk, sel, keep, arr1, 1 - h2)
        arr2 = from_partner(send, "gx", bits_x - 2)
        keep = level1(chunk, sel, keep, arr1, h2)
        return level2(chunk, sel, keep, arr2)

    chunks = [(0, base // 2), (base // 2, base // 2)]
    arrived = [
        from_partner(through(chunk, 1 - h3), "gy", bits_y - 2) for chunk in chunks
    ]
    kept = through((0, base), h3)
    out = level3(kept, arrived, base)
    return out.reshape(1, 1, boxes, CH)


def solution(mesh):
    return jax.shard_map(
        shards,
        mesh=mesh,
        in_specs=(P("gx", "gy", None, None), P(None, "gx", "gy", None, None)),
        out_specs=P("gx", "gy", None, None),
        check_vma=False,
    )
```

time: 242 us -> 115 us (0.48)
  the two profiles are of different devices: /device:TPU:38 before, /device:TPU:32 now
where the time goes in v1:
time: 115 us
  starting transfers between devices  50.2 us (44%)
  waiting for transfers between devices  30.6 us (27%)
  Pallas kernels  26.1 us (23%)
  local copies, waits for them, and re-layouts  6.91 us (6%)
    ppermute x11, starting transfers between devices, from_partner(): return lax.ppermute(block, axis, route)  50.2 us
    ppermute x11, waiting for transfers between devices, from_partner(): return lax.ppermute(block, axis, route)  30.6 us
    pallas_call x16, Pallas kernels, level_call(): pl.pallas_call(functools.partial(level_kernel, tile), out_shape=jax.Shape...  26.1 us
    unnamed x20, local copies, waits for them, and re-layouts  4.95 us
  transfers between devices with their start and end apart: 11, of which 2 were waited for; matrix products, arithmetic and copies ran while one was open for 1% of the time, Pallas kernels for 17%

profile of v1, /device:TPU:32, one launch (start us, length us, event | category | flops | bytes accessed | tf_op | source)
XLA Modules:
  0.0 114.8 jit_solution(15111574444410331523)
XLA Ops:
  1.0 5.1 %collective-permute-start.3 = (f32[2,2,64,128]{3,2,1,0:T(8,128)S(1)}, f32[2,2,64,128]{3,2,1,0:T(8,128)S(1)}, u32[]{:S(2)}, u32[]{:S(2)}) collective-permute-start(f32[2,2,64,128]{3,2,1,0:T(8,128)S(1)} %get-tuple-element.5), channel_id=1, source_target_pairs={{0,256},{32,288},{64,320},{96,352},{128,384},{160,416},{192,448},{... | collective-permute-start | bytes 393224 | tf_op jit(solution)/shard_map/ppermute | solution.py:139
  6.1 2.2 %collective-permute-start.7 = (f32[2,2,64,128]{3,2,1,0:T(8,128)S(1)}, f32[2,2,64,128]{3,2,1,0:T(8,128)S(1)}, u32[]{:S(2)}, u32[]{:S(2)}) collective-permute-start(f32[2,2,64,128]{3,2,1,0:T(8,128)S(1)} %get-tuple-element.6), channel_id=1, source_target_pairs={{0,256},{32,288},{64,320},{96,352},{128,384},{160,416},{192,448},{... | collective-permute-start | bytes 393224 | tf_op jit(solution)/shard_map/ppermute | solution.py:139
  9.3 5.1 %collective-permute-start = (f32[2,2,128,128]{3,2,1,0:T(8,128)S(1)}, f32[2,2,128,128]{3,2,1,0:T(8,128)S(1)}, u32[]{:S(2)}, u32[]{:S(2)}) collective-permute-start(f32[2,2,128,128]{3,2,1,0:T(8,128)S(1)} %dynamic-slice_bitcast_fusion), channel_id=1, source_target_pairs={{0,256},{32,288},{64,320},{96,352},{128,384},{160,416},{192,448},{... | collective-permute-start | bytes 786440 | tf_op jit(solution)/shard_map/ppermute | solution.py:139
  14.8 1.6 %copy-done = bf16[4,1,1,2048,128]{4,3,2,1,0:T(8,128)(2,1)S(1)} copy-done((bf16[4,1,1,2048,128]{4,3,2,1,0:T(8,128)(2,1)S(1)}, bf16[4,1,1,2048,128]{4,3,2,1,0:T(8,128)(2,1)}, u32[]{:S(2)}) %copy-start) | copy-done | bytes 2097176
  21.0 2.7 %collective-permute-start.4 = (f32[2,128,128]{2,1,0:T(8,128)S(1)}, f32[2,128,128]{2,1,0:T(8,128)S(1)}, u32[]{:S(2)}, u32[]{:S(2)}) collective-permute-start(f32[2,128,128]{2,1,0:T(8,128)S(1)} %shard_map.70), channel_id=1, source_target_pairs={{0,16},{1,17},{2,18},{3,19},{4,20},{5,21},{6,22},{7,23},{8,24},{9,... | collective-permute-start | bytes 393224 | tf_op jit(solution)/shard_map/ppermute | solution.py:139
  25.0 3.2 %collective-permute-start.8 = (f32[2,128,128]{2,1,0:T(8,128)S(1)}, f32[2,128,128]{2,1,0:T(8,128)S(1)}, u32[]{:S(2)}, u32[]{:S(2)}) collective-permute-start(f32[2,128,128]{2,1,0:T(8,128)S(1)} %shard_map.75), channel_id=1, source_target_pairs={{0,16},{1,17},{2,18},{3,19},{4,20},{5,21},{6,22},{7,23},{8,24},{9,... | collective-permute-start | bytes 393224 | tf_op jit(solution)/shard_map/ppermute | solution.py:139
  28.3 1.4 %shard_map.65 = f32[2,256,128]{2,1,0:T(8,128)S(1)} custom-call(s32[3]{0:T(128)S(1)} %pad_add_fusion.7.scal, f32[2,2,2,2,128,128]{5,4,3,2,1,0:T(8,128)S(1)} %bitcast.39, f32[2,2,128,128]{3,2,1,0:T(8,128)S(1)} %collective-permute-done.arr, bf16[4,2,2,2,256,128]{5,4,3,2,1,0:T(8,128)(2,1)S(1)} %bitcast.21, bf16[2,256,512]{2,1,0:T(8,128)(2,1)S(1)} %copy-done.6, ...), custom_call_target="tpu_custom_call" | custom-call | flops 201326592 | bytes 786432 | tf_op jit(solution)/shard_map/pallas_call | solution.py:113
  29.7 2.6 %collective-permute-start.1 = (f32[2,256,128]{2,1,0:T(8,128)S(1)}, f32[2,256,128]{2,1,0:T(8,128)S(1)}, u32[]{:S(2)}, u32[]{:S(2)}) collective-permute-start(f32[2,256,128]{2,1,0:T(8,128)S(1)} %shard_map.65), channel_id=1, source_target_pairs={{0,16},{1,17},{2,18},{3,19},{4,20},{5,21},{6,22},{7,23},{8,24},{9,... | collective-permute-start | bytes 786440 | tf_op jit(solution)/shard_map/ppermute | solution.py:139
  32.3 1.3 %shard_map.69.own = f32[2,128,128]{2,1,0:T(8,128)S(1)} custom-call(s32[3]{0:T(128)S(1)} %pad_add_fusion.12.scal, f32[2,2,2,2,128,128]{5,4,3,2,1,0:T(8,128)S(1)} %bitcast.40, f32[2,2,64,128]{3,2,1,0:T(8,128)S(1)} %collective-permute-done.3.arr, bf16[4,2,2,2,256,128]{5,4,3,2,1,0:T(8,128)(2,1)S(1)} %bitcast.22, bf16[2,256,512]{2,1,0:T(8,128)(2,1)S(1)} %copy-done.6, ...), custom_call_target="tpu_custom_call" | custom-call | flops 100663296 | bytes 393216 | tf_op jit(solution)/shard_map/pallas_call | solution.py:113
  33.6 1.3 %shard_map.74.own = f32[2,128,128]{2,1,0:T(8,128)S(1)} custom-call(s32[3]{0:T(128)S(1)} %pad_add_fusion.12.scal, f32[2,2,2,2,128,128]{5,4,3,2,1,0:T(8,128)S(1)} %bitcast.41, f32[2,2,64,128]{3,2,1,0:T(8,128)S(1)} %collective-permute-done.7.arr, bf16[4,2,2,2,256,128]{5,4,3,2,1,0:T(8,128)(2,1)S(1)} %bitcast.23, bf16[2,256,512]{2,1,0:T(8,128)(2,1)S(1)} %copy-done.6, ...), custom_call_target="tpu_custom_call" | custom-call | flops 100663296 | bytes 393216 | tf_op jit(solution)/shard_map/pallas_call | solution.py:113
  36.2 4.9 %collective-permute-start.9 = (f32[256,128]{1,0:T(8,128)S(1)}, f32[256,128]{1,0:T(8,128)S(1)}, u32[]{:S(2)}, u32[]{:S(2)}) collective-permute-start(f32[256,128]{1,0:T(8,128)S(1)} %shard_map.77), channel_id=1, source_target_pairs={{0,128},{32,160},{64,192},{96,224},{128,0},{160,32},{192,64},{224,... | collective-permute-start | bytes 393224 | tf_op jit(solution)/shard_map/ppermute | solution.py:139
  42.4 2.4 %collective-permute-start.5 = (f32[256,128]{1,0:T(8,128)S(1)}, f32[256,128]{1,0:T(8,128)S(1)}, u32[]{:S(2)}, u32[]{:S(2)}) collective-permute-start(f32[256,128]{1,0:T(8,128)S(1)} %shard_map.72), channel_id=1, source_target_pairs={{0,128},{32,160},{64,192},{96,224},{128,0},{160,32},{192,64},{224,... | collective-permute-start | bytes 393224 | tf_op jit(solution)/shard_map/ppermute | solution.py:139
  47.4 1.9 %shard_map.78 = f32[512,128]{1,0:T(8,128)S(1)} custom-call(s32[2]{0:T(128)S(1)} %pad_add_fusion.5.scal, f32[256,128]{1,0:T(8,128)S(1)} %shard_map.76.own, f32[256,128]{1,0:T(8,128)S(1)} %collective-permute-done.9.arr, bf16[4,2,1024,128]{3,2,1,0:T(8,128)(2,1)S(1)} %bitcast.28, bf16[2,256,512]{2,1,0:T(8,128)(2,1)S(1)} %copy-done.7, ...), custom_call_target="tpu_custom_call" | custom-call | flops 201326592 | bytes 786432 | tf_op jit(solution)/shard_map/pallas_call | solution.py:113
  49.4 15.0 %collective-permute-start.10 = (f32[512,128]{1,0:T(8,128)S(1)}, f32[512,128]{1,0:T(8,128)S(1)}, u32[]{:S(2)}, u32[]{:S(2)}) collective-permute-start(f32[512,128]{1,0:T(8,128)S(1)} %shard_map.78), channel_id=1, source_target_pairs={{0,8},{1,9},{2,10},{3,11},{4,12},{5,13},{6,14},{7,15},{8,0},{9,1},... | collective-permute-start | bytes 786440 | tf_op jit(solution)/shard_map/ppermute | solution.py:139
  64.4 1.9 %shard_map.73 = f32[512,128]{1,0:T(8,128)S(1)} custom-call(s32[2]{0:T(128)S(1)} %pad_add_fusion.5.scal, f32[256,128]{1,0:T(8,128)S(1)} %shard_map.71.own, f32[256,128]{1,0:T(8,128)S(1)} %collective-permute-done.5.arr, bf16[4,2,1024,128]{3,2,1,0:T(8,128)(2,1)S(1)} %bitcast.29, bf16[2,256,512]{2,1,0:T(8,128)(2,1)S(1)} %copy-done.7, ...), custom_call_target="tpu_custom_call" | custom-call | flops 201326592 | bytes 786432 | tf_op jit(solution)/shard_map/pallas_call | solution.py:113
  66.3 1.9 %collective-permute-start.6 = (f32[512,128]{1,0:T(8,128)S(1)}, f32[512,128]{1,0:T(8,128)S(1)}, u32[]{:S(2)}, u32[]{:S(2)}) collective-permute-start(f32[512,128]{1,0:T(8,128)S(1)} %shard_map.73), channel_id=1, source_target_pairs={{0,8},{1,9},{2,10},{3,11},{4,12},{5,13},{6,14},{7,15},{8,0},{9,1},... | collective-permute-start | bytes 786440 | tf_op jit(solution)/shard_map/ppermute | solution.py:139
  68.3 1.3 %shard_map.64.own = f32[2,256,128]{2,1,0:T(8,128)S(1)} custom-call(s32[3]{0:T(128)S(1)} %get-tuple-element.8.scal, f32[2,2,2,2,128,128]{5,4,3,2,1,0:T(8,128)S(1)} %bitcast.42, f32[2,2,128,128]{3,2,1,0:T(8,128)S(1)} %collective-permute-done.arr, bf16[4,2,2,2,256,128]{5,4,3,2,1,0:T(8,128)(2,1)S(1)} %bitcast.30, bf16[2,256,512]{2,1,0:T(8,128)(2,1)S(1)} %copy-done.7, ...), custom_call_target="tpu_custom_call" | custom-call | flops 201326592 | bytes 786432 | tf_op jit(solution)/shard_map/pallas_call | solution.py:113
  69.6 1.3 %shard_map.67 = f32[512,128]{1,0:T(8,128)S(1)} custom-call(s32[3]{0:T(128)S(1)} %get-tuple-element.7.scal, f32[2,256,128]{2,1,0:T(8,128)S(1)} %shard_map.64.own, f32[2,256,128]{2,1,0:T(8,128)S(1)} %collective-permute-done.1.arr, bf16[4,2,2,512,128]{4,3,2,1,0:T(8,128)(2,1)S(1)} %bitcast.31, bf16[2,256,512]{2,1,0:T(8,128)(2,1)S(1)} %copy-done.9, ...), custom_call_target="tpu_custom_call" | custom-call | flops 201326592 | bytes 786432 | tf_op jit(solution)/shard_map/pallas_call | solution.py:113
  71.0 4.9 %collective-permute-start.2 = (f32[512,128]{1,0:T(8,128)S(1)}, f32[512,128]{1,0:T(8,128)S(1)}, u32[]{:S(2)}, u32[]{:S(2)}) collective-permute-start(f32[512,128]{1,0:T(8,128)S(1)} %shard_map.67), channel_id=1, source_target_pairs={{0,128},{32,160},{64,192},{96,224},{128,0},{160,32},{192,64},{224,... | collective-permute-start | bytes 786440 | tf_op jit(solution)/shard_map/ppermute | solution.py:139
  76.1 1.3 %shard_map.66.own = f32[512,128]{1,0:T(8,128)S(1)} custom-call(s32[3]{0:T(128)S(1)} %pad_add_fusion.9.scal, f32[2,256,128]{2,1,0:T(8,128)S(1)} %shard_map.64.own, f32[2,256,128]{2,1,0:T(8,128)S(1)} %collective-permute-done.1.arr, bf16[4,2,2,512,128]{4,3,2,1,0:T(8,128)(2,1)S(1)} %bitcast.32, bf16[2,256,512]{2,1,0:T(8,128)(2,1)S(1)} %copy-done.9, ...), custom_call_target="tpu_custom_call" | custom-call | flops 201326592 | bytes 786432 | tf_op jit(solution)/shard_map/pallas_call | solution.py:113
  77.4 26.0 %collective-permute-done.10 = f32[512,128]{1,0:T(8,128)S(1)} collective-permute-done((f32[512,128]{1,0:T(8,128)S(1)}, f32[512,128]{1,0:T(8,128)S(1)}, u32[]{:S(2)}, u32[]{:S(2)}) %collective-permute-start.10) | collective-permute-done | bytes 262176 | tf_op jit(solution)/shard_map/ppermute | solution.py:139
  103.4 4.5 %collective-permute-done.6 = f32[512,128]{1,0:T(8,128)S(1)} collective-permute-done((f32[512,128]{1,0:T(8,128)S(1)}, f32[512,128]{1,0:T(8,128)S(1)}, u32[]{:S(2)}, u32[]{:S(2)}) %collective-permute-start.6) | collective-permute-done | bytes 262176 | tf_op jit(solution)/shard_map/ppermute | solution.py:139
  108.0 2.1 %shard_map.68.own = f32[1024,128]{1,0:T(8,128)S(1)} custom-call(s32[2]{0:T(128)S(1)} %pad_add_fusion.scal, f32[512,128]{1,0:T(8,128)S(1)} %shard_map.66.own, f32[512,128]{1,0:T(8,128)S(1)} %collective-permute-done.2.arr, bf16[4,2,1024,128]{3,2,1,0:T(8,128)(2,1)S(1)} %bitcast.33, bf16[2,256,512]{2,1,0:T(8,128)(2,1)S(1)} %copy-done.7, ...), custom_call_target="tpu_custom_call" | custom-call | flops 402653184 | bytes 1572864 | tf_op jit(solution)/shard_map/pallas_call | solution.py:113
  110.1 4.6 %shard_map.79 = f32[2048,128]{1,0:T(8,128)} custom-call(s32[1]{0:T(128)} %bitcast.scal, f32[1024,128]{1,0:T(8,128)S(1)} %shard_map.68.own, f32[1024,128]{1,0:T(8,128)S(1)} %pad_maximum_fusion.arr, bf16[4,2048,128]{2,1,0:T(8,128)(2,1)S(1)} %bitcast.34, bf16[2,256,512]{2,1,0:T(8,128)(2,1)S(1)} %copy-done.9, bf16[2,256,512]{2,1,0:T(8,128)(2,1)S(1)} %copy-done.8), custom_call_target="tpu_custom_call" | custom-call | flops 805306368 | bytes 3145728 | tf_op jit(solution)/shard_map/pallas_call | solution.py:113
  (46 shorter events, 13.6 us)
Async XLA Ops:
  1.0 13.8 %collective-permute-start.3 = (f32[2,2,64,128]{3,2,1,0:T(8,128)S(1)}, f32[2,2,64,128]{3,2,1,0:T(8,128)S(1)}, u32[]{:S(2)}, u32[]{:S(2)}) collective-permute-start(f32[2,2,64,128]{3,2,1,0:T(8,128)S(1)} %get-tuple-element.5), channel_id=1, source_target_pairs={{0,256},{32,288},{64,320},{96,352},{128,384},{160,416},{192,448},{... | collective-permute-start | bytes 393224 | tf_op jit(solution)/shard_map/ppermute | solution.py:139
  6.1 17.7 %collective-permute-start.7 = (f32[2,2,64,128]{3,2,1,0:T(8,128)S(1)}, f32[2,2,64,128]{3,2,1,0:T(8,128)S(1)}, u32[]{:S(2)}, u32[]{:S(2)}) collective-permute-start(f32[2,2,64,128]{3,2,1,0:T(8,128)S(1)} %get-tuple-element.6), channel_id=1, source_target_pairs={{0,256},{32,288},{64,320},{96,352},{128,384},{160,416},{192,448},{... | collective-permute-start | bytes 393224 | tf_op jit(solution)/shard_map/ppermute | solution.py:139
  9.3 18.9 %collective-permute-start = (f32[2,2,128,128]{3,2,1,0:T(8,128)S(1)}, f32[2,2,128,128]{3,2,1,0:T(8,128)S(1)}, u32[]{:S(2)}, u32[]{:S(2)}) collective-permute-start(f32[2,2,128,128]{3,2,1,0:T(8,128)S(1)} %dynamic-slice_bitcast_fusion), channel_id=1, source_target_pairs={{0,256},{32,288},{64,320},{96,352},{128,384},{160,416},{192,448},{... | collective-permute-start | bytes 786440 | tf_op jit(solution)/shard_map/ppermute | solution.py:139
  14.8 1.6 %copy-start = (bf16[4,1,1,2048,128]{4,3,2,1,0:T(8,128)(2,1)S(1)}, bf16[4,1,1,2048,128]{4,3,2,1,0:T(8,128)(2,1)}, u32[]{:S(2)}) copy-start(bf16[4,1,1,2048,128]{4,3,2,1,0:T(8,128)(2,1)} %param.7) | copy-start | bytes 6291460
  16.4 1.2 %copy-start.2 = (f32[1,1,2048,128]{3,2,1,0:T(8,128)S(1)}, f32[1,1,2048,128]{3,2,1,0:T(8,128)}, u32[]{:S(2)}) copy-start(f32[1,1,2048,128]{3,2,1,0:T(8,128)} %param.6) | copy-start | bytes 3145732
  17.7 1.0 copy-start.4
  18.7 1.0 copy-start.6
  21.0 7.3 %copy-start.1 = (bf16[4,1,1,2048,128]{4,3,2,1,0:T(8,128)(2,1)S(1)}, bf16[4,1,1,2048,128]{4,3,2,1,0:T(8,128)(2,1)}, u32[]{:S(2)}) copy-start(bf16[4,1,1,2048,128]{4,3,2,1,0:T(8,128)(2,1)} %param.7) | copy-start | bytes 6291460
  21.0 7.3 %copy-start.5 = (bf16[2,256,512]{2,1,0:T(8,128)(2,1)S(1)}, bf16[2,256,512]{2,1,0:T(8,128)(2,1)}, u32[]{:S(2)}) copy-start(bf16[2,256,512]{2,1,0:T(8,128)(2,1)} %constant.32.clone.low) | copy-start | bytes 1572868
  21.0 20.1 %collective-permute-start.4 = (f32[2,128,128]{2,1,0:T(8,128)S(1)}, f32[2,128,128]{2,1,0:T(8,128)S(1)}, u32[]{:S(2)}, u32[]{:S(2)}) collective-permute-start(f32[2,128,128]{2,1,0:T(8,128)S(1)} %shard_map.70), channel_id=1, source_target_pairs={{0,16},{1,17},{2,18},{3,19},{4,20},{5,21},{6,22},{7,23},{8,24},{9,... | collective-permute-start | bytes 393224 | tf_op jit(solution)/shard_map/ppermute | solution.py:139
  25.0 9.9 %collective-permute-start.8 = (f32[2,128,128]{2,1,0:T(8,128)S(1)}, f32[2,128,128]{2,1,0:T(8,128)S(1)}, u32[]{:S(2)}, u32[]{:S(2)}) collective-permute-start(f32[2,128,128]{2,1,0:T(8,128)S(1)} %shard_map.75), channel_id=1, source_target_pairs={{0,16},{1,17},{2,18},{3,19},{4,20},{5,21},{6,22},{7,23},{8,24},{9,... | collective-permute-start | bytes 393224 | tf_op jit(solution)/shard_map/ppermute | solution.py:139
  29.7 40.0 %collective-permute-start.1 = (f32[2,256,128]{2,1,0:T(8,128)S(1)}, f32[2,256,128]{2,1,0:T(8,128)S(1)}, u32[]{:S(2)}, u32[]{:S(2)}) collective-permute-start(f32[2,256,128]{2,1,0:T(8,128)S(1)} %shard_map.65), channel_id=1, source_target_pairs={{0,16},{1,17},{2,18},{3,19},{4,20},{5,21},{6,22},{7,23},{8,24},{9,... | collective-permute-start | bytes 786440 | tf_op jit(solution)/shard_map/ppermute | solution.py:139
  33.6 1.3 %copy-start.8 = (bf16[2,256,512]{2,1,0:T(8,128)(2,1)S(1)}, bf16[2,256,512]{2,1,0:T(8,128)(2,1)}, u32[]{:S(2)}) copy-start(bf16[2,256,512]{2,1,0:T(8,128)(2,1)} %constant.34.clone.low) | copy-start | bytes 1572868
  33.6 1.3 %copy-start.9 = (bf16[2,256,512]{2,1,0:T(8,128)(2,1)S(1)}, bf16[2,256,512]{2,1,0:T(8,128)(2,1)}, u32[]{:S(2)}) copy-start(bf16[2,256,512]{2,1,0:T(8,128)(2,1)} %constant.33.clone.high) | copy-start | bytes 1572868
  36.2 11.2 %collective-permute-start.9 = (f32[256,128]{1,0:T(8,128)S(1)}, f32[256,128]{1,0:T(8,128)S(1)}, u32[]{:S(2)}, u32[]{:S(2)}) collective-permute-start(f32[256,128]{1,0:T(8,128)S(1)} %shard_map.77), channel_id=1, source_target_pairs={{0,128},{32,160},{64,192},{96,224},{128,0},{160,32},{192,64},{224,... | collective-permute-start | bytes 393224 | tf_op jit(solution)/shard_map/ppermute | solution.py:139
  42.4 22.0 %collective-permute-start.5 = (f32[256,128]{1,0:T(8,128)S(1)}, f32[256,128]{1,0:T(8,128)S(1)}, u32[]{:S(2)}, u32[]{:S(2)}) collective-permute-start(f32[256,128]{1,0:T(8,128)S(1)} %shard_map.72), channel_id=1, source_target_pairs={{0,128},{32,160},{64,192},{96,224},{128,0},{160,32},{192,64},{224,... | collective-permute-start | bytes 393224 | tf_op jit(solution)/shard_map/ppermute | solution.py:139
  46.2 1.3 %copy-start.7 = (bf16[2,256,512]{2,1,0:T(8,128)(2,1)S(1)}, bf16[2,256,512]{2,1,0:T(8,128)(2,1)}, u32[]{:S(2)}) copy-start(bf16[2,256,512]{2,1,0:T(8,128)(2,1)} %constant.31.clone.high) | copy-start | bytes 1572868
  49.4 18.9 %copy-start.3 = (f32[1,1,2048,128]{3,2,1,0:T(8,128)S(1)}, f32[1,1,2048,128]{3,2,1,0:T(8,128)}, u32[]{:S(2)}) copy-start(f32[1,1,2048,128]{3,2,1,0:T(8,128)} %param.6) | copy-start | bytes 3145732
  49.4 54.0 %collective-permute-start.10 = (f32[512,128]{1,0:T(8,128)S(1)}, f32[512,128]{1,0:T(8,128)S(1)}, u32[]{:S(2)}, u32[]{:S(2)}) collective-permute-start(f32[512,128]{1,0:T(8,128)S(1)} %shard_map.78), channel_id=1, source_target_pairs={{0,8},{1,9},{2,10},{3,11},{4,12},{5,13},{6,14},{7,15},{8,0},{9,1},... | collective-permute-start | bytes 786440 | tf_op jit(solution)/shard_map/ppermute | solution.py:139
  66.3 41.6 %collective-permute-start.6 = (f32[512,128]{1,0:T(8,128)S(1)}, f32[512,128]{1,0:T(8,128)S(1)}, u32[]{:S(2)}, u32[]{:S(2)}) collective-permute-start(f32[512,128]{1,0:T(8,128)S(1)} %shard_map.73), channel_id=1, source_target_pairs={{0,8},{1,9},{2,10},{3,11},{4,12},{5,13},{6,14},{7,15},{8,0},{9,1},... | collective-permute-start | bytes 786440 | tf_op jit(solution)/shard_map/ppermute | solution.py:139
  71.0 37.0 %collective-permute-start.2 = (f32[512,128]{1,0:T(8,128)S(1)}, f32[512,128]{1,0:T(8,128)S(1)}, u32[]{:S(2)}, u32[]{:S(2)}) collective-permute-start(f32[512,128]{1,0:T(8,128)S(1)} %shard_map.67), channel_id=1, source_target_pairs={{0,128},{32,160},{64,192},{96,224},{128,0},{160,32},{192,64},{224,... | collective-permute-start | bytes 786440 | tf_op jit(solution)/shard_map/ppermute | solution.py:139

commit v2 on v1

v2 whole, which is shorter than its diff:
```python
import functools

import jax
import jax.numpy as jnp
import ml_dtypes
import numpy as np
from jax import lax
from jax.experimental import pallas as pl
from jax.experimental.pallas import tpu as pltpu
from jax.sharding import PartitionSpec as P

P_SIZE = 8
SQUARE = P_SIZE * P_SIZE
CH = 2 * SQUARE

def half_angle_polys():
    nodes = np.cos((2 * np.arange(64) + 1) * np.pi / 128)
    top = 3.15**2
    u = (nodes + 1) / 2 * top
    x = np.sqrt(u)
    fit = np.polynomial.chebyshev.Chebyshev.fit
    power = np.polynomial.Polynomial
    sine = fit(u, np.sin(x / 2) / x, 5, domain=[0, top]).convert(kind=power)
    cosine = fit(u, 2 * np.cos(x / 2), 6, domain=[0, top]).convert(kind=power)
    return [float(v) for v in sine.coef], [float(v) for v in cosine.coef]


SINE, COSINE = half_angle_polys()


def horner(coef, u):
    total = jnp.full_like(u, coef[-1])
    for c in coef[-2::-1]:
        total = total * u + c
    return total


def cos_sin(x):
    u = x * x
    s = x * horner(SINE, u)
    c2 = horner(COSINE, u)
    return 1.0 - 2.0 * (s * s), s * c2


def child_tables(degree_count):
    cheb_nodes = np.cos((2.0 * np.arange(degree_count) + 1.0) * np.pi / (2.0 * degree_count))
    lagrange = np.ones((2, degree_count, degree_count))
    for parity in range(2):
        points = (cheb_nodes + (2.0 * parity - 1.0)) / 2.0
        for target in range(degree_count):
            for source in range(degree_count):
                for others in range(degree_count):
                    if others != source:
                        lagrange[parity, target, source] *= (
                            points[target] - cheb_nodes[others]
                        ) / (cheb_nodes[source] - cheb_nodes[others])
    return lagrange


def child_blocks():
    lagrange = child_tables(P_SIZE).astype(np.float32)
    eye = np.eye(P_SIZE, dtype=np.float32)
    blocks = np.zeros((2, 2, 2, SQUARE, CH), np.float32)
    for a in range(2):
        turned = lagrange[a].T
        for slot in range(2):
            half = slice(slot * SQUARE, (slot + 1) * SQUARE)
            blocks[0, a, slot, :, half] = np.kron(turned, eye)
            blocks[1, a, slot, :, half] = np.kron(eye, turned)
    return blocks.reshape(8 * SQUARE, CH)


def expand(blocks, outs):
    for out in outs:
        out[...] = jnp.zeros_like(out)
    for axis in range(2):
        for a in range(2):
            for slot in range(2):
                part = blocks[pl.ds(((axis * 2 + a) * 2 + slot) * SQUARE, SQUARE), :]
                high = part.astype(jnp.bfloat16)
                low = (part - high.astype(jnp.float32)).astype(jnp.bfloat16)
                for k in range(2):
                    rows = pl.ds(slot * CH + k * SQUARE, SQUARE)
                    columns = pl.ds((2 * a + k) * CH, CH)
                    outs[2 * axis][rows, columns] = high
                    outs[2 * axis + 1][rows, columns] = low


VMEM = pl.BlockSpec(memory_space=pltpu.VMEM)
HBM = pl.BlockSpec(memory_space=pltpu.HBM)


def limits(mib=6):
    return pltpu.CompilerParams(vmem_limit_bytes=mib * 1024 * 1024)


def load_kernel(weights, angles, blocks, near_weights, near_angles, *rest):
    sems = rest[-1]
    copies = [
        pltpu.make_async_copy(weights, near_weights, sems.at[0]),
        pltpu.make_async_copy(angles, near_angles, sems.at[1]),
    ]
    for copy in copies:
        copy.start()
    expand(blocks, rest[:-1])
    for copy in copies:
        copy.wait()


def load(weights, angles):
    part = jax.ShapeDtypeStruct((2 * CH, 4 * CH), jnp.bfloat16)
    return pl.pallas_call(
        load_kernel,
        out_shape=[
            jax.ShapeDtypeStruct(weights.shape, weights.dtype),
            jax.ShapeDtypeStruct(angles.shape, angles.dtype),
        ]
        + [part] * 4,
        in_specs=[HBM, HBM, VMEM],
        out_specs=[VMEM] * 6,
        scratch_shapes=[pltpu.SemaphoreType.DMA((2,))],
        compiler_params=limits(48),
        cost_estimate=pl.CostEstimate(
            flops=0, bytes_accessed=4 * 1024 * 1024, transcendentals=0
        ),
    )(weights, angles, jnp.asarray(child_blocks()))


def take_kernel(rows, n, weights, out, sems):
    copies = [
        pltpu.make_async_copy(
            weights.at[pl.ds(row, n)], out.at[pl.ds(k * n, n)], sems.at[k]
        )
        for k, row in enumerate(rows())
    ]
    for copy in copies:
        copy.start()
    for copy in copies:
        copy.wait()


def take(weights, rows, n, where):
    return pl.pallas_call(
        functools.partial(take_kernel, rows, n),
        out_shape=jax.ShapeDtypeStruct((4 * n, CH), jnp.float32),
        in_specs=[where],
        out_specs=VMEM,
        scratch_shapes=[pltpu.SemaphoreType.DMA((4,))],
        compiler_params=limits(48 if where is HBM else 6),
        cost_estimate=pl.CostEstimate(
            flops=0, bytes_accessed=4 * 1024 * 1024, transcendentals=0
        ),
    )(weights)


def own_bit(k):
    axis = ("gx", "gy")[k % 2]
    bit = lax.axis_size(axis).bit_length() - 2 - k // 2
    return lax.axis_index(axis) >> bit & 1


def turn(y, angle):
    c, s = cos_sin(angle)
    re, im = y[:, :CH], y[:, CH:]
    u = c * re - s * im
    v = s * re + c * im
    left = lax.broadcasted_iota(jnp.int32, u.shape, 1) < SQUARE
    return jnp.where(left, u, v) + pltpu.roll(jnp.where(left, v, u), SQUARE, 1)


def level_kernel(level, segments, tile, own, arr, ang, high, low, out, scratch):
    upper = own_bit(level) == 1

    def piece(parts):
        count = sum(n for *_, n in parts)
        near, far = (
            jnp.concatenate([ref[pl.ds(row[k], row[4]), :] for row in parts], axis=0)
            for k, ref in ((0, own), (1, arr))
        )
        x = jnp.concatenate([jnp.where(upper, far, near), jnp.where(upper, near, far)], axis=1)
        x_hi = x.astype(jnp.bfloat16)
        x_lo = (x - x_hi.astype(jnp.float32)).astype(jnp.bfloat16)
        dot = functools.partial(jnp.dot, preferred_element_type=jnp.float32)
        y = dot(x_hi, high[...]) + (dot(x_lo, high[...]) + dot(x_hi, low[...]))
        at = 0
        for _, _, row, _, n in parts:
            scratch[pl.ds(2 * at, 2 * n), :] = ang[pl.ds(row, 2 * n), :].astype(jnp.float32)
            at += n
        for a in range(2):
            turned = turn(
                y[:, 2 * a * CH : 2 * (a + 1) * CH], scratch[pl.ds(a, count, stride=2), :]
            )
            at = 0
            for _, _, _, row, n in parts:
                out[pl.ds(row + a, n, stride=2), :] = turned[at : at + n]
                at += n

    parts = segments()
    if parts[0][4] <= tile:
        piece(parts)
        return

    for row_own, row_arr, row_ang, row_out, n in parts:

        def step(i):
            b = pl.multiple_of(i * tile, tile)
            piece([(row_own + b, row_arr + b, row_ang + 2 * b, row_out + 2 * b, tile)])

        pl.loop(0, n // tile)(step)


def level_call(level, segments, own, arr, ang, table, rows):
    tile = min(rows // 2, 256)
    return pl.pallas_call(
        functools.partial(level_kernel, level, segments, tile),
        out_shape=jax.ShapeDtypeStruct((rows, CH), jnp.float32),
        in_specs=[VMEM] * 5,
        out_specs=VMEM,
        scratch_shapes=[pltpu.VMEM((2 * tile, CH), jnp.float32)],
        compiler_params=limits(),
        cost_estimate=pl.CostEstimate(
            flops=0, bytes_accessed=rows * 8 * 1024, transcendentals=0
        ),
    )(own, arr, ang, *table)


def last_kernel(own, arr, ang, high, low, *rest):
    out, scratch = rest[-2:]
    n = own.shape[0]
    level_kernel(3, lambda: [(0, 0, 0, 0, n)], n, own, arr, ang, high, low, out, scratch)


def last_call(own, arr, ang, table, row, earlier, boxes):
    rows = arr.shape[0]
    tile = min(rows, 256)
    k = row // tile
    whole = lambda g: (0, 0)
    operands = [own, arr, ang, *table]
    specs = [
        pl.BlockSpec((tile, CH), lambda g: (k + g, 0)),
        pl.BlockSpec((tile, CH), lambda g: (g, 0)),
        pl.BlockSpec((2 * tile, CH), lambda g: (3 * (boxes // 2 // tile) + k + g, 0)),
        VMEM,
        VMEM,
    ]
    aliases = {}
    if earlier is not None:
        aliases = {len(operands): 0}
        operands.append(earlier)
        specs.append(pl.BlockSpec(memory_space=pl.ANY))
    return pl.pallas_call(
        last_kernel,
        out_shape=jax.ShapeDtypeStruct((boxes, CH), jnp.float32),
        grid=(rows // tile,),
        in_specs=specs,
        out_specs=pl.BlockSpec((2 * tile, CH), lambda g: (k + g, 0)),
        scratch_shapes=[pltpu.VMEM((2 * tile, CH), jnp.float32)],
        input_output_aliases=aliases,
        compiler_params=limits(),
        cost_estimate=pl.CostEstimate(
            flops=0, bytes_accessed=rows * 16 * 1024, transcendentals=0
        ),
    )(*operands)


def from_partner(block, axis, bit):
    count = lax.axis_size(axis)
    route = [(low, low ^ (1 << bit)) for low in range(count)]
    return lax.ppermute(block, axis, route)


def after(value, *others):
    return lax.optimization_barrier((value, *others))[0]


def shards(weights, angles):
    bits_x = lax.axis_size("gx").bit_length() - 1
    bits_y = lax.axis_size("gy").bit_length() - 1
    boxes = weights.shape[2]
    base = boxes // 16
    far = weights.reshape(boxes, CH)
    w2, ang, *ready = load(far, angles.reshape(4 * boxes, CH))
    tab_x, tab_y = ready[:2], ready[2:]
    env = [ang, tab_x, tab_y, w2]
    aligned = lambda row: pl.multiple_of(row, 16)

    def target(k, other):
        return 1 - own_bit(k) if other else own_bit(k)

    def first(source, where, chunk, given):
        at, n = chunk

        def rows():
            low = [target(3, given) + 2 * t for t in range(4)]
            return [aligned(((1 - own_bit(0)) * 8 + k) * base + at) for k in low]

        return from_partner(take(source, rows, n, where), "gx", bits_x - 1)

    def level0(chunk, given, arr, send):
        at, n = chunk

        def segments():
            t1, t3 = target(1, send), target(3, given)
            parts = []
            for t2 in range(2):
                low = (t1 * 2 + t2) * 2 + t3
                parts.append(
                    (
                        aligned((own_bit(0) * 8 + low) * base + at),
                        aligned((t1 * 2 + t2) * n),
                        aligned(low * 2 * base + 2 * at),
                        t2 * 2 * n,
                        n,
                    )
                )
            return parts

        return level_call(0, segments, env[3], arr, env[0], env[1], 4 * n)

    def level1(chunk, given, own, arr, send):
        at, n = chunk

        def segments():
            t2, t3 = target(2, send), target(3, given)
            row = aligned(t2 * 2 * n)
            return [(row, row, aligned(boxes + (t2 * 2 + t3) * 4 * base + 4 * at), 0, 2 * n)]

        return level_call(1, segments, own, arr, env[0], env[2], 4 * n)

    def level2(chunk, given, own, arr):
        at, n = chunk

        def segments():
            t3 = target(3, given)
            return [(0, 0, aligned(2 * boxes + t3 * 8 * base + 8 * at), 0, 4 * n)]

        return level_call(2, segments, own, arr, env[0], env[1], 8 * n)

    def swap1(part):
        return from_partner(part, "gy", bits_y - 1)

    def swap2(part):
        return from_partner(part, "gx", bits_x - 2)

    def swap3(part):
        return from_partner(part, "gy", bits_y - 2)

    cut = base // 2
    a, b, k = (0, cut), (cut, base - cut), (0, base)
    arr_a = first(far, HBM, a, True)
    arr_b = first(w2, VMEM, b, True)
    send_a = level0(a, True, arr_a, True)
    arr1_a = swap1(send_a)
    keep_a = level0(a, True, after(arr_a, arr_b), False)
    send_b = level0(b, True, arr_b, True)
    arr1_b = swap1(send_b)
    arr2_a = swap2(level1(a, True, keep_a, after(arr1_a, send_b), True))
    arr_k = first(after(w2, send_b), VMEM, k, False)
    keep_a = level1(a, True, keep_a, after(arr1_a, arr1_b), False)
    given_a = level2(a, True, keep_a, arr2_a)
    z_a = swap3(given_a)
    here = after(lax.axis_index("gx"), given_a[0, 0]) < lax.axis_size("gx")

    def beside(w2, ang, tab_x, tab_y, arr_b, arr1_b, arr_k):
        env[:] = [ang, tab_x, tab_y, w2]
        keep_b = level0(b, True, arr_b, False)
        arr2_b = swap2(level1(b, True, keep_b, arr1_b, True))
        send_k = level0(k, False, arr_k, True)
        arr1_k = swap1(send_k)
        keep_b = level1(b, True, keep_b, arr1_b, False)
        keep_k = level0(k, False, arr_k, False)
        arr2_k = swap2(level1(k, False, keep_k, arr1_k, True))
        given_b = level2(b, True, keep_b, arr2_b)
        z_b = swap3(given_b)
        keep_k = level1(k, False, keep_k, arr1_k, False)
        return level2(k, False, keep_k, arr2_k), z_b

    def nothing(*_):
        return jnp.zeros((8 * base, CH)), jnp.zeros((8 * b[1], CH))

    kept, z_b = lax.cond(here, beside, nothing, w2, ang, tab_x, tab_y, arr_b, arr1_b, arr_k)
    out = last_call(kept, z_a, ang, tab_y, 0, None, boxes)
    out = last_call(kept, z_b, ang, tab_y, 8 * cut, out, boxes)
    return out.reshape(1, 1, boxes, CH)


def solution(mesh):
    return jax.shard_map(
        shards,
        mesh=mesh,
        in_specs=(P("gx", "gy", None, None), P(None, "gx", "gy", None, None)),
        out_specs=P("gx", "gy", None, None),
        check_vma=False,
    )
```

time: 115 us -> 103 us (0.90)
  the two profiles are of different devices: /device:TPU:32 before, /device:TPU:96 now
where the time goes in v2:
time: 103 us; the launch traced here: 102 us
  starting transfers between devices  50.8 us (49%)
  waiting for transfers between devices  29.5 us (29%)
  Pallas kernels  17.5 us (17%)
  local copies, waits for them, and re-layouts  3.8 us (4%)
    ppermute x11, starting transfers between devices, from_partner(): return lax.ppermute(block, axis, route)  50.8 us
    ppermute x11, waiting for transfers between devices, from_partner(): return lax.ppermute(block, axis, route)  29.5 us
    pallas_call x15, Pallas kernels, level_call(): pl.pallas_call(functools.partial(level_kernel, level, segments, tile), ou...  10.4 us
    pallas_call x2, Pallas kernels, last_call(): pl.pallas_call(last_kernel, out_shape=jax.ShapeDtypeStruct((boxes, CH), j...  5.93 us
    unnamed x18, local copies, waits for them, and re-layouts  3.79 us
  transfers between devices with their start and end apart: 11, of which 2 were waited for; matrix products, arithmetic and copies ran while one was open for 0% of the time, Pallas kernels for 11%

profile of v2, /device:TPU:96, one launch (start us, length us, event | category | flops | bytes accessed | tf_op | source)
XLA Modules:
  0.0 101.9 jit_solution(11999513264334037097)
XLA Ops:
  0.0 1.2 %copy-done = f32[1,1,2048,128]{3,2,1,0:T(8,128)S(1)} copy-done((f32[1,1,2048,128]{3,2,1,0:T(8,128)S(1)}, f32[1,1,2048,128]{3,2,1,0:T(8,128)}, u32[]{:S(2)}) %copy-start) | copy-done | bytes 1048600
  1.4 5.1 %collective-permute-start.7 = (f32[256,128]{1,0:T(8,128)S(1)}, f32[256,128]{1,0:T(8,128)S(1)}, u32[]{:S(2)}, u32[]{:S(2)}) collective-permute-start(f32[256,128]{1,0:T(8,128)S(1)} %shard_map.41), channel_id=1, source_target_pairs={{0,256},{32,288},{64,320},{96,352},{128,384},{160,416},{192,448},{... | collective-permute-start | bytes 393224 | tf_op jit(solution)/shard_map/ppermute | solution.py:269
  6.5 1.6 %copy-done.1 = bf16[4,1,1,2048,128]{4,3,2,1,0:T(8,128)(2,1)S(1)} copy-done((bf16[4,1,1,2048,128]{4,3,2,1,0:T(8,128)(2,1)S(1)}, bf16[4,1,1,2048,128]{4,3,2,1,0:T(8,128)(2,1)}, u32[]{:S(2)}) %copy-start.1) | copy-done | bytes 2097176
  8.1 0.9 copy-done.2
  9.7 2.2 %collective-permute-start.4 = (f32[256,128]{1,0:T(8,128)S(1)}, f32[256,128]{1,0:T(8,128)S(1)}, u32[]{:S(2)}, u32[]{:S(2)}) collective-permute-start(f32[256,128]{1,0:T(8,128)S(1)} %shard_map.38), channel_id=1, source_target_pairs={{0,256},{32,288},{64,320},{96,352},{128,384},{160,416},{192,448},{... | collective-permute-start | bytes 393224 | tf_op jit(solution)/shard_map/ppermute | solution.py:269
  12.4 3.5 %collective-permute-start.8 = (f32[256,128]{1,0:T(8,128)S(1)}, f32[256,128]{1,0:T(8,128)S(1)}, u32[]{:S(2)}, u32[]{:S(2)}) collective-permute-start(f32[256,128]{1,0:T(8,128)S(1)} %shard_map.43), channel_id=1, source_target_pairs={{0,16},{1,17},{2,18},{3,19},{4,20},{5,21},{6,22},{7,23},{8,24},{9,... | collective-permute-start | bytes 393224 | tf_op jit(solution)/shard_map/ppermute | solution.py:269
  15.9 2.2 %collective-permute-done.4.arr = f32[256,128]{1,0:T(8,128)S(1)} collective-permute-done((f32[256,128]{1,0:T(8,128)S(1)}, f32[256,128]{1,0:T(8,128)S(1)}, u32[]{:S(2)}, u32[]{:S(2)}) %collective-permute-start.4) | collective-permute-done | bytes 131104 | tf_op jit(solution)/shard_map/ppermute | solution.py:269
  18.5 2.6 %collective-permute-start.6 = (f32[256,128]{1,0:T(8,128)S(1)}, f32[256,128]{1,0:T(8,128)S(1)}, u32[]{:S(2)}, u32[]{:S(2)}) collective-permute-start(f32[256,128]{1,0:T(8,128)S(1)} %shard_map.39), channel_id=1, source_target_pairs={{0,16},{1,17},{2,18},{3,19},{4,20},{5,21},{6,22},{7,23},{8,24},{9,... | collective-permute-start | bytes 393224 | tf_op jit(solution)/shard_map/ppermute | solution.py:269
  21.9 4.9 %collective-permute-start.9 = (f32[256,128]{1,0:T(8,128)S(1)}, f32[256,128]{1,0:T(8,128)S(1)}, u32[]{:S(2)}, u32[]{:S(2)}) collective-permute-start(f32[256,128]{1,0:T(8,128)S(1)} %shard_map.45), channel_id=1, source_target_pairs={{0,128},{32,160},{64,192},{96,224},{128,0},{160,32},{192,64},{224,... | collective-permute-start | bytes 393224 | tf_op jit(solution)/shard_map/ppermute | solution.py:269
  27.2 4.1 %collective-permute-start.5 = (f32[512,128]{1,0:T(8,128)S(1)}, f32[512,128]{1,0:T(8,128)}, u32[]{:S(2)}, u32[]{:S(2)}) collective-permute-start(f32[512,128]{1,0:T(8,128)S(1)} %shard_map.40), channel_id=1, source_target_pairs={{0,256},{32,288},{64,320},{96,352},{128,384},{160,416},{192,448},{... | collective-permute-start | bytes 786440 | tf_op jit(solution)/shard_map/ppermute | solution.py:269
  31.7 0.6 shard_map.46
  32.3 13.0 %collective-permute-start.10 = (f32[512,128]{1,0:T(8,128)S(1)}, f32[512,128]{1,0:T(8,128)S(1)}, u32[]{:S(2)}, u32[]{:S(2)}) collective-permute-start(f32[512,128]{1,0:T(8,128)S(1)} %shard_map.46), channel_id=1, source_target_pairs={{0,8},{1,9},{2,10},{3,11},{4,12},{5,13},{6,14},{7,15},{8,0},{9,1},... | collective-permute-start | bytes 786440 | tf_op jit(solution)/shard_map/ppermute | solution.py:269
  45.4 50.6 %conditional.1 = (f32[1024,128]{1,0:T(8,128)S(1)}, f32[512,128]{1,0:T(8,128)}) conditional(s32[]{:T(128)} %convert_element_type.3, () %tuple.18, (f32[2048,128]{1,0:T(8,128)}, f32[512,128]{1,0:T(8,128)}, bf16[8192,128]{1,0:T(8,128)(2,1)S(1)}, bf16[256,512]{1,0:T(8,128)(2,1)S(1)}, bf16[256,512]{1,0:T(8,128)(2,1)S(1)}, ...), branch_computations={%region_0.0_spmd, %region_1.0_spmd} | conditional | bytes 46137632 | solution.py:381
  45.4 2.0 %branch_1_fun.10 = f32[512,128]{1,0:T(8,128)S(1)} custom-call(f32[2048,128]{1,0:T(8,128)} %get-tuple-element.23.own, f32[512,128]{1,0:T(8,128)} %get-tuple-element.24.arr, bf16[8192,128]{1,0:T(8,128)(2,1)S(1)} %get-tuple-element.25.ang, bf16[256,512]{1,0:T(8,128)(2,1)S(1)} %get-tuple-element.26.high, bf16[256,512]{1,0:T(8,128)(2,1)S(1)} %get-tuple-element.27.low), custom_call_target="tpu_custom_call" | custom-call | bytes 4194304 | tf_op jit(solution)/shard_map/cond/branch_1_fun/pallas_call | solution.py:214
  47.4 2.1 %collective-permute-start = (f32[512,128]{1,0:T(8,128)S(1)}, f32[512,128]{1,0:T(8,128)S(1)}, u32[]{:S(2)}, u32[]{:S(2)}) collective-permute-start(f32[512,128]{1,0:T(8,128)S(1)} %branch_1_fun.10), channel_id=1, source_target_pairs={{0,16},{1,17},{2,18},{3,19},{4,20},{5,21},{6,22},{7,23},{8,24},{9,... | collective-permute-start | bytes 786440 | tf_op jit(solution)/shard_map/cond/branch_1_fun/ppermute | solution.py:269
  50.3 4.7 %collective-permute-start.2 = (f32[256,128]{1,0:T(8,128)S(1)}, f32[256,128]{1,0:T(8,128)S(1)}, u32[]{:S(2)}, u32[]{:S(2)}) collective-permute-start(f32[256,128]{1,0:T(8,128)S(1)} %branch_1_fun.16), channel_id=1, source_target_pairs={{0,128},{32,160},{64,192},{96,224},{128,0},{160,32},{192,64},{224,... | collective-permute-start | bytes 393224 | tf_op jit(solution)/shard_map/cond/branch_1_fun/ppermute | solution.py:269
  55.0 1.6 %branch_1_fun.9.own = f32[512,128]{1,0:T(8,128)S(1)} custom-call(f32[2048,128]{1,0:T(8,128)S(1)} %copy-done.4, f32[512,128]{1,0:T(8,128)} %get-tuple-element.24.arr, bf16[8192,128]{1,0:T(8,128)(2,1)S(1)} %get-tuple-element.25.ang, bf16[256,512]{1,0:T(8,128)(2,1)S(1)} %get-tuple-element.26.high, bf16[256,512]{1,0:T(8,128)(2,1)S(1)} %get-tuple-element.27.low), custom_call_target="tpu_custom_call" | custom-call | bytes 4194304 | tf_op jit(solution)/shard_map/cond/branch_1_fun/pallas_call | solution.py:214
  57.0 0.6 branch_1_fun.12
  57.6 2.6 %collective-permute-start.1 = (f32[512,128]{1,0:T(8,128)S(1)}, f32[512,128]{1,0:T(8,128)S(1)}, u32[]{:S(2)}, u32[]{:S(2)}) collective-permute-start(f32[512,128]{1,0:T(8,128)S(1)} %branch_1_fun.12), channel_id=1, source_target_pairs={{0,128},{32,160},{64,192},{96,224},{128,0},{160,32},{192,64},{224,... | collective-permute-start | bytes 786440 | tf_op jit(solution)/shard_map/cond/branch_1_fun/ppermute | solution.py:269
  60.8 6.0 %collective-permute-start.3 = (f32[512,128]{1,0:T(8,128)S(1)}, f32[512,128]{1,0:T(8,128)}, u32[]{:S(2)}, u32[]{:S(2)}) collective-permute-start(f32[512,128]{1,0:T(8,128)S(1)} %branch_1_fun.17), channel_id=1, source_target_pairs={{0,8},{1,9},{2,10},{3,11},{4,12},{5,13},{6,14},{7,15},{8,0},{9,1},... | collective-permute-start | bytes 786440 | tf_op jit(solution)/shard_map/cond/branch_1_fun/ppermute | solution.py:269
  67.5 1.2 %branch_1_fun.13 = f32[1024,128]{1,0:T(8,128)S(1)} custom-call(f32[512,128]{1,0:T(8,128)S(1)} %branch_1_fun.11.own, f32[512,128]{1,0:T(8,128)S(1)} %collective-permute-done.1.arr, bf16[8192,128]{1,0:T(8,128)(2,1)S(1)} %get-tuple-element.25.ang, bf16[256,512]{1,0:T(8,128)(2,1)S(1)} %get-tuple-element.26.high, bf16[256,512]{1,0:T(8,128)(2,1)S(1)} %get-tuple-element.27.low), custom_call_target="tpu_custom_call" | custom-call | bytes 8388608 | tf_op jit(solution)/shard_map/cond/branch_1_fun/pallas_call | solution.py:214
  68.7 27.3 %collective-permute-done.3 = f32[512,128]{1,0:T(8,128)} collective-permute-done((f32[512,128]{1,0:T(8,128)S(1)}, f32[512,128]{1,0:T(8,128)}, u32[]{:S(2)}, u32[]{:S(2)}) %collective-permute-start.3) | collective-permute-done | bytes 262176 | tf_op jit(solution)/shard_map/cond/branch_1_fun/ppermute | solution.py:269
  96.0 3.1 %shard_map.47.rest_0_ = f32[2048,128]{1,0:T(8,128)} custom-call(f32[1024,128]{1,0:T(8,128)S(1)} %get-tuple-element.51.own, f32[512,128]{1,0:T(8,128)S(1)} %collective-permute-done.10.arr, bf16[8192,128]{1,0:T(8,128)(2,1)S(1)} %get-tuple-element.45.ang, bf16[256,512]{1,0:T(8,128)(2,1)} %copy-done.5, bf16[256,512]{1,0:T(8,128)(2,1)} %copy-done.8), custom_call_target="tpu_custom_call" | custom-call | bytes 8388608 | tf_op jit(solution)/shard_map/pallas_call | solution.py:251
  99.1 2.9 %shard_map.48 = f32[2048,128]{1,0:T(8,128)} custom-call(f32[1024,128]{1,0:T(8,128)S(1)} %get-tuple-element.51.own, f32[512,128]{1,0:T(8,128)} %get-tuple-element.52.arr, bf16[8192,128]{1,0:T(8,128)(2,1)S(1)} %get-tuple-element.45.ang, bf16[256,512]{1,0:T(8,128)(2,1)S(1)} %copy-done.6, ...), custom_call_target="tpu_custom_call", output_to_operand_aliasing={{}: (5, {})} | custom-call | bytes 8388608 | tf_op jit(solution)/shard_map/pallas_call | solution.py:251
  (46 shorter events, 5.6 us)
Async XLA Ops:
  0.0 1.2 %copy-start = (f32[1,1,2048,128]{3,2,1,0:T(8,128)S(1)}, f32[1,1,2048,128]{3,2,1,0:T(8,128)}, u32[]{:S(2)}) copy-start(f32[1,1,2048,128]{3,2,1,0:T(8,128)} %param.5) | copy-start | bytes 3145732
  1.4 10.6 %collective-permute-start.7 = (f32[256,128]{1,0:T(8,128)S(1)}, f32[256,128]{1,0:T(8,128)S(1)}, u32[]{:S(2)}, u32[]{:S(2)}) collective-permute-start(f32[256,128]{1,0:T(8,128)S(1)} %shard_map.41), channel_id=1, source_target_pairs={{0,256},{32,288},{64,320},{96,352},{128,384},{160,416},{192,448},{... | collective-permute-start | bytes 393224 | tf_op jit(solution)/shard_map/ppermute | solution.py:269
  6.5 1.6 %copy-start.1 = (bf16[4,1,1,2048,128]{4,3,2,1,0:T(8,128)(2,1)S(1)}, bf16[4,1,1,2048,128]{4,3,2,1,0:T(8,128)(2,1)}, u32[]{:S(2)}) copy-start(bf16[4,1,1,2048,128]{4,3,2,1,0:T(8,128)(2,1)} %param.6) | copy-start | bytes 6291460
  8.1 0.9 copy-start.2
  9.4 17.4 %copy-start.3 = (f32[2048,128]{1,0:T(8,128)}, f32[2048,128]{1,0:T(8,128)S(1)}, u32[]{:S(2)}) copy-start(f32[2048,128]{1,0:T(8,128)S(1)} %get-tuple-element.48.weights.own) | copy-start | bytes 3145732
  9.5 21.8 %copy-start.5 = (bf16[256,512]{1,0:T(8,128)(2,1)}, bf16[256,512]{1,0:T(8,128)(2,1)S(1)}, u32[]{:S(2)}) copy-start(bf16[256,512]{1,0:T(8,128)(2,1)S(1)} %get-tuple-element.49.high) | copy-start | bytes 786436
  9.5 21.8 %copy-start.8 = (bf16[256,512]{1,0:T(8,128)(2,1)}, bf16[256,512]{1,0:T(8,128)(2,1)S(1)}, u32[]{:S(2)}) copy-start(bf16[256,512]{1,0:T(8,128)(2,1)S(1)} %get-tuple-element.50.low) | copy-start | bytes 786436
  9.7 8.4 %collective-permute-start.4 = (f32[256,128]{1,0:T(8,128)S(1)}, f32[256,128]{1,0:T(8,128)S(1)}, u32[]{:S(2)}, u32[]{:S(2)}) collective-permute-start(f32[256,128]{1,0:T(8,128)S(1)} %shard_map.38), channel_id=1, source_target_pairs={{0,256},{32,288},{64,320},{96,352},{128,384},{160,416},{192,448},{... | collective-permute-start | bytes 393224 | tf_op jit(solution)/shard_map/ppermute | solution.py:269
  12.4 9.1 %collective-permute-start.8 = (f32[256,128]{1,0:T(8,128)S(1)}, f32[256,128]{1,0:T(8,128)S(1)}, u32[]{:S(2)}, u32[]{:S(2)}) collective-permute-start(f32[256,128]{1,0:T(8,128)S(1)} %shard_map.43), channel_id=1, source_target_pairs={{0,16},{1,17},{2,18},{3,19},{4,20},{5,21},{6,22},{7,23},{8,24},{9,... | collective-permute-start | bytes 393224 | tf_op jit(solution)/shard_map/ppermute | solution.py:269
  18.5 12.8 %collective-permute-start.6 = (f32[256,128]{1,0:T(8,128)S(1)}, f32[256,128]{1,0:T(8,128)S(1)}, u32[]{:S(2)}, u32[]{:S(2)}) collective-permute-start(f32[256,128]{1,0:T(8,128)S(1)} %shard_map.39), channel_id=1, source_target_pairs={{0,16},{1,17},{2,18},{3,19},{4,20},{5,21},{6,22},{7,23},{8,24},{9,... | collective-permute-start | bytes 393224 | tf_op jit(solution)/shard_map/ppermute | solution.py:269
  21.9 9.9 %collective-permute-start.9 = (f32[256,128]{1,0:T(8,128)S(1)}, f32[256,128]{1,0:T(8,128)S(1)}, u32[]{:S(2)}, u32[]{:S(2)}) collective-permute-start(f32[256,128]{1,0:T(8,128)S(1)} %shard_map.45), channel_id=1, source_target_pairs={{0,128},{32,160},{64,192},{96,224},{128,0},{160,32},{192,64},{224,... | collective-permute-start | bytes 393224 | tf_op jit(solution)/shard_map/ppermute | solution.py:269
  27.2 18.2 %collective-permute-start.5 = (f32[512,128]{1,0:T(8,128)S(1)}, f32[512,128]{1,0:T(8,128)}, u32[]{:S(2)}, u32[]{:S(2)}) collective-permute-start(f32[512,128]{1,0:T(8,128)S(1)} %shard_map.40), channel_id=1, source_target_pairs={{0,256},{32,288},{64,320},{96,352},{128,384},{160,416},{192,448},{... | collective-permute-start | bytes 786440 | tf_op jit(solution)/shard_map/ppermute | solution.py:269
  31.3 14.1 %copy-start.11 = (f32[256,128]{1,0:T(8,128)}, f32[256,128]{1,0:T(8,128)S(1)}, u32[]{:S(2)}) copy-start(f32[256,128]{1,0:T(8,128)S(1)} %collective-permute-done.6) | copy-start | bytes 393220
  32.3 63.6 %collective-permute-start.10 = (f32[512,128]{1,0:T(8,128)S(1)}, f32[512,128]{1,0:T(8,128)S(1)}, u32[]{:S(2)}, u32[]{:S(2)}) collective-permute-start(f32[512,128]{1,0:T(8,128)S(1)} %shard_map.46), channel_id=1, source_target_pairs={{0,8},{1,9},{2,10},{3,11},{4,12},{5,13},{6,14},{7,15},{8,0},{9,1},... | collective-permute-start | bytes 786440 | tf_op jit(solution)/shard_map/ppermute | solution.py:269
  45.4 4.1 %copy-start.4 = (f32[2048,128]{1,0:T(8,128)S(1)}, f32[2048,128]{1,0:T(8,128)}, u32[]{:S(2)}) copy-start(f32[2048,128]{1,0:T(8,128)} %get-tuple-element.23.own) | copy-start | bytes 3145732 | tf_op jit(solution)/shard_map/cond
  47.4 2.5 %copy-start.7 = (bf16[256,512]{1,0:T(8,128)(2,1)S(1)}, bf16[256,512]{1,0:T(8,128)(2,1)}, u32[]{:S(2)}) copy-start(bf16[256,512]{1,0:T(8,128)(2,1)} %get-tuple-element.28.high) | copy-start | bytes 786436 | tf_op jit(solution)/shard_map/cond
  47.4 2.5 %copy-start.10 = (bf16[256,512]{1,0:T(8,128)(2,1)S(1)}, bf16[256,512]{1,0:T(8,128)(2,1)}, u32[]{:S(2)}) copy-start(bf16[256,512]{1,0:T(8,128)(2,1)} %get-tuple-element.29.low) | copy-start | bytes 786436 | tf_op jit(solution)/shard_map/cond
  47.4 2.5 %copy-start.12 = (f32[256,128]{1,0:T(8,128)S(1)}, f32[256,128]{1,0:T(8,128)}, u32[]{:S(2)}) copy-start(f32[256,128]{1,0:T(8,128)} %get-tuple-element.31.arr) | copy-start | bytes 393220 | tf_op jit(solution)/shard_map/cond
  47.4 9.6 %collective-permute-start = (f32[512,128]{1,0:T(8,128)S(1)}, f32[512,128]{1,0:T(8,128)S(1)}, u32[]{:S(2)}, u32[]{:S(2)}) collective-permute-start(f32[512,128]{1,0:T(8,128)S(1)} %branch_1_fun.10), channel_id=1, source_target_pairs={{0,16},{1,17},{2,18},{3,19},{4,20},{5,21},{6,22},{7,23},{8,24},{9,... | collective-permute-start | bytes 786440 | tf_op jit(solution)/shard_map/cond/branch_1_fun/ppermute | solution.py:269
  50.3 9.9 %collective-permute-start.2 = (f32[256,128]{1,0:T(8,128)S(1)}, f32[256,128]{1,0:T(8,128)S(1)}, u32[]{:S(2)}, u32[]{:S(2)}) collective-permute-start(f32[256,128]{1,0:T(8,128)S(1)} %branch_1_fun.16), channel_id=1, source_target_pairs={{0,128},{32,160},{64,192},{96,224},{128,0},{160,32},{192,64},{224,... | collective-permute-start | bytes 393224 | tf_op jit(solution)/shard_map/cond/branch_1_fun/ppermute | solution.py:269
  57.6 9.9 %collective-permute-start.1 = (f32[512,128]{1,0:T(8,128)S(1)}, f32[512,128]{1,0:T(8,128)S(1)}, u32[]{:S(2)}, u32[]{:S(2)}) collective-permute-start(f32[512,128]{1,0:T(8,128)S(1)} %branch_1_fun.12), channel_id=1, source_target_pairs={{0,128},{32,160},{64,192},{96,224},{128,0},{160,32},{192,64},{224,... | collective-permute-start | bytes 786440 | tf_op jit(solution)/shard_map/cond/branch_1_fun/ppermute | solution.py:269
  60.8 35.2 %collective-permute-start.3 = (f32[512,128]{1,0:T(8,128)S(1)}, f32[512,128]{1,0:T(8,128)}, u32[]{:S(2)}, u32[]{:S(2)}) collective-permute-start(f32[512,128]{1,0:T(8,128)S(1)} %branch_1_fun.17), channel_id=1, source_target_pairs={{0,8},{1,9},{2,10},{3,11},{4,12},{5,13},{6,14},{7,15},{8,0},{9,1},... | collective-permute-start | bytes 786440 | tf_op jit(solution)/shard_map/cond/branch_1_fun/ppermute | solution.py:269
  96.0 3.1 %copy-start.6 = (bf16[256,512]{1,0:T(8,128)(2,1)S(1)}, bf16[256,512]{1,0:T(8,128)(2,1)}, u32[]{:S(2)}) copy-start(bf16[256,512]{1,0:T(8,128)(2,1)} %copy-done.5) | copy-start | bytes 786436
  96.0 3.1 %copy-start.9 = (bf16[256,512]{1,0:T(8,128)(2,1)S(1)}, bf16[256,512]{1,0:T(8,128)(2,1)}, u32[]{:S(2)}) copy-start(bf16[256,512]{1,0:T(8,128)(2,1)} %copy-done.8) | copy-start | bytes 786436

commit v3 on v2

--- a/solution.py
+++ b/solution.py
@@ -25,6 +25,7 @@
     return [float(v) for v in sine.coef], [float(v) for v in cosine.coef]
 
 
+COST_A, COST_B = 7 * 1024 * 1024, 4 * 1024 * 1024
 SINE, COSINE = half_angle_polys()
 
 
@@ -94,36 +95,43 @@
     return pltpu.CompilerParams(vmem_limit_bytes=mib * 1024 * 1024)
 
 
-def load_kernel(weights, angles, blocks, near_weights, near_angles, *rest):
+def load_kernel(angles, blocks, near_angles, *rest):
     sems = rest[-1]
-    copies = [
-        pltpu.make_async_copy(weights, near_weights, sems.at[0]),
-        pltpu.make_async_copy(angles, near_angles, sems.at[1]),
-    ]
-    for copy in copies:
-        copy.start()
+    copy = pltpu.make_async_copy(angles, near_angles, sems.at[0])
+    copy.start()
     expand(blocks, rest[:-1])
-    for copy in copies:
-        copy.wait()
-
-
-def load(weights, angles):
+    copy.wait()
+
+
+def load(angles):
     part = jax.ShapeDtypeStruct((2 * CH, 4 * CH), jnp.bfloat16)
     return pl.pallas_call(
         load_kernel,
-        out_shape=[
-            jax.ShapeDtypeStruct(weights.shape, weights.dtype),
-            jax.ShapeDtypeStruct(angles.shape, angles.dtype),
-        ]
-        + [part] * 4,
-        in_specs=[HBM, HBM, VMEM],
-        out_specs=[VMEM] * 6,
-        scratch_shapes=[pltpu.SemaphoreType.DMA((2,))],
+        out_shape=[jax.ShapeDtypeStruct(angles.shape, angles.dtype)] + [part] * 4,
+        in_specs=[HBM, VMEM],
+        out_specs=[VMEM] * 5,
+        scratch_shapes=[pltpu.SemaphoreType.DMA((1,))],
         compiler_params=limits(48),
         cost_estimate=pl.CostEstimate(
             flops=0, bytes_accessed=4 * 1024 * 1024, transcendentals=0
         ),
-    )(weights, angles, jnp.asarray(child_blocks()))
+    )(angles, jnp.asarray(child_blocks()))
+
+
+def tables_kernel(blocks, *outs):
+    expand(blocks, outs)
+
+
+def make_tables(blocks):
+    part = jax.ShapeDtypeStruct((2 * CH, 4 * CH), jnp.bfloat16)
+    return pl.pallas_call(
+        tables_kernel,
+        out_shape=[part] * 4,
+        in_specs=[VMEM],
+        out_specs=[VMEM] * 4,
+        compiler_params=limits(),
+        cost_estimate=pl.CostEstimate(flops=0, bytes_accessed=1024 * 1024, transcendentals=0),
+    )(blocks)
 
 
 def take_kernel(rows, n, weights, out, sems):
@@ -196,7 +204,7 @@
                 at += n
 
     parts = segments()
-    if parts[0][4] <= tile:
+    if len(parts) > 1 or parts[0][4] == tile:
         piece(parts)
         return
 
@@ -209,14 +217,55 @@
         pl.loop(0, n // tile)(step)
 
 
-def level_call(level, segments, own, arr, ang, table, rows):
-    tile = min(rows // 2, 256)
-    return pl.pallas_call(
-        functools.partial(level_kernel, level, segments, tile),
+def far_kernel(level, segments, tile, move, own, arr, ang, high, low, out, scratch, *rest):
+    near_ang, near_high, near_low, near_own, sems = rest
+    parts, copies, moved, at = segments(), [], [], 0
+    for row_own, row_arr, row_ang, row_out, n in parts:
+        pairs = [(ang.at[pl.ds(row_ang, 2 * n)], near_ang.at[pl.ds(2 * at, 2 * n)])]
+        if move:
+            pairs.append((own.at[pl.ds(row_own, n)], near_own.at[pl.ds(at, n)]))
+        copies += pairs
+        moved.append((at if move else row_own, row_arr, 2 * at, row_out, n))
+        at += n
+    copies += [(high, near_high), (low, near_low)]
+    copies = [
+        pltpu.make_async_copy(source, target, sems.at[i])
+        for i, (source, target) in enumerate(copies)
+    ]
+    for copy in copies:
+        copy.start()
+    for copy in copies:
+        copy.wait()
+    level_kernel(
+        level, lambda: moved, tile, near_own if move else own, arr, near_ang, near_high, near_low,
+        out, scratch,
+    )
+
+
+def level_call(level, segments, own, arr, ang, table, rows, far=False):
+    steps = -(-rows // 512)
+    tile = rows // 2 // steps
+    kernel = functools.partial(level_kernel, level, segments, tile)
+    scratch = [pltpu.VMEM((2 * tile, CH), jnp.float32)]
+    specs = [VMEM] * 5
+    if far:
+        move = level == 0
+        kernel = functools.partial(far_kernel, level, segments, tile, move)
+        scratch += [
+            pltpu.VMEM((rows, CH), jnp.bfloat16),
+            pltpu.VMEM((2 * CH, 4 * CH), jnp.bfloat16),
+            pltpu.VMEM((2 * CH, 4 * CH), jnp.bfloat16),
+            pltpu.VMEM((rows // 2, CH), jnp.float32),
+            pltpu.SemaphoreType.DMA((6,)),
+        ]
+        anywhere = pl.BlockSpec(memory_space=pl.ANY)
+        specs = [anywhere if move else VMEM, VMEM] + [anywhere] * 3
+    return pl.pallas_call(
+        kernel,
         out_shape=jax.ShapeDtypeStruct((rows, CH), jnp.float32),
-        in_specs=[VMEM] * 5,
+        in_specs=specs,
         out_specs=VMEM,
-        scratch_shapes=[pltpu.VMEM((2 * tile, CH), jnp.float32)],
+        scratch_shapes=scratch,
         compiler_params=limits(),
         cost_estimate=pl.CostEstimate(
             flops=0, bytes_accessed=rows * 8 * 1024, transcendentals=0
@@ -224,41 +273,68 @@
     )(own, arr, ang, *table)
 
 
-def last_kernel(own, arr, ang, high, low, *rest):
-    out, scratch = rest[-2:]
-    n = own.shape[0]
-    level_kernel(3, lambda: [(0, 0, 0, 0, n)], n, own, arr, ang, high, low, out, scratch)
-
-
-def last_call(own, arr, ang, table, row, earlier, boxes):
+def fetch_kernel(row, far, near, sem):
+    copy = pltpu.make_async_copy(far.at[pl.ds(row, near.shape[0])], near, sem)
+    copy.start()
+    copy.wait()
+
+
+def fetch(far, row, rows):
+    return pl.pallas_call(
+        functools.partial(fetch_kernel, row),
+        out_shape=jax.ShapeDtypeStruct((rows, CH), far.dtype),
+        in_specs=[pl.BlockSpec(memory_space=pl.ANY)],
+        out_specs=VMEM,
+        scratch_shapes=[pltpu.SemaphoreType.DMA(())],
+        compiler_params=limits(),
+        cost_estimate=pl.CostEstimate(flops=0, bytes_accessed=1024 * 1024, transcendentals=0),
+    )(far)
+
+
+def last_kernel(row, own, arr, ang, high, low, *rest):
+    out, scratch, near_out, sems = rest[-4:]
+    count, rows = near_out.shape[:2]
+    tile = rows // 2
+    copies = []
+    for i in range(count):
+        at = i * tile
+        part = near_out.at[i]
+        segment = (row + at, at, 2 * (row + at), 0, tile)
+        level_kernel(3, lambda: [segment], tile, own, arr, ang, high, low, part, scratch)
+        copy = pltpu.make_async_copy(
+            part, out.at[pl.ds(2 * (row + at), rows)], sems.at[i]
+        )
+        copy.start()
+        copies.append(copy)
+    for copy in copies:
+        copy.wait()
+
+
+def last_call(own, arr, ang, table, row, earlier, boxes, cost):
     rows = arr.shape[0]
-    tile = min(rows, 256)
-    k = row // tile
-    whole = lambda g: (0, 0)
+    count = -(-rows // 256)
+    tile = rows // count
     operands = [own, arr, ang, *table]
-    specs = [
-        pl.BlockSpec((tile, CH), lambda g: (k + g, 0)),
-        pl.BlockSpec((tile, CH), lambda g: (g, 0)),
-        pl.BlockSpec((2 * tile, CH), lambda g: (3 * (boxes // 2 // tile) + k + g, 0)),
-        VMEM,
-        VMEM,
-    ]
+    specs = [VMEM] * 5
     aliases = {}
     if earlier is not None:
         aliases = {len(operands): 0}
         operands.append(earlier)
-        specs.append(pl.BlockSpec(memory_space=pl.ANY))
-    return pl.pallas_call(
-        last_kernel,
+        specs.append(HBM)
+    return pl.pallas_call(
+        functools.partial(last_kernel, row),
         out_shape=jax.ShapeDtypeStruct((boxes, CH), jnp.float32),
-        grid=(rows // tile,),
         in_specs=specs,
-        out_specs=pl.BlockSpec((2 * tile, CH), lambda g: (k + g, 0)),
-        scratch_shapes=[pltpu.VMEM((2 * tile, CH), jnp.float32)],
+        out_specs=HBM,
+        scratch_shapes=[
+            pltpu.VMEM((2 * tile, CH), jnp.float32),
+            pltpu.VMEM((count, 2 * tile, CH), jnp.float32),
+            pltpu.SemaphoreType.DMA((count,)),
+        ],
         input_output_aliases=aliases,
         compiler_params=limits(),
         cost_estimate=pl.CostEstimate(
-            flops=0, bytes_accessed=rows * 16 * 1024, transcendentals=0
+            flops=0, bytes_accessed=cost, transcendentals=0
         ),
     )(*operands)
 
@@ -279,9 +355,11 @@
     boxes = weights.shape[2]
     base = boxes // 16
     far = weights.reshape(boxes, CH)
-    w2, ang, *ready = load(far, angles.reshape(4 * boxes, CH))
+    ang, *ready = load(angles.reshape(4 * boxes, CH))
+    w2 = far
     tab_x, tab_y = ready[:2], ready[2:]
-    env = [ang, tab_x, tab_y, w2]
+    env = [ang, tab_x, tab_y, w2, False]
+    ang_far = angles.reshape(4 * boxes, CH)
     aligned = lambda row: pl.multiple_of(row, 16)
 
     def target(k, other):
@@ -294,7 +372,8 @@
             low = [target(3, given) + 2 * t for t in range(4)]
             return [aligned(((1 - own_bit(0)) * 8 + k) * base + at) for k in low]
 
-        return from_partner(take(source, rows, n, where), "gx", bits_x - 1)
+        taken = take(source, rows, n, where)
+        return taken, from_partner(taken, "gx", bits_x - 1)
 
     def level0(chunk, given, arr, send):
         at, n = chunk
@@ -315,7 +394,7 @@
                 )
             return parts
 
-        return level_call(0, segments, env[3], arr, env[0], env[1], 4 * n)
+        return level_call(0, segments, env[3], arr, env[0], env[1], 4 * n, env[4])
 
     def level1(chunk, given, own, arr, send):
         at, n = chunk
@@ -325,7 +404,7 @@
             row = aligned(t2 * 2 * n)
             return [(row, row, aligned(boxes + (t2 * 2 + t3) * 4 * base + 4 * at), 0, 2 * n)]
 
-        return level_call(1, segments, own, arr, env[0], env[2], 4 * n)
+        return level_call(1, segments, own, arr, env[0], env[2], 4 * n, env[4])
 
     def level2(chunk, given, own, arr):
         at, n = chunk
@@ -334,7 +413,7 @@
             t3 = target(3, given)
             return [(0, 0, aligned(2 * boxes + t3 * 8 * base + 8 * at), 0, 4 * n)]
 
-        return level_call(2, segments, own, arr, env[0], env[1], 8 * n)
+        return level_call(2, segments, own, arr, env[0], env[1], 8 * n, env[4])
 
     def swap1(part):
         return from_partner(part, "gy", bits_y - 1)
@@ -348,39 +427,46 @@
     cut = base // 2
     a, b, k = (0, cut), (cut, base - cut), (0, base)
     arr_a = first(far, HBM, a, True)
-    arr_b = first(w2, VMEM, b, True)
+    arr_b = first(after(w2, arr_a[0]), VMEM, b, True)
+    arr_a = arr_a[1]
+    arr_b = arr_b[1]
     send_a = level0(a, True, arr_a, True)
     arr1_a = swap1(send_a)
     keep_a = level0(a, True, after(arr_a, arr_b), False)
-    send_b = level0(b, True, arr_b, True)
+    send_b = level0(b, True, after(arr_b, send_a), True)
     arr1_b = swap1(send_b)
-    arr2_a = swap2(level1(a, True, keep_a, after(arr1_a, send_b), True))
-    arr_k = first(after(w2, send_b), VMEM, k, False)
-    keep_a = level1(a, True, keep_a, after(arr1_a, arr1_b), False)
-    given_a = level2(a, True, keep_a, arr2_a)
+    send_a = level1(a, True, keep_a, after(arr1_a, send_b), True)
+    arr2_a = swap2(send_a)
+    keep_b = level0(b, True, after(arr_b, send_a), False)
+    send_b = level1(b, True, keep_b, arr1_b, True)
+    arr2_b = swap2(send_b)
+    keep_b = level1(b, True, keep_b, arr1_b, False)
+    keep_a = level1(a, True, keep_a, arr1_a, False)
+    given_a = level2(a, True, keep_a, after(arr2_a, send_b, keep_b))
     z_a = swap3(given_a)
-    here = after(lax.axis_index("gx"), given_a[0, 0]) < lax.axis_size("gx")
-
-    def beside(w2, ang, tab_x, tab_y, arr_b, arr1_b, arr_k):
-        env[:] = [ang, tab_x, tab_y, w2]
-        keep_b = level0(b, True, arr_b, False)
-        arr2_b = swap2(level1(b, True, keep_b, arr1_b, True))
-        send_k = level0(k, False, arr_k, True)
-        arr1_k = swap1(send_k)
-        keep_b = level1(b, True, keep_b, arr1_b, False)
+
+    given_b = level2(b, True, keep_b, arr2_b)
+    z_b = swap3(given_b)
+
+    here = after(lax.axis_index("gx"), given_b[0, 0]) < lax.axis_size("gx")
+
+    def beside(w2, ang, blocks):
+        ready = make_tables(blocks)
+        env[:] = [ang, ready[:2], ready[2:], w2, False]
+        arr_k = first(w2, HBM, k, False)[1]
+        arr1_k = swap1(level0(k, False, arr_k, True))
         keep_k = level0(k, False, arr_k, False)
         arr2_k = swap2(level1(k, False, keep_k, arr1_k, True))
-        given_b = level2(b, True, keep_b, arr2_b)
-        z_b = swap3(given_b)
         keep_k = level1(k, False, keep_k, arr1_k, False)
-        return level2(k, False, keep_k, arr2_k), z_b
-
-    def nothing(*_):
-        return jnp.zeros((8 * base, CH)), jnp.zeros((8 * b[1], CH))
-
-    kept, z_b = lax.cond(here, beside, nothing, w2, ang, tab_x, tab_y, arr_b, arr1_b, arr_k)
-    out = last_call(kept, z_a, ang, tab_y, 0, None, boxes)
-    out = last_call(kept, z_b, ang, tab_y, 8 * cut, out, boxes)
+        return level2(k, False, keep_k, arr2_k)
+
+    kept = lax.cond(
+        here, beside, lambda *_: jnp.zeros((8 * base, CH)), far, ang_far, jnp.asarray(child_blocks())
+    )
+    near_ang = fetch(after(ang_far, kept), 3 * boxes, boxes)
+    kept = after(kept, near_ang)
+    out = last_call(kept, z_a, near_ang, tab_y, 0, None, boxes, COST_A)
+    out = last_call(kept, z_b, near_ang, tab_y, 8 * cut, out, boxes, COST_B)
     return out.reshape(1, 1, boxes, CH)
 
 

time: 103 us -> 90.1 us (0.87)
  the two profiles are of different devices: /device:TPU:96 before, /device:TPU:32 now
where the time goes in v3:
time: 90.1 us; the launch traced here: 89.7 us
  starting transfers between devices  50.2 us (56%)
  waiting for transfers between devices  21.5 us (24%)
  Pallas kernels  17.7 us (20%)
    ppermute x11, starting transfers between devices, from_partner(): return lax.ppermute(block, axis, route)  50.2 us
    ppermute x11, waiting for transfers between devices, from_partner(): return lax.ppermute(block, axis, route)  21.5 us
    pallas_call x15, Pallas kernels, level_call(): pl.pallas_call(kernel, out_shape=jax.ShapeDtypeStruct((rows, CH), jnp.flo...  9.82 us
    pallas_call x2, Pallas kernels, last_call(): pl.pallas_call(functools.partial(last_kernel, row), out_shape=jax.ShapeDt...  3.63 us
    pallas_call x3, Pallas kernels, take(): pl.pallas_call(functools.partial(take_kernel, rows, n), out_shape=jax.Sha...  2.8 us
  transfers between devices with their start and end apart: 11, of which 6 were waited for; matrix products, arithmetic and copies ran while one was open for 0% of the time, Pallas kernels for 17%

profile of v3, /device:TPU:32, one launch (start us, length us, event | category | flops | bytes accessed | tf_op | source)
XLA Modules:
  0.0 89.7 jit_solution(7955276617863521472)
XLA Ops:
  0.0 1.0 %shard_map.47 = f32[256,128]{1,0:T(8,128)S(1)} custom-call(f32[2048,128]{1,0:T(8,128)} %bitcast.6), custom_call_target="tpu_custom_call" | custom-call | bytes 4194304 | tf_op jit(solution)/shard_map/pallas_call | solution.py:151
  1.0 5.2 %collective-permute-start.4 = (f32[256,128]{1,0:T(8,128)S(1)}, f32[256,128]{1,0:T(8,128)S(1)}, u32[]{:S(2)}, u32[]{:S(2)}) collective-permute-start(f32[256,128]{1,0:T(8,128)S(1)} %shard_map.47), channel_id=1, source_target_pairs={{0,256},{32,288},{64,320},{96,352},{128,384},{160,416},{192,448},{... | collective-permute-start | bytes 393224 | tf_op jit(solution)/shard_map/ppermute | solution.py:345
  6.3 1.4 %shard_map.48 = f32[256,128]{1,0:T(8,128)S(1)} custom-call(f32[2048,128]{1,0:T(8,128)} %bitcast.7), custom_call_target="tpu_custom_call" | custom-call | bytes 4194304 | tf_op jit(solution)/shard_map/pallas_call | solution.py:151
  7.7 2.2 %collective-permute-start.3 = (f32[256,128]{1,0:T(8,128)S(1)}, f32[256,128]{1,0:T(8,128)S(1)}, u32[]{:S(2)}, u32[]{:S(2)}) collective-permute-start(f32[256,128]{1,0:T(8,128)S(1)} %shard_map.48), channel_id=1, source_target_pairs={{0,256},{32,288},{64,320},{96,352},{128,384},{160,416},{192,448},{... | collective-permute-start | bytes 393224 | tf_op jit(solution)/shard_map/ppermute | solution.py:345
  10.7 3.5 %collective-permute-start.5 = (f32[256,128]{1,0:T(8,128)S(1)}, f32[256,128]{1,0:T(8,128)S(1)}, u32[]{:S(2)}, u32[]{:S(2)}) collective-permute-start(f32[256,128]{1,0:T(8,128)S(1)} %shard_map.51), channel_id=1, source_target_pairs={{0,16},{1,17},{2,18},{3,19},{4,20},{5,21},{6,22},{7,23},{8,24},{9,... | collective-permute-start | bytes 393224 | tf_op jit(solution)/shard_map/ppermute | solution.py:345
  14.1 1.9 %collective-permute-done.3.arr = f32[256,128]{1,0:T(8,128)S(1)} collective-permute-done((f32[256,128]{1,0:T(8,128)S(1)}, f32[256,128]{1,0:T(8,128)S(1)}, u32[]{:S(2)}, u32[]{:S(2)}) %collective-permute-start.3) | collective-permute-done | bytes 131104 | tf_op jit(solution)/shard_map/ppermute | solution.py:345
  16.4 2.6 %collective-permute-start.6 = (f32[256,128]{1,0:T(8,128)S(1)}, f32[256,128]{1,0:T(8,128)S(1)}, u32[]{:S(2)}, u32[]{:S(2)}) collective-permute-start(f32[256,128]{1,0:T(8,128)S(1)} %shard_map.52), channel_id=1, source_target_pairs={{0,16},{1,17},{2,18},{3,19},{4,20},{5,21},{6,22},{7,23},{8,24},{9,... | collective-permute-start | bytes 393224 | tf_op jit(solution)/shard_map/ppermute | solution.py:345
  19.8 4.9 %collective-permute-start.9 = (f32[256,128]{1,0:T(8,128)S(1)}, f32[256,128]{1,0:T(8,128)S(1)}, u32[]{:S(2)}, u32[]{:S(2)}) collective-permute-start(f32[256,128]{1,0:T(8,128)S(1)} %shard_map.53), channel_id=1, source_target_pairs={{0,128},{32,160},{64,192},{96,224},{128,0},{160,32},{192,64},{224,... | collective-permute-start | bytes 393224 | tf_op jit(solution)/shard_map/ppermute | solution.py:345
  25.6 3.1 %collective-permute-start.7 = (f32[256,128]{1,0:T(8,128)S(1)}, f32[256,128]{1,0:T(8,128)S(1)}, u32[]{:S(2)}, u32[]{:S(2)}) collective-permute-start(f32[256,128]{1,0:T(8,128)S(1)} %shard_map.56), channel_id=1, source_target_pairs={{0,128},{32,160},{64,192},{96,224},{128,0},{160,32},{192,64},{224,... | collective-permute-start | bytes 393224 | tf_op jit(solution)/shard_map/ppermute | solution.py:345
  30.0 14.8 %collective-permute-start.10 = (f32[512,128]{1,0:T(8,128)S(1)}, f32[512,128]{1,0:T(8,128)S(1)}, u32[]{:S(2)}, u32[]{:S(2)}) collective-permute-start(f32[512,128]{1,0:T(8,128)S(1)} %shard_map.59), channel_id=1, source_target_pairs={{0,8},{1,9},{2,10},{3,11},{4,12},{5,13},{6,14},{7,15},{8,0},{9,1},... | collective-permute-start | bytes 786440 | tf_op jit(solution)/shard_map/ppermute | solution.py:345
  45.5 3.9 %collective-permute-start.8 = (f32[512,128]{1,0:T(8,128)S(1)}, f32[512,128]{1,0:T(8,128)S(1)}, u32[]{:S(2)}, u32[]{:S(2)}) collective-permute-start(f32[512,128]{1,0:T(8,128)S(1)} %shard_map.57), channel_id=1, source_target_pairs={{0,8},{1,9},{2,10},{3,11},{4,12},{5,13},{6,14},{7,15},{8,0},{9,1},... | collective-permute-start | bytes 786440 | tf_op jit(solution)/shard_map/ppermute | solution.py:345
  49.3 32.4 %conditional.1 = (f32[1024,128]{1,0:T(8,128)S(1)}) conditional(s32[]{:T(128)} %convert_element_type.3, () %tuple.20, (f32[2048,128]{1,0:T(8,128)S(1)}, f32[512,128]{1,0:T(8,128)S(1)}, bf16[8192,128]{1,0:T(8,128)(2,1)}) %tuple.34), branch_computations={%region_0.0_spmd, %region_1.0_spmd} | conditional | bytes 41943196 | solution.py:463
  49.8 3.8 %collective-permute-start = (f32[512,128]{1,0:T(8,128)S(1)}, f32[512,128]{1,0:T(8,128)S(1)}, u32[]{:S(2)}, u32[]{:S(2)}) collective-permute-start(f32[512,128]{1,0:T(8,128)S(1)} %branch_1_fun.7), channel_id=1, source_target_pairs={{0,256},{32,288},{64,320},{96,352},{128,384},{160,416},{192,448},{... | collective-permute-start | bytes 786440 | tf_op jit(solution)/shard_map/cond/branch_1_fun/ppermute | solution.py:345
  53.7 5.9 %collective-permute-done.arr = f32[512,128]{1,0:T(8,128)S(1)} collective-permute-done((f32[512,128]{1,0:T(8,128)S(1)}, f32[512,128]{1,0:T(8,128)S(1)}, u32[]{:S(2)}, u32[]{:S(2)}) %collective-permute-start) | collective-permute-done | bytes 262176 | tf_op jit(solution)/shard_map/cond/branch_1_fun/ppermute | solution.py:345
  59.5 2.4 %branch_1_fun.10 = f32[512,128]{1,0:T(8,128)S(1)} custom-call(f32[2048,128]{1,0:T(8,128)S(1)} %get-tuple-element.14.weights.own, f32[512,128]{1,0:T(8,128)S(1)} %collective-permute-done.arr, bf16[8192,128]{1,0:T(8,128)(2,1)} %get-tuple-element.15.ang, bf16[256,512]{1,0:T(8,128)(2,1)S(1)} %get-tuple-element.17.high, bf16[256,512]{1,0:T(8,128)(2,1)S(1)} %get-tuple-element.18.low), custom_call_target="tpu_custom_call" | custom-call | bytes 4194304 | tf_op jit(solution)/shard_map/cond/branch_1_fun/pallas_call | solution.py:263
  61.9 3.3 %collective-permute-start.1 = (f32[512,128]{1,0:T(8,128)S(1)}, f32[512,128]{1,0:T(8,128)S(1)}, u32[]{:S(2)}, u32[]{:S(2)}) collective-permute-start(f32[512,128]{1,0:T(8,128)S(1)} %branch_1_fun.10), channel_id=1, source_target_pairs={{0,16},{1,17},{2,18},{3,19},{4,20},{5,21},{6,22},{7,23},{8,24},{9,... | collective-permute-start | bytes 786440 | tf_op jit(solution)/shard_map/cond/branch_1_fun/ppermute | solution.py:345
  65.8 4.4 %collective-permute-done.1.arr = f32[512,128]{1,0:T(8,128)S(1)} collective-permute-done((f32[512,128]{1,0:T(8,128)S(1)}, f32[512,128]{1,0:T(8,128)S(1)}, u32[]{:S(2)}, u32[]{:S(2)}) %collective-permute-start.1) | collective-permute-done | bytes 262176 | tf_op jit(solution)/shard_map/cond/branch_1_fun/ppermute | solution.py:345
  70.8 3.1 %collective-permute-start.2 = (f32[512,128]{1,0:T(8,128)S(1)}, f32[512,128]{1,0:T(8,128)S(1)}, u32[]{:S(2)}, u32[]{:S(2)}) collective-permute-start(f32[512,128]{1,0:T(8,128)S(1)} %branch_1_fun.12), channel_id=1, source_target_pairs={{0,128},{32,160},{64,192},{96,224},{128,0},{160,32},{192,64},{224,... | collective-permute-start | bytes 786440 | tf_op jit(solution)/shard_map/cond/branch_1_fun/ppermute | solution.py:345
  74.4 6.1 %collective-permute-done.2.arr = f32[512,128]{1,0:T(8,128)S(1)} collective-permute-done((f32[512,128]{1,0:T(8,128)S(1)}, f32[512,128]{1,0:T(8,128)S(1)}, u32[]{:S(2)}, u32[]{:S(2)}) %collective-permute-start.2) | collective-permute-done | bytes 262176 | tf_op jit(solution)/shard_map/cond/branch_1_fun/ppermute | solution.py:345
  80.5 1.2 %branch_1_fun.13 = f32[1024,128]{1,0:T(8,128)S(1)} custom-call(f32[512,128]{1,0:T(8,128)S(1)} %branch_1_fun.11.own, f32[512,128]{1,0:T(8,128)S(1)} %collective-permute-done.2.arr, bf16[8192,128]{1,0:T(8,128)(2,1)S(1)} %copy-done.1, bf16[256,512]{1,0:T(8,128)(2,1)S(1)} %get-tuple-element.17.high, bf16[256,512]{1,0:T(8,128)(2,1)S(1)} %get-tuple-element.18.low), custom_call_target="tpu_custom_call" | custom-call | bytes 8388608 | tf_op jit(solution)/shard_map/cond/branch_1_fun/pallas_call | solution.py:263
  81.7 1.1 %shard_map.46.ang = bf16[2048,128]{1,0:T(8,128)(2,1)S(1)} custom-call(bf16[8192,128]{1,0:T(8,128)(2,1)} %bitcast.4), custom_call_target="tpu_custom_call" | custom-call | bytes 1048576 | tf_op jit(solution)/shard_map/pallas_call | solution.py:283
  83.3 1.8 %shard_map.60.rest_0_ = f32[2048,128]{1,0:T(8,128)} custom-call(f32[1024,128]{1,0:T(8,128)S(1)} %get-tuple-element.47.own, f32[512,128]{1,0:T(8,128)S(1)} %collective-permute-done.10.arr, bf16[2048,128]{1,0:T(8,128)(2,1)S(1)} %shard_map.46.ang, bf16[256,512]{1,0:T(8,128)(2,1)S(1)} %get-tuple-element.43.high, bf16[256,512]{1,0:T(8,128)(2,1)S(1)} %get-tuple-element.44.low), custom_call_target="tpu_custom_call" | custom-call | bytes 7340032 | tf_op jit(solution)/shard_map/pallas_call | solution.py:324
  85.1 2.7 %collective-permute-done.8.arr = f32[512,128]{1,0:T(8,128)S(1)} collective-permute-done((f32[512,128]{1,0:T(8,128)S(1)}, f32[512,128]{1,0:T(8,128)S(1)}, u32[]{:S(2)}, u32[]{:S(2)}) %collective-permute-start.8) | collective-permute-done | bytes 262176 | tf_op jit(solution)/shard_map/ppermute | solution.py:345
  87.9 1.8 %shard_map.61 = f32[2048,128]{1,0:T(8,128)} custom-call(f32[1024,128]{1,0:T(8,128)S(1)} %get-tuple-element.47.own, f32[512,128]{1,0:T(8,128)S(1)} %collective-permute-done.8.arr, bf16[2048,128]{1,0:T(8,128)(2,1)S(1)} %shard_map.46.ang, bf16[256,512]{1,0:T(8,128)(2,1)S(1)} %get-tuple-element.43.high, ...), custom_call_target="tpu_custom_call", output_to_operand_aliasing={{}: (5, {})} | custom-call | bytes 4194304 | tf_op jit(solution)/shard_map/pallas_call | solution.py:324
  (30 shorter events, 7.6 us)
Async XLA Ops:
  0.0 9.9 %copy-start.3 = (f32[512,128]{1,0:T(8,128)S(1)}, f32[512,128]{1,0:T(8,128)}, u32[]{:S(2)}) copy-start(f32[512,128]{1,0:T(8,128)} %constant.12.clone.blocks) | copy-start | bytes 786436
  0.0 9.9 %copy-start = (bf16[4,1,1,2048,128]{4,3,2,1,0:T(8,128)(2,1)S(1)}, bf16[4,1,1,2048,128]{4,3,2,1,0:T(8,128)(2,1)}, u32[]{:S(2)}) copy-start(bf16[4,1,1,2048,128]{4,3,2,1,0:T(8,128)(2,1)} %param.7) | copy-start | bytes 6291460
  0.0 10.3 %copy-start.2 = (f32[1,1,2048,128]{3,2,1,0:T(8,128)S(1)}, f32[1,1,2048,128]{3,2,1,0:T(8,128)}, u32[]{:S(2)}) copy-start(f32[1,1,2048,128]{3,2,1,0:T(8,128)} %param.6) | copy-start | bytes 3145732
  1.0 9.2 %collective-permute-start.4 = (f32[256,128]{1,0:T(8,128)S(1)}, f32[256,128]{1,0:T(8,128)S(1)}, u32[]{:S(2)}, u32[]{:S(2)}) collective-permute-start(f32[256,128]{1,0:T(8,128)S(1)} %shard_map.47), channel_id=1, source_target_pairs={{0,256},{32,288},{64,320},{96,352},{128,384},{160,416},{192,448},{... | collective-permute-start | bytes 393224 | tf_op jit(solution)/shard_map/ppermute | solution.py:345
  7.7 8.4 %collective-permute-start.3 = (f32[256,128]{1,0:T(8,128)S(1)}, f32[256,128]{1,0:T(8,128)S(1)}, u32[]{:S(2)}, u32[]{:S(2)}) collective-permute-start(f32[256,128]{1,0:T(8,128)S(1)} %shard_map.48), channel_id=1, source_target_pairs={{0,256},{32,288},{64,320},{96,352},{128,384},{160,416},{192,448},{... | collective-permute-start | bytes 393224 | tf_op jit(solution)/shard_map/ppermute | solution.py:345
  10.7 8.8 %collective-permute-start.5 = (f32[256,128]{1,0:T(8,128)S(1)}, f32[256,128]{1,0:T(8,128)S(1)}, u32[]{:S(2)}, u32[]{:S(2)}) collective-permute-start(f32[256,128]{1,0:T(8,128)S(1)} %shard_map.51), channel_id=1, source_target_pairs={{0,16},{1,17},{2,18},{3,19},{4,20},{5,21},{6,22},{7,23},{8,24},{9,... | collective-permute-start | bytes 393224 | tf_op jit(solution)/shard_map/ppermute | solution.py:345
  16.4 8.7 %collective-permute-start.6 = (f32[256,128]{1,0:T(8,128)S(1)}, f32[256,128]{1,0:T(8,128)S(1)}, u32[]{:S(2)}, u32[]{:S(2)}) collective-permute-start(f32[256,128]{1,0:T(8,128)S(1)} %shard_map.52), channel_id=1, source_target_pairs={{0,16},{1,17},{2,18},{3,19},{4,20},{5,21},{6,22},{7,23},{8,24},{9,... | collective-permute-start | bytes 393224 | tf_op jit(solution)/shard_map/ppermute | solution.py:345
  19.8 9.6 %collective-permute-start.9 = (f32[256,128]{1,0:T(8,128)S(1)}, f32[256,128]{1,0:T(8,128)S(1)}, u32[]{:S(2)}, u32[]{:S(2)}) collective-permute-start(f32[256,128]{1,0:T(8,128)S(1)} %shard_map.53), channel_id=1, source_target_pairs={{0,128},{32,160},{64,192},{96,224},{128,0},{160,32},{192,64},{224,... | collective-permute-start | bytes 393224 | tf_op jit(solution)/shard_map/ppermute | solution.py:345
  25.6 19.3 %collective-permute-start.7 = (f32[256,128]{1,0:T(8,128)S(1)}, f32[256,128]{1,0:T(8,128)S(1)}, u32[]{:S(2)}, u32[]{:S(2)}) collective-permute-start(f32[256,128]{1,0:T(8,128)S(1)} %shard_map.56), channel_id=1, source_target_pairs={{0,128},{32,160},{64,192},{96,224},{128,0},{160,32},{192,64},{224,... | collective-permute-start | bytes 393224 | tf_op jit(solution)/shard_map/ppermute | solution.py:345
  30.0 53.3 %collective-permute-start.10 = (f32[512,128]{1,0:T(8,128)S(1)}, f32[512,128]{1,0:T(8,128)S(1)}, u32[]{:S(2)}, u32[]{:S(2)}) collective-permute-start(f32[512,128]{1,0:T(8,128)S(1)} %shard_map.59), channel_id=1, source_target_pairs={{0,8},{1,9},{2,10},{3,11},{4,12},{5,13},{6,14},{7,15},{8,0},{9,1},... | collective-permute-start | bytes 786440 | tf_op jit(solution)/shard_map/ppermute | solution.py:345
  45.5 42.4 %collective-permute-start.8 = (f32[512,128]{1,0:T(8,128)S(1)}, f32[512,128]{1,0:T(8,128)S(1)}, u32[]{:S(2)}, u32[]{:S(2)}) collective-permute-start(f32[512,128]{1,0:T(8,128)S(1)} %shard_map.57), channel_id=1, source_target_pairs={{0,8},{1,9},{2,10},{3,11},{4,12},{5,13},{6,14},{7,15},{8,0},{9,1},... | collective-permute-start | bytes 786440 | tf_op jit(solution)/shard_map/ppermute | solution.py:345
  49.8 9.8 %collective-permute-start = (f32[512,128]{1,0:T(8,128)S(1)}, f32[512,128]{1,0:T(8,128)S(1)}, u32[]{:S(2)}, u32[]{:S(2)}) collective-permute-start(f32[512,128]{1,0:T(8,128)S(1)} %branch_1_fun.7), channel_id=1, source_target_pairs={{0,256},{32,288},{64,320},{96,352},{128,384},{160,416},{192,448},{... | collective-permute-start | bytes 786440 | tf_op jit(solution)/shard_map/cond/branch_1_fun/ppermute | solution.py:345
  59.5 5.6 %copy-start.1 = (bf16[8192,128]{1,0:T(8,128)(2,1)S(1)}, bf16[8192,128]{1,0:T(8,128)(2,1)}, u32[]{:S(2)}) copy-start(bf16[8192,128]{1,0:T(8,128)(2,1)} %get-tuple-element.15.ang) | copy-start | bytes 6291460 | tf_op jit(solution)/shard_map/cond
  61.9 8.3 %collective-permute-start.1 = (f32[512,128]{1,0:T(8,128)S(1)}, f32[512,128]{1,0:T(8,128)S(1)}, u32[]{:S(2)}, u32[]{:S(2)}) collective-permute-start(f32[512,128]{1,0:T(8,128)S(1)} %branch_1_fun.10), channel_id=1, source_target_pairs={{0,16},{1,17},{2,18},{3,19},{4,20},{5,21},{6,22},{7,23},{8,24},{9,... | collective-permute-start | bytes 786440 | tf_op jit(solution)/shard_map/cond/branch_1_fun/ppermute | solution.py:345
  70.8 9.8 %collective-permute-start.2 = (f32[512,128]{1,0:T(8,128)S(1)}, f32[512,128]{1,0:T(8,128)S(1)}, u32[]{:S(2)}, u32[]{:S(2)}) collective-permute-start(f32[512,128]{1,0:T(8,128)S(1)} %branch_1_fun.12), channel_id=1, source_target_pairs={{0,128},{32,160},{64,192},{96,224},{128,0},{160,32},{192,64},{224,... | collective-permute-start | bytes 786440 | tf_op jit(solution)/shard_map/cond/branch_1_fun/ppermute | solution.py:345

commit v4 on v3

--- a/solution.py
+++ b/solution.py
@@ -95,27 +95,44 @@
     return pltpu.CompilerParams(vmem_limit_bytes=mib * 1024 * 1024)
 
 
+PIECES = 8
+
+
 def load_kernel(angles, blocks, near_angles, *rest):
-    sems = rest[-1]
-    copy = pltpu.make_async_copy(angles, near_angles, sems.at[0])
-    copy.start()
-    expand(blocks, rest[:-1])
-    copy.wait()
+    near_blocks, sems = rest[-2:]
+    first = pltpu.make_async_copy(blocks, near_blocks, sems.at[PIECES])
+    first.start()
+    rows = angles.shape[0] // PIECES
+    copies = []
+    for i in range(PIECES):
+        part = pl.ds(i * rows, rows)
+        copies.append(
+            pltpu.make_async_copy(angles.at[part], near_angles.at[part], sems.at[i])
+        )
+        copies[-1].start()
+    first.wait()
+    expand(near_blocks, rest[:-2])
+    for copy in copies:
+        copy.wait()
 
 
 def load(angles):
     part = jax.ShapeDtypeStruct((2 * CH, 4 * CH), jnp.bfloat16)
+    blocks = jnp.asarray(child_blocks())
     return pl.pallas_call(
         load_kernel,
         out_shape=[jax.ShapeDtypeStruct(angles.shape, angles.dtype)] + [part] * 4,
-        in_specs=[HBM, VMEM],
+        in_specs=[HBM, HBM],
         out_specs=[VMEM] * 5,
-        scratch_shapes=[pltpu.SemaphoreType.DMA((1,))],
+        scratch_shapes=[
+            pltpu.VMEM(blocks.shape, blocks.dtype),
+            pltpu.SemaphoreType.DMA((PIECES + 1,)),
+        ],
         compiler_params=limits(48),
         cost_estimate=pl.CostEstimate(
             flops=0, bytes_accessed=4 * 1024 * 1024, transcendentals=0
         ),
-    )(angles, jnp.asarray(child_blocks()))
+    )(angles, blocks)
 
 
 def tables_kernel(blocks, *outs):
@@ -134,29 +151,34 @@
     )(blocks)
 
 
-def take_kernel(rows, n, weights, out, sems):
-    copies = [
-        pltpu.make_async_copy(
-            weights.at[pl.ds(row, n)], out.at[pl.ds(k * n, n)], sems.at[k]
-        )
-        for k, row in enumerate(rows())
-    ]
+def take_kernel(rows, weights, *rest):
+    outs, sems = rest[:-1], rest[-1]
+    copies = []
+    for out, parts in zip(outs, rows()):
+        at = 0
+        for row, n in parts:
+            copies.append(
+                pltpu.make_async_copy(
+                    weights.at[pl.ds(row, n)], out.at[pl.ds(at, n)], sems.at[len(copies)]
+                )
+            )
+            at += n
     for copy in copies:
         copy.start()
     for copy in copies:
         copy.wait()
 
 
-def take(weights, rows, n, where):
+def take(weights, rows, sizes, parts):
     return pl.pallas_call(
-        functools.partial(take_kernel, rows, n),
-        out_shape=jax.ShapeDtypeStruct((4 * n, CH), jnp.float32),
-        in_specs=[where],
-        out_specs=VMEM,
-        scratch_shapes=[pltpu.SemaphoreType.DMA((4,))],
-        compiler_params=limits(48 if where is HBM else 6),
+        functools.partial(take_kernel, rows),
+        out_shape=[jax.ShapeDtypeStruct((n, CH), jnp.float32) for n in sizes],
+        in_specs=[HBM],
+        out_specs=[VMEM] * len(sizes),
+        scratch_shapes=[pltpu.SemaphoreType.DMA((parts,))],
+        compiler_params=limits(48),
         cost_estimate=pl.CostEstimate(
-            flops=0, bytes_accessed=4 * 1024 * 1024, transcendentals=0
+            flops=0, bytes_accessed=20 * 1024 * 1024, transcendentals=0
         ),
     )(weights)
 
@@ -365,15 +387,16 @@
     def target(k, other):
         return 1 - own_bit(k) if other else own_bit(k)
 
-    def first(source, where, chunk, given):
-        at, n = chunk
-
+    def first(chunks, given):
         def rows():
             low = [target(3, given) + 2 * t for t in range(4)]
-            return [aligned(((1 - own_bit(0)) * 8 + k) * base + at) for k in low]
-
-        taken = take(source, rows, n, where)
-        return taken, from_partner(taken, "gx", bits_x - 1)
+            return [
+                [(aligned(((1 - own_bit(0)) * 8 + k) * base + at), n) for k in low]
+                for at, n in chunks
+            ]
+
+        taken = take(far, rows, [4 * n for _, n in chunks], 4 * len(chunks))
+        return [from_partner(part, "gx", bits_x - 1) for part in taken]
 
     def level0(chunk, given, arr, send):
         at, n = chunk
@@ -426,14 +449,11 @@
 
     cut = base // 2
     a, b, k = (0, cut), (cut, base - cut), (0, base)
-    arr_a = first(far, HBM, a, True)
-    arr_b = first(after(w2, arr_a[0]), VMEM, b, True)
-    arr_a = arr_a[1]
-    arr_b = arr_b[1]
+    arr_a, arr_b = first([a, b], True)
     send_a = level0(a, True, arr_a, True)
     arr1_a = swap1(send_a)
-    keep_a = level0(a, True, after(arr_a, arr_b), False)
-    send_b = level0(b, True, after(arr_b, send_a), True)
+    keep_a = level0(a, True, after(arr_a, send_a), False)
+    send_b = level0(b, True, after(arr_b, keep_a), True)
     arr1_b = swap1(send_b)
     send_a = level1(a, True, keep_a, after(arr1_a, send_b), True)
     arr2_a = swap2(send_a)
@@ -451,9 +471,11 @@
     here = after(lax.axis_index("gx"), given_b[0, 0]) < lax.axis_size("gx")
 
     def beside(w2, ang, blocks):
+        nonlocal far
+        far = w2
         ready = make_tables(blocks)
         env[:] = [ang, ready[:2], ready[2:], w2, False]
-        arr_k = first(w2, HBM, k, False)[1]
+        (arr_k,) = first([k], False)
         arr1_k = swap1(level0(k, False, arr_k, True))
         keep_k = level0(k, False, arr_k, False)
         arr2_k = swap2(level1(k, False, keep_k, arr1_k, True))

time: 90.1 us -> 89.2 us (0.990)
  waiting for transfers between devices: 21.5 us -> 18.4 us
  starting transfers between devices: 50.2 us -> 52.4 us
    ppermute x11, waiting for transfers between devices: 21.5 us -> 18.4 us  [from_partner(): return lax.ppermute(block, axis, route)]
    ppermute x11, starting transfers between devices: 50.2 us -> 52.4 us  [from_partner(): return lax.ppermute(block, axis, route)]
    pallas_call x3 -> x2, Pallas kernels: 2.8 us -> 1.42 us  [take(): pl.pallas_call(functools.partial(take_kernel, rows), out_shape=[jax.Shape...]
    pallas_call x1, Pallas kernels: 0.29 us -> 1.66 us  [load(): pl.pallas_call(load_kernel, out_shape=[jax.ShapeDtypeStruct(angles.shape,...]
where the time goes in v4:
time: 89.2 us; the launch traced here: 88.7 us
  starting transfers between devices  52.4 us (59%)
  waiting for transfers between devices  18.4 us (21%)
  Pallas kernels  17.7 us (20%)
    ppermute x11, starting transfers between devices, from_partner(): return lax.ppermute(block, axis, route)  52.4 us
    ppermute x11, waiting for transfers between devices, from_partner(): return lax.ppermute(block, axis, route)  18.4 us
    pallas_call x15, Pallas kernels, level_call(): pl.pallas_call(kernel, out_shape=jax.ShapeDtypeStruct((rows, CH), jnp.flo...  9.82 us
    pallas_call x2, Pallas kernels, last_call(): pl.pallas_call(functools.partial(last_kernel, row), out_shape=jax.ShapeDt...  3.63 us
  transfers between devices with their start and end apart: 11, of which 6 were waited for; matrix products, arithmetic and copies ran while one was open for 0% of the time, Pallas kernels for 17%

profile of v4, /device:TPU:32, one launch (start us, length us, event | category | flops | bytes accessed | tf_op | source)
XLA Modules:
  0.0 88.7 jit_solution(4747684285444527668)
XLA Ops:
  0.0 1.0 %shard_map.47 = (f32[256,128]{1,0:T(8,128)S(1)}, f32[256,128]{1,0:T(8,128)S(1)}) custom-call(f32[2048,128]{1,0:T(8,128)} %bitcast.6), custom_call_target="tpu_custom_call" | custom-call | bytes 20971520 | tf_op jit(solution)/shard_map/pallas_call | solution.py:173
  1.0 5.1 %collective-permute-start.4 = (f32[256,128]{1,0:T(8,128)S(1)}, f32[256,128]{1,0:T(8,128)S(1)}, u32[]{:S(2)}, u32[]{:S(2)}) collective-permute-start(f32[256,128]{1,0:T(8,128)S(1)} %get-tuple-element.38), channel_id=1, source_target_pairs={{0,256},{32,288},{64,320},{96,352},{128,384},{160,416},{192,448},{... | collective-permute-start | bytes 393224 | tf_op jit(solution)/shard_map/ppermute | solution.py:367
  6.1 2.2 %collective-permute-start.3 = (f32[256,128]{1,0:T(8,128)S(1)}, f32[256,128]{1,0:T(8,128)S(1)}, u32[]{:S(2)}, u32[]{:S(2)}) collective-permute-start(f32[256,128]{1,0:T(8,128)S(1)} %get-tuple-element.37), channel_id=1, source_target_pairs={{0,256},{32,288},{64,320},{96,352},{128,384},{160,416},{192,448},{... | collective-permute-start | bytes 393224 | tf_op jit(solution)/shard_map/ppermute | solution.py:367
  8.4 1.7 %shard_map.48 = (bf16[8192,128]{1,0:T(8,128)(2,1)S(1)}, bf16[256,512]{1,0:T(8,128)(2,1)S(1)}, bf16[256,512]{1,0:T(8,128)(2,1)S(1)}, bf16[256,512]{1,0:T(8,128)(2,1)S(1)}, bf16[256,512]{1,0:T(8,128)(2,1)S(1)}) custom-call(bf16[8192,128]{1,0:T(8,128)(2,1)} %bitcast.3, f32[512,128]{1,0:T(8,128)} %constant.12.clone.blocks), custom_call_target="tpu_custom_call" | custom-call | bytes 4194304 | tf_op jit(solution)/shard_map/pallas_call | solution.py:122
  10.5 3.5 %collective-permute-start.5 = (f32[256,128]{1,0:T(8,128)S(1)}, f32[256,128]{1,0:T(8,128)S(1)}, u32[]{:S(2)}, u32[]{:S(2)}) collective-permute-start(f32[256,128]{1,0:T(8,128)S(1)} %shard_map.49), channel_id=1, source_target_pairs={{0,16},{1,17},{2,18},{3,19},{4,20},{5,21},{6,22},{7,23},{8,24},{9,... | collective-permute-start | bytes 393224 | tf_op jit(solution)/shard_map/ppermute | solution.py:367
  14.9 2.6 %collective-permute-start.6 = (f32[256,128]{1,0:T(8,128)S(1)}, f32[256,128]{1,0:T(8,128)S(1)}, u32[]{:S(2)}, u32[]{:S(2)}) collective-permute-start(f32[256,128]{1,0:T(8,128)S(1)} %shard_map.51), channel_id=1, source_target_pairs={{0,16},{1,17},{2,18},{3,19},{4,20},{5,21},{6,22},{7,23},{8,24},{9,... | collective-permute-start | bytes 393224 | tf_op jit(solution)/shard_map/ppermute | solution.py:367
  17.9 4.9 %collective-permute-start.9 = (f32[256,128]{1,0:T(8,128)S(1)}, f32[256,128]{1,0:T(8,128)S(1)}, u32[]{:S(2)}, u32[]{:S(2)}) collective-permute-start(f32[256,128]{1,0:T(8,128)S(1)} %shard_map.52), channel_id=1, source_target_pairs={{0,128},{32,160},{64,192},{96,224},{128,0},{160,32},{192,64},{224,... | collective-permute-start | bytes 393224 | tf_op jit(solution)/shard_map/ppermute | solution.py:367
  23.6 3.4 %collective-permute-start.7 = (f32[256,128]{1,0:T(8,128)S(1)}, f32[256,128]{1,0:T(8,128)S(1)}, u32[]{:S(2)}, u32[]{:S(2)}) collective-permute-start(f32[256,128]{1,0:T(8,128)S(1)} %shard_map.55), channel_id=1, source_target_pairs={{0,128},{32,160},{64,192},{96,224},{128,0},{160,32},{192,64},{224,... | collective-permute-start | bytes 393224 | tf_op jit(solution)/shard_map/ppermute | solution.py:367
  28.5 15.0 %collective-permute-start.10 = (f32[512,128]{1,0:T(8,128)S(1)}, f32[512,128]{1,0:T(8,128)S(1)}, u32[]{:S(2)}, u32[]{:S(2)}) collective-permute-start(f32[512,128]{1,0:T(8,128)S(1)} %shard_map.58), channel_id=1, source_target_pairs={{0,8},{1,9},{2,10},{3,11},{4,12},{5,13},{6,14},{7,15},{8,0},{9,1},... | collective-permute-start | bytes 786440 | tf_op jit(solution)/shard_map/ppermute | solution.py:367
  44.1 3.3 %collective-permute-start.8 = (f32[512,128]{1,0:T(8,128)S(1)}, f32[512,128]{1,0:T(8,128)S(1)}, u32[]{:S(2)}, u32[]{:S(2)}) collective-permute-start(f32[512,128]{1,0:T(8,128)S(1)} %shard_map.56), channel_id=1, source_target_pairs={{0,8},{1,9},{2,10},{3,11},{4,12},{5,13},{6,14},{7,15},{8,0},{9,1},... | collective-permute-start | bytes 786440 | tf_op jit(solution)/shard_map/ppermute | solution.py:367
  47.4 32.4 %conditional.1 = (f32[1024,128]{1,0:T(8,128)S(1)}) conditional(s32[]{:T(128)} %convert_element_type.3, () %tuple.19, (f32[2048,128]{1,0:T(8,128)S(1)}, f32[512,128]{1,0:T(8,128)S(1)}, bf16[8192,128]{1,0:T(8,128)(2,1)}) %tuple.32), branch_computations={%region_0.0_spmd, %region_1.0_spmd} | conditional | bytes 58720412 | solution.py:485
  47.9 5.4 %collective-permute-start = (f32[512,128]{1,0:T(8,128)S(1)}, f32[512,128]{1,0:T(8,128)S(1)}, u32[]{:S(2)}, u32[]{:S(2)}) collective-permute-start(f32[512,128]{1,0:T(8,128)S(1)} %branch_1_fun.7), channel_id=1, source_target_pairs={{0,256},{32,288},{64,320},{96,352},{128,384},{160,416},{192,448},{... | collective-permute-start | bytes 786440 | tf_op jit(solution)/shard_map/cond/branch_1_fun/ppermute | solution.py:367
  53.4 4.2 %collective-permute-done.arr = f32[512,128]{1,0:T(8,128)S(1)} collective-permute-done((f32[512,128]{1,0:T(8,128)S(1)}, f32[512,128]{1,0:T(8,128)S(1)}, u32[]{:S(2)}, u32[]{:S(2)}) %collective-permute-start) | collective-permute-done | bytes 262176 | tf_op jit(solution)/shard_map/cond/branch_1_fun/ppermute | solution.py:367
  57.6 2.4 %branch_1_fun.10 = f32[512,128]{1,0:T(8,128)S(1)} custom-call(f32[2048,128]{1,0:T(8,128)S(1)} %get-tuple-element.14.weights.own, f32[512,128]{1,0:T(8,128)S(1)} %collective-permute-done.arr, bf16[8192,128]{1,0:T(8,128)(2,1)} %get-tuple-element.15.ang, bf16[256,512]{1,0:T(8,128)(2,1)S(1)} %get-tuple-element.17.high, bf16[256,512]{1,0:T(8,128)(2,1)S(1)} %get-tuple-element.18.low), custom_call_target="tpu_custom_call" | custom-call | bytes 4194304 | tf_op jit(solution)/shard_map/cond/branch_1_fun/pallas_call | solution.py:285
  60.0 3.5 %collective-permute-start.1 = (f32[512,128]{1,0:T(8,128)S(1)}, f32[512,128]{1,0:T(8,128)S(1)}, u32[]{:S(2)}, u32[]{:S(2)}) collective-permute-start(f32[512,128]{1,0:T(8,128)S(1)} %branch_1_fun.10), channel_id=1, source_target_pairs={{0,16},{1,17},{2,18},{3,19},{4,20},{5,21},{6,22},{7,23},{8,24},{9,... | collective-permute-start | bytes 786440 | tf_op jit(solution)/shard_map/cond/branch_1_fun/ppermute | solution.py:367
  64.1 4.1 %collective-permute-done.1.arr = f32[512,128]{1,0:T(8,128)S(1)} collective-permute-done((f32[512,128]{1,0:T(8,128)S(1)}, f32[512,128]{1,0:T(8,128)S(1)}, u32[]{:S(2)}, u32[]{:S(2)}) %collective-permute-start.1) | collective-permute-done | bytes 262176 | tf_op jit(solution)/shard_map/cond/branch_1_fun/ppermute | solution.py:367
  68.9 3.4 %collective-permute-start.2 = (f32[512,128]{1,0:T(8,128)S(1)}, f32[512,128]{1,0:T(8,128)S(1)}, u32[]{:S(2)}, u32[]{:S(2)}) collective-permute-start(f32[512,128]{1,0:T(8,128)S(1)} %branch_1_fun.12), channel_id=1, source_target_pairs={{0,128},{32,160},{64,192},{96,224},{128,0},{160,32},{192,64},{224,... | collective-permute-start | bytes 786440 | tf_op jit(solution)/shard_map/cond/branch_1_fun/ppermute | solution.py:367
  72.9 5.7 %collective-permute-done.2.arr = f32[512,128]{1,0:T(8,128)S(1)} collective-permute-done((f32[512,128]{1,0:T(8,128)S(1)}, f32[512,128]{1,0:T(8,128)S(1)}, u32[]{:S(2)}, u32[]{:S(2)}) %collective-permute-start.2) | collective-permute-done | bytes 262176 | tf_op jit(solution)/shard_map/cond/branch_1_fun/ppermute | solution.py:367
  78.6 1.2 %branch_1_fun.13 = f32[1024,128]{1,0:T(8,128)S(1)} custom-call(f32[512,128]{1,0:T(8,128)S(1)} %branch_1_fun.11.own, f32[512,128]{1,0:T(8,128)S(1)} %collective-permute-done.2.arr, bf16[8192,128]{1,0:T(8,128)(2,1)S(1)} %copy-done, bf16[256,512]{1,0:T(8,128)(2,1)S(1)} %get-tuple-element.17.high, bf16[256,512]{1,0:T(8,128)(2,1)S(1)} %get-tuple-element.18.low), custom_call_target="tpu_custom_call" | custom-call | bytes 8388608 | tf_op jit(solution)/shard_map/cond/branch_1_fun/pallas_call | solution.py:285
  79.8 1.1 %shard_map.46.ang = bf16[2048,128]{1,0:T(8,128)(2,1)S(1)} custom-call(bf16[8192,128]{1,0:T(8,128)(2,1)} %bitcast.5), custom_call_target="tpu_custom_call" | custom-call | bytes 1048576 | tf_op jit(solution)/shard_map/pallas_call | solution.py:305
  80.9 1.5 %collective-permute-done.10.arr = f32[512,128]{1,0:T(8,128)S(1)} collective-permute-done((f32[512,128]{1,0:T(8,128)S(1)}, f32[512,128]{1,0:T(8,128)S(1)}, u32[]{:S(2)}, u32[]{:S(2)}) %collective-permute-start.10) | collective-permute-done | bytes 262176 | tf_op jit(solution)/shard_map/ppermute | solution.py:367
  82.4 1.8 %shard_map.59.rest_0_ = f32[2048,128]{1,0:T(8,128)} custom-call(f32[1024,128]{1,0:T(8,128)S(1)} %get-tuple-element.49.own, f32[512,128]{1,0:T(8,128)S(1)} %collective-permute-done.10.arr, bf16[2048,128]{1,0:T(8,128)(2,1)S(1)} %shard_map.46.ang, bf16[256,512]{1,0:T(8,128)(2,1)S(1)} %get-tuple-element.45.high, bf16[256,512]{1,0:T(8,128)(2,1)S(1)} %get-tuple-element.46.low), custom_call_target="tpu_custom_call" | custom-call | bytes 7340032 | tf_op jit(solution)/shard_map/pallas_call | solution.py:346
  84.2 2.7 %collective-permute-done.8.arr = f32[512,128]{1,0:T(8,128)S(1)} collective-permute-done((f32[512,128]{1,0:T(8,128)S(1)}, f32[512,128]{1,0:T(8,128)S(1)}, u32[]{:S(2)}, u32[]{:S(2)}) %collective-permute-start.8) | collective-permute-done | bytes 262176 | tf_op jit(solution)/shard_map/ppermute | solution.py:367
  86.9 1.8 %shard_map.60 = f32[2048,128]{1,0:T(8,128)} custom-call(f32[1024,128]{1,0:T(8,128)S(1)} %get-tuple-element.49.own, f32[512,128]{1,0:T(8,128)S(1)} %collective-permute-done.8.arr, bf16[2048,128]{1,0:T(8,128)(2,1)S(1)} %shard_map.46.ang, bf16[256,512]{1,0:T(8,128)(2,1)S(1)} %get-tuple-element.45.high, ...), custom_call_target="tpu_custom_call", output_to_operand_aliasing={{}: (5, {})} | custom-call | bytes 4194304 | tf_op jit(solution)/shard_map/pallas_call | solution.py:346
  (27 shorter events, 6.9 us)
Async XLA Ops:
  0.0 10.1 %copy-start.1 = (f32[1,1,2048,128]{3,2,1,0:T(8,128)S(1)}, f32[1,1,2048,128]{3,2,1,0:T(8,128)}, u32[]{:S(2)}) copy-start(f32[1,1,2048,128]{3,2,1,0:T(8,128)} %param.6) | copy-start | bytes 3145732
  1.0 9.0 %collective-permute-start.4 = (f32[256,128]{1,0:T(8,128)S(1)}, f32[256,128]{1,0:T(8,128)S(1)}, u32[]{:S(2)}, u32[]{:S(2)}) collective-permute-start(f32[256,128]{1,0:T(8,128)S(1)} %get-tuple-element.38), channel_id=1, source_target_pairs={{0,256},{32,288},{64,320},{96,352},{128,384},{160,416},{192,448},{... | collective-permute-start | bytes 393224 | tf_op jit(solution)/shard_map/ppermute | solution.py:367
  6.1 8.4 %collective-permute-start.3 = (f32[256,128]{1,0:T(8,128)S(1)}, f32[256,128]{1,0:T(8,128)S(1)}, u32[]{:S(2)}, u32[]{:S(2)}) collective-permute-start(f32[256,128]{1,0:T(8,128)S(1)} %get-tuple-element.37), channel_id=1, source_target_pairs={{0,256},{32,288},{64,320},{96,352},{128,384},{160,416},{192,448},{... | collective-permute-start | bytes 393224 | tf_op jit(solution)/shard_map/ppermute | solution.py:367
  10.5 7.0 %collective-permute-start.5 = (f32[256,128]{1,0:T(8,128)S(1)}, f32[256,128]{1,0:T(8,128)S(1)}, u32[]{:S(2)}, u32[]{:S(2)}) collective-permute-start(f32[256,128]{1,0:T(8,128)S(1)} %shard_map.49), channel_id=1, source_target_pairs={{0,16},{1,17},{2,18},{3,19},{4,20},{5,21},{6,22},{7,23},{8,24},{9,... | collective-permute-start | bytes 393224 | tf_op jit(solution)/shard_map/ppermute | solution.py:367
  14.9 8.3 %collective-permute-start.6 = (f32[256,128]{1,0:T(8,128)S(1)}, f32[256,128]{1,0:T(8,128)S(1)}, u32[]{:S(2)}, u32[]{:S(2)}) collective-permute-start(f32[256,128]{1,0:T(8,128)S(1)} %shard_map.51), channel_id=1, source_target_pairs={{0,16},{1,17},{2,18},{3,19},{4,20},{5,21},{6,22},{7,23},{8,24},{9,... | collective-permute-start | bytes 393224 | tf_op jit(solution)/shard_map/ppermute | solution.py:367
  17.9 10.0 %collective-permute-start.9 = (f32[256,128]{1,0:T(8,128)S(1)}, f32[256,128]{1,0:T(8,128)S(1)}, u32[]{:S(2)}, u32[]{:S(2)}) collective-permute-start(f32[256,128]{1,0:T(8,128)S(1)} %shard_map.52), channel_id=1, source_target_pairs={{0,128},{32,160},{64,192},{96,224},{128,0},{160,32},{192,64},{224,... | collective-permute-start | bytes 393224 | tf_op jit(solution)/shard_map/ppermute | solution.py:367
  23.6 19.8 %collective-permute-start.7 = (f32[256,128]{1,0:T(8,128)S(1)}, f32[256,128]{1,0:T(8,128)S(1)}, u32[]{:S(2)}, u32[]{:S(2)}) collective-permute-start(f32[256,128]{1,0:T(8,128)S(1)} %shard_map.55), channel_id=1, source_target_pairs={{0,128},{32,160},{64,192},{96,224},{128,0},{160,32},{192,64},{224,... | collective-permute-start | bytes 393224 | tf_op jit(solution)/shard_map/ppermute | solution.py:367
  28.5 18.9 %copy-start.2 = (f32[512,128]{1,0:T(8,128)S(1)}, f32[512,128]{1,0:T(8,128)}, u32[]{:S(2)}) copy-start(f32[512,128]{1,0:T(8,128)} %constant.12.clone.blocks) | copy-start | bytes 786436
  28.5 53.9 %collective-permute-start.10 = (f32[512,128]{1,0:T(8,128)S(1)}, f32[512,128]{1,0:T(8,128)S(1)}, u32[]{:S(2)}, u32[]{:S(2)}) collective-permute-start(f32[512,128]{1,0:T(8,128)S(1)} %shard_map.58), channel_id=1, source_target_pairs={{0,8},{1,9},{2,10},{3,11},{4,12},{5,13},{6,14},{7,15},{8,0},{9,1},... | collective-permute-start | bytes 786440 | tf_op jit(solution)/shard_map/ppermute | solution.py:367
  44.1 42.8 %collective-permute-start.8 = (f32[512,128]{1,0:T(8,128)S(1)}, f32[512,128]{1,0:T(8,128)S(1)}, u32[]{:S(2)}, u32[]{:S(2)}) collective-permute-start(f32[512,128]{1,0:T(8,128)S(1)} %shard_map.56), channel_id=1, source_target_pairs={{0,8},{1,9},{2,10},{3,11},{4,12},{5,13},{6,14},{7,15},{8,0},{9,1},... | collective-permute-start | bytes 786440 | tf_op jit(solution)/shard_map/ppermute | solution.py:367
  47.9 9.8 %collective-permute-start = (f32[512,128]{1,0:T(8,128)S(1)}, f32[512,128]{1,0:T(8,128)S(1)}, u32[]{:S(2)}, u32[]{:S(2)}) collective-permute-start(f32[512,128]{1,0:T(8,128)S(1)} %branch_1_fun.7), channel_id=1, source_target_pairs={{0,256},{32,288},{64,320},{96,352},{128,384},{160,416},{192,448},{... | collective-permute-start | bytes 786440 | tf_op jit(solution)/shard_map/cond/branch_1_fun/ppermute | solution.py:367
  57.6 5.9 %copy-start = (bf16[8192,128]{1,0:T(8,128)(2,1)S(1)}, bf16[8192,128]{1,0:T(8,128)(2,1)}, u32[]{:S(2)}) copy-start(bf16[8192,128]{1,0:T(8,128)(2,1)} %get-tuple-element.15.ang) | copy-start | bytes 6291460 | tf_op jit(solution)/shard_map/cond
  60.0 8.3 %collective-permute-start.1 = (f32[512,128]{1,0:T(8,128)S(1)}, f32[512,128]{1,0:T(8,128)S(1)}, u32[]{:S(2)}, u32[]{:S(2)}) collective-permute-start(f32[512,128]{1,0:T(8,128)S(1)} %branch_1_fun.10), channel_id=1, source_target_pairs={{0,16},{1,17},{2,18},{3,19},{4,20},{5,21},{6,22},{7,23},{8,24},{9,... | collective-permute-start | bytes 786440 | tf_op jit(solution)/shard_map/cond/branch_1_fun/ppermute | solution.py:367
  68.9 9.8 %collective-permute-start.2 = (f32[512,128]{1,0:T(8,128)S(1)}, f32[512,128]{1,0:T(8,128)S(1)}, u32[]{:S(2)}, u32[]{:S(2)}) collective-permute-start(f32[512,128]{1,0:T(8,128)S(1)} %branch_1_fun.12), channel_id=1, source_target_pairs={{0,128},{32,160},{64,192},{96,224},{128,0},{160,32},{192,64},{224,... | collective-permute-start | bytes 786440 | tf_op jit(solution)/shard_map/cond/branch_1_fun/ppermute | solution.py:367

commit v5 on v4

--- a/solution.py
+++ b/solution.py
@@ -25,7 +25,7 @@
     return [float(v) for v in sine.coef], [float(v) for v in cosine.coef]
 
 
-COST_A, COST_B = 7 * 1024 * 1024, 4 * 1024 * 1024
+AHEAD = 0
 SINE, COSINE = half_angle_polys()
 
 
@@ -72,7 +72,7 @@
 
 
 def expand(blocks, outs):
-    for out in outs:
+    for out in outs[:4]:
         out[...] = jnp.zeros_like(out)
     for axis in range(2):
         for a in range(2):
@@ -80,6 +80,10 @@
                 part = blocks[pl.ds(((axis * 2 + a) * 2 + slot) * SQUARE, SQUARE), :]
                 high = part.astype(jnp.bfloat16)
                 low = (part - high.astype(jnp.float32)).astype(jnp.bfloat16)
+                if axis == 1 and len(outs) > 4:
+                    at = pl.ds(slot * SQUARE, SQUARE), pl.ds(a * CH, CH)
+                    outs[4][at] = high
+                    outs[5][at] = low
                 for k in range(2):
                     rows = pl.ds(slot * CH + k * SQUARE, SQUARE)
                     columns = pl.ds((2 * a + k) * CH, CH)
@@ -95,44 +99,28 @@
     return pltpu.CompilerParams(vmem_limit_bytes=mib * 1024 * 1024)
 
 
-PIECES = 8
-
-
 def load_kernel(angles, blocks, near_angles, *rest):
-    near_blocks, sems = rest[-2:]
-    first = pltpu.make_async_copy(blocks, near_blocks, sems.at[PIECES])
-    first.start()
-    rows = angles.shape[0] // PIECES
-    copies = []
-    for i in range(PIECES):
-        part = pl.ds(i * rows, rows)
-        copies.append(
-            pltpu.make_async_copy(angles.at[part], near_angles.at[part], sems.at[i])
-        )
-        copies[-1].start()
-    first.wait()
-    expand(near_blocks, rest[:-2])
-    for copy in copies:
-        copy.wait()
+    sem = rest[-1]
+    copy = pltpu.make_async_copy(angles, near_angles, sem)
+    copy.start()
+    expand(blocks, rest[:-1])
+    copy.wait()
 
 
 def load(angles):
     part = jax.ShapeDtypeStruct((2 * CH, 4 * CH), jnp.bfloat16)
-    blocks = jnp.asarray(child_blocks())
     return pl.pallas_call(
         load_kernel,
-        out_shape=[jax.ShapeDtypeStruct(angles.shape, angles.dtype)] + [part] * 4,
-        in_specs=[HBM, HBM],
-        out_specs=[VMEM] * 5,
-        scratch_shapes=[
-            pltpu.VMEM(blocks.shape, blocks.dtype),
-            pltpu.SemaphoreType.DMA((PIECES + 1,)),
-        ],
-        compiler_params=limits(48),
+        out_shape=[jax.ShapeDtypeStruct(angles.shape, angles.dtype)] + [part] * 4
+        + [jax.ShapeDtypeStruct((CH, 2 * CH), jnp.bfloat16)] * 2,
+        in_specs=[HBM, VMEM],
+        out_specs=[VMEM] * 7,
+        scratch_shapes=[pltpu.SemaphoreType.DMA(())],
+        compiler_params=limits(),
         cost_estimate=pl.CostEstimate(
             flops=0, bytes_accessed=4 * 1024 * 1024, transcendentals=0
         ),
-    )(angles, blocks)
+    )(angles, jnp.asarray(child_blocks()))
 
 
 def tables_kernel(blocks, *outs):
@@ -176,9 +164,9 @@
         in_specs=[HBM],
         out_specs=[VMEM] * len(sizes),
         scratch_shapes=[pltpu.SemaphoreType.DMA((parts,))],
-        compiler_params=limits(48),
+        compiler_params=limits(),
         cost_estimate=pl.CostEstimate(
-            flops=0, bytes_accessed=20 * 1024 * 1024, transcendentals=0
+            flops=20_000_000_000, bytes_accessed=4 * 1024 * 1024, transcendentals=0
         ),
     )(weights)
 
@@ -239,58 +227,20 @@
         pl.loop(0, n // tile)(step)
 
 
-def far_kernel(level, segments, tile, move, own, arr, ang, high, low, out, scratch, *rest):
-    near_ang, near_high, near_low, near_own, sems = rest
-    parts, copies, moved, at = segments(), [], [], 0
-    for row_own, row_arr, row_ang, row_out, n in parts:
-        pairs = [(ang.at[pl.ds(row_ang, 2 * n)], near_ang.at[pl.ds(2 * at, 2 * n)])]
-        if move:
-            pairs.append((own.at[pl.ds(row_own, n)], near_own.at[pl.ds(at, n)]))
-        copies += pairs
-        moved.append((at if move else row_own, row_arr, 2 * at, row_out, n))
-        at += n
-    copies += [(high, near_high), (low, near_low)]
-    copies = [
-        pltpu.make_async_copy(source, target, sems.at[i])
-        for i, (source, target) in enumerate(copies)
-    ]
-    for copy in copies:
-        copy.start()
-    for copy in copies:
-        copy.wait()
-    level_kernel(
-        level, lambda: moved, tile, near_own if move else own, arr, near_ang, near_high, near_low,
-        out, scratch,
-    )
-
-
-def level_call(level, segments, own, arr, ang, table, rows, far=False):
+def level_call(level, segments, own, arr, ang, table, rows, weight=0):
     steps = -(-rows // 512)
     tile = rows // 2 // steps
     kernel = functools.partial(level_kernel, level, segments, tile)
     scratch = [pltpu.VMEM((2 * tile, CH), jnp.float32)]
-    specs = [VMEM] * 5
-    if far:
-        move = level == 0
-        kernel = functools.partial(far_kernel, level, segments, tile, move)
-        scratch += [
-            pltpu.VMEM((rows, CH), jnp.bfloat16),
-            pltpu.VMEM((2 * CH, 4 * CH), jnp.bfloat16),
-            pltpu.VMEM((2 * CH, 4 * CH), jnp.bfloat16),
-            pltpu.VMEM((rows // 2, CH), jnp.float32),
-            pltpu.SemaphoreType.DMA((6,)),
-        ]
-        anywhere = pl.BlockSpec(memory_space=pl.ANY)
-        specs = [anywhere if move else VMEM, VMEM] + [anywhere] * 3
     return pl.pallas_call(
         kernel,
         out_shape=jax.ShapeDtypeStruct((rows, CH), jnp.float32),
-        in_specs=specs,
+        in_specs=[VMEM] * 5,
         out_specs=VMEM,
         scratch_shapes=scratch,
         compiler_params=limits(),
         cost_estimate=pl.CostEstimate(
-            flops=0, bytes_accessed=rows * 8 * 1024, transcendentals=0
+            flops=weight * 1_000_000_000, bytes_accessed=rows * 8 * 1024, transcendentals=0
         ),
     )(own, arr, ang, *table)
 
@@ -313,7 +263,7 @@
     )(far)
 
 
-def last_kernel(row, own, arr, ang, high, low, *rest):
+def direct_kernel(row, own, arr, ang, high, low, *rest):
     out, scratch, near_out, sems = rest[-4:]
     count, rows = near_out.shape[:2]
     tile = rows // 2
@@ -332,31 +282,115 @@
         copy.wait()
 
 
-def last_call(own, arr, ang, table, row, earlier, boxes, cost):
+def direct_call(own, arr, ang, table, row, boxes):
     rows = arr.shape[0]
     count = -(-rows // 256)
     tile = rows // count
-    operands = [own, arr, ang, *table]
-    specs = [VMEM] * 5
-    aliases = {}
-    if earlier is not None:
-        aliases = {len(operands): 0}
-        operands.append(earlier)
-        specs.append(HBM)
-    return pl.pallas_call(
-        functools.partial(last_kernel, row),
+    return pl.pallas_call(
+        functools.partial(direct_kernel, row),
         out_shape=jax.ShapeDtypeStruct((boxes, CH), jnp.float32),
-        in_specs=specs,
+        in_specs=[VMEM] * 5,
         out_specs=HBM,
         scratch_shapes=[
             pltpu.VMEM((2 * tile, CH), jnp.float32),
             pltpu.VMEM((count, 2 * tile, CH), jnp.float32),
             pltpu.SemaphoreType.DMA((count,)),
         ],
-        input_output_aliases=aliases,
         compiler_params=limits(),
         cost_estimate=pl.CostEstimate(
-            flops=0, bytes_accessed=cost, transcendentals=0
+            flops=0, bytes_accessed=rows * 8 * 1024, transcendentals=0
+        ),
+    )(own, arr, ang, *table)
+
+
+def spread_last(x, high, low, scratch):
+    n = x.shape[0]
+    x_hi = x.astype(jnp.bfloat16)
+    x_lo = (x - x_hi.astype(jnp.float32)).astype(jnp.bfloat16)
+    dot = functools.partial(jnp.dot, preferred_element_type=jnp.float32)
+    y = dot(x_hi, high[...]) + (dot(x_lo, high[...]) + dot(x_hi, low[...]))
+    for a in range(2):
+        scratch[pl.ds(a, n, stride=2), :] = y[:, a * CH : (a + 1) * CH]
+    return scratch[...]
+
+
+def before_kernel(row, tile, own, ang, high, low, part, cos_out, sin_out, scratch):
+    upper = own_bit(3) == 1
+
+    def step(i):
+        rows = pl.ds(pl.multiple_of(2 * i * tile, 2 * tile), 2 * tile)
+        near = pl.ds(pl.multiple_of(row + i * tile, tile), tile)
+        y = spread_last(own[near, :], high, low, scratch)
+        at = pl.ds(pl.multiple_of(2 * (row + i * tile), 2 * tile), 2 * tile)
+        c, s = cos_sin(ang[at, :].astype(jnp.float32))
+        left = lax.broadcasted_iota(jnp.int32, c.shape, 1) < SQUARE
+        c_far, s_far = pltpu.roll(c, SQUARE, 1), pltpu.roll(s, SQUARE, 1)
+        c0, c1 = jnp.where(left, c, c_far), jnp.where(left, c_far, c)
+        s0, s1 = jnp.where(left, -s, s_far), jnp.where(left, -s_far, s)
+        part[rows, :] = jnp.where(upper, c1, c0) * y + jnp.where(upper, s1, s0) * pltpu.roll(
+            y, SQUARE, 1
+        )
+        cos_out[rows, :] = jnp.where(upper, c0, c1)
+        sin_out[rows, :] = jnp.where(upper, s0, s1)
+
+    pl.loop(0, part.shape[0] // (2 * tile))(step)
+
+
+def before_call(own, ang, table, row):
+    tile = 128
+    part = jax.ShapeDtypeStruct((2 * (own.shape[0] - row), CH), jnp.float32)
+    return pl.pallas_call(
+        functools.partial(before_kernel, row, tile),
+        out_shape=[part] * 3,
+        in_specs=[VMEM] * 4,
+        out_specs=[VMEM] * 3,
+        scratch_shapes=[pltpu.VMEM((2 * tile, CH), jnp.float32)],
+        compiler_params=limits(),
+        cost_estimate=pl.CostEstimate(
+            flops=0, bytes_accessed=4 * 1024 * 1024, transcendentals=0
+        ),
+    )(own, ang, *table)
+
+
+def last_kernel(row, arr, part, cos_in, sin_in, high, low, *rest):
+    out, scratch, near_out, sems = rest[-4:]
+    count, rows = near_out.shape[:2]
+    tile = rows // 2
+    copies = []
+    for i in range(count):
+        at = pl.ds(i * rows, rows)
+        y = spread_last(arr[pl.ds(i * tile, tile), :], high, low, scratch)
+        near_out[i] = (
+            part[at, :] + cos_in[at, :] * y + sin_in[at, :] * pltpu.roll(y, SQUARE, 1)
+        )
+        copy = pltpu.make_async_copy(
+            near_out.at[i], out.at[pl.ds(2 * row + i * rows, rows)], sems.at[i]
+        )
+        copy.start()
+        copies.append(copy)
+    for copy in copies:
+        copy.wait()
+
+
+def last_call(arr, ready, table, row, earlier):
+    rows = arr.shape[0]
+    tile = 128
+    count = rows // tile
+    operands = [arr, *ready, *table, earlier]
+    return pl.pallas_call(
+        functools.partial(last_kernel, row),
+        out_shape=jax.ShapeDtypeStruct(earlier.shape, jnp.float32),
+        in_specs=[VMEM] * 6 + [HBM],
+        out_specs=HBM,
+        scratch_shapes=[
+            pltpu.VMEM((2 * tile, CH), jnp.float32),
+            pltpu.VMEM((count, 2 * tile, CH), jnp.float32),
+            pltpu.SemaphoreType.DMA((count,)),
+        ],
+        input_output_aliases={6: 0},
+        compiler_params=limits(),
+        cost_estimate=pl.CostEstimate(
+            flops=0, bytes_accessed=rows * 8 * 1024, transcendentals=0
         ),
     )(*operands)
 
@@ -379,8 +413,8 @@
     far = weights.reshape(boxes, CH)
     ang, *ready = load(angles.reshape(4 * boxes, CH))
     w2 = far
-    tab_x, tab_y = ready[:2], ready[2:]
-    env = [ang, tab_x, tab_y, w2, False]
+    tab_x, tab_y, tab_last = ready[:2], ready[2:4], ready[4:]
+    env = [ang, tab_x, tab_y, w2]
     ang_far = angles.reshape(4 * boxes, CH)
     aligned = lambda row: pl.multiple_of(row, 16)
 
@@ -398,7 +432,7 @@
         taken = take(far, rows, [4 * n for _, n in chunks], 4 * len(chunks))
         return [from_partner(part, "gx", bits_x - 1) for part in taken]
 
-    def level0(chunk, given, arr, send):
+    def level0(chunk, given, arr, send, weight=0):
         at, n = chunk
 
         def segments():
@@ -417,9 +451,9 @@
                 )
             return parts
 
-        return level_call(0, segments, env[3], arr, env[0], env[1], 4 * n, env[4])
-
-    def level1(chunk, given, own, arr, send):
+        return level_call(0, segments, env[3], arr, env[0], env[1], 4 * n, weight)
+
+    def level1(chunk, given, own, arr, send, weight=0):
         at, n = chunk
 
         def segments():
@@ -427,16 +461,16 @@
             row = aligned(t2 * 2 * n)
             return [(row, row, aligned(boxes + (t2 * 2 + t3) * 4 * base + 4 * at), 0, 2 * n)]
 
-        return level_call(1, segments, own, arr, env[0], env[2], 4 * n, env[4])
-
-    def level2(chunk, given, own, arr):
+        return level_call(1, segments, own, arr, env[0], env[2], 4 * n, weight)
+
+    def level2(chunk, given, own, arr, weight=0):
         at, n = chunk
 
         def segments():
             t3 = target(3, given)
             return [(0, 0, aligned(2 * boxes + t3 * 8 * base + 8 * at), 0, 4 * n)]
 
-        return level_call(2, segments, own, arr, env[0], env[1], 8 * n, env[4])
+        return level_call(2, segments, own, arr, env[0], env[1], 8 * n, weight)
 
     def swap1(part):
         return from_partner(part, "gy", bits_y - 1)
@@ -450,19 +484,19 @@
     cut = base // 2
     a, b, k = (0, cut), (cut, base - cut), (0, base)
     arr_a, arr_b = first([a, b], True)
-    send_a = level0(a, True, arr_a, True)
+    send_a = level0(a, True, arr_a, True, AHEAD)
     arr1_a = swap1(send_a)
-    keep_a = level0(a, True, after(arr_a, send_a), False)
+    keep_a = level0(a, True, after(arr_a, send_a), False, AHEAD)
     send_b = level0(b, True, after(arr_b, keep_a), True)
     arr1_b = swap1(send_b)
-    send_a = level1(a, True, keep_a, after(arr1_a, send_b), True)
+    send_a = level1(a, True, keep_a, after(arr1_a, send_b), True, AHEAD)
     arr2_a = swap2(send_a)
     keep_b = level0(b, True, after(arr_b, send_a), False)
     send_b = level1(b, True, keep_b, arr1_b, True)
     arr2_b = swap2(send_b)
     keep_b = level1(b, True, keep_b, arr1_b, False)
     keep_a = level1(a, True, keep_a, arr1_a, False)
-    given_a = level2(a, True, keep_a, after(arr2_a, send_b, keep_b))
+    given_a = level2(a, True, keep_a, after(arr2_a, send_b))
     z_a = swap3(given_a)
 
     given_b = level2(b, True, keep_b, arr2_b)
@@ -474,7 +508,7 @@
         nonlocal far
         far = w2
         ready = make_tables(blocks)
-        env[:] = [ang, ready[:2], ready[2:], w2, False]
+        env[:] = [ang, ready[:2], ready[2:], w2]
         (arr_k,) = first([k], False)
         arr1_k = swap1(level0(k, False, arr_k, True))
         keep_k = level0(k, False, arr_k, False)
@@ -487,8 +521,9 @@
     )
     near_ang = fetch(after(ang_far, kept), 3 * boxes, boxes)
     kept = after(kept, near_ang)
-    out = last_call(kept, z_a, near_ang, tab_y, 0, None, boxes, COST_A)
-    out = last_call(kept, z_b, near_ang, tab_y, 8 * cut, out, boxes, COST_B)
+    done = before_call(kept, near_ang, tab_last, 8 * cut)
+    out = direct_call(after(kept, done[0]), z_a, near_ang, tab_y, 0, boxes)
+    out = last_call(z_b, done, tab_last, 8 * cut, out)
     return out.reshape(1, 1, boxes, CH)
 
 

time: 89.2 us -> 88.2 us (0.989)
  Pallas kernels: 17.7 us -> 15.3 us
  waiting for transfers between devices: 18.4 us -> 20.5 us
    pallas_call x0 -> x2, Pallas kernels: none -> 2.99 us  [the longest x1 1.81 us: direct_call(): pl.pallas_call(functools.partial(direct_kernel, row), out_shape=jax.Shape...]
    pallas_call x2 -> x1, Pallas kernels: 3.63 us -> 1.23 us  [last_call(): pl.pallas_call(functools.partial(last_kernel, row), out_shape=jax.ShapeDt...]
    ppermute x11, waiting for transfers between devices: 18.4 us -> 20.5 us  [from_partner(): return lax.ppermute(block, axis, route)]
    pallas_call x15, Pallas kernels: 9.82 us -> 8.07 us  [level_call(): pl.pallas_call(kernel, out_shape=jax.ShapeDtypeStruct((rows, CH), jnp.flo...]
    pallas_call x1, Pallas kernels: 1.66 us -> 0.31 us  [load(): pl.pallas_call(load_kernel, out_shape=[jax.ShapeDtypeStruct(angles.shape,...]
  transfers between devices with their start and end apart: 11 -> 11, of which waited for: 6 -> 7; matrix products, arithmetic and copies ran while one was open for 0% -> 0% of each run, Pallas kernels for 17% -> 15%
where the time goes in v5:
time: 88.2 us; the launch traced here: 87.8 us
  starting transfers between devices  51.8 us (59%)
  waiting for transfers between devices  20.5 us (23%)
  Pallas kernels  15.3 us (17%)
    ppermute x11, starting transfers between devices, from_partner(): return lax.ppermute(block, axis, route)  51.8 us
    ppermute x11, waiting for transfers between devices, from_partner(): return lax.ppermute(block, axis, route)  20.5 us
    pallas_call x15, Pallas kernels, level_call(): pl.pallas_call(kernel, out_shape=jax.ShapeDtypeStruct((rows, CH), jnp.flo...  8.07 us
    pallas_call x1, Pallas kernels, direct_call(): pl.pallas_call(functools.partial(direct_kernel, row), out_shape=jax.Shape...  1.81 us
  transfers between devices with their start and end apart: 11, of which 7 were waited for; matrix products, arithmetic and copies ran while one was open for 0% of the time, Pallas kernels for 15%

profile of v5, /device:TPU:32, one launch (start us, length us, event | category | flops | bytes accessed | tf_op | source)
XLA Modules:
  0.0 87.8 jit_solution(7797946194378265960)
XLA Ops:
  0.0 1.1 %shard_map.46 = (f32[256,128]{1,0:T(8,128)S(1)}, f32[256,128]{1,0:T(8,128)S(1)}) custom-call(f32[2048,128]{1,0:T(8,128)} %bitcast.6), custom_call_target="tpu_custom_call" | custom-call | flops 20000000000 | bytes 4194304 | tf_op jit(solution)/shard_map/pallas_call | solution.py:161
  1.1 5.2 %collective-permute-start.4 = (f32[256,128]{1,0:T(8,128)S(1)}, f32[256,128]{1,0:T(8,128)S(1)}, u32[]{:S(2)}, u32[]{:S(2)}) collective-permute-start(f32[256,128]{1,0:T(8,128)S(1)} %get-tuple-element.42), channel_id=1, source_target_pairs={{0,256},{32,288},{64,320},{96,352},{128,384},{160,416},{192,448},{... | collective-permute-start | bytes 393224 | tf_op jit(solution)/shard_map/ppermute | solution.py:401
  6.4 2.2 %collective-permute-start.3 = (f32[256,128]{1,0:T(8,128)S(1)}, f32[256,128]{1,0:T(8,128)S(1)}, u32[]{:S(2)}, u32[]{:S(2)}) collective-permute-start(f32[256,128]{1,0:T(8,128)S(1)} %get-tuple-element.41), channel_id=1, source_target_pairs={{0,256},{32,288},{64,320},{96,352},{128,384},{160,416},{192,448},{... | collective-permute-start | bytes 393224 | tf_op jit(solution)/shard_map/ppermute | solution.py:401
  8.9 1.0 %collective-permute-done.4.arr = f32[256,128]{1,0:T(8,128)S(1)} collective-permute-done((f32[256,128]{1,0:T(8,128)S(1)}, f32[256,128]{1,0:T(8,128)S(1)}, u32[]{:S(2)}, u32[]{:S(2)}) %collective-permute-start.4) | collective-permute-done | bytes 131104 | tf_op jit(solution)/shard_map/ppermute | solution.py:401
  10.3 3.4 %collective-permute-start.5 = (f32[256,128]{1,0:T(8,128)S(1)}, f32[256,128]{1,0:T(8,128)S(1)}, u32[]{:S(2)}, u32[]{:S(2)}) collective-permute-start(f32[256,128]{1,0:T(8,128)S(1)} %shard_map.48), channel_id=1, source_target_pairs={{0,16},{1,17},{2,18},{3,19},{4,20},{5,21},{6,22},{7,23},{8,24},{9,... | collective-permute-start | bytes 393224 | tf_op jit(solution)/shard_map/ppermute | solution.py:401
  15.1 2.6 %collective-permute-start.6 = (f32[256,128]{1,0:T(8,128)S(1)}, f32[256,128]{1,0:T(8,128)S(1)}, u32[]{:S(2)}, u32[]{:S(2)}) collective-permute-start(f32[256,128]{1,0:T(8,128)S(1)} %shard_map.50), channel_id=1, source_target_pairs={{0,16},{1,17},{2,18},{3,19},{4,20},{5,21},{6,22},{7,23},{8,24},{9,... | collective-permute-start | bytes 393224 | tf_op jit(solution)/shard_map/ppermute | solution.py:401
  18.1 4.9 %collective-permute-start.9 = (f32[256,128]{1,0:T(8,128)S(1)}, f32[256,128]{1,0:T(8,128)S(1)}, u32[]{:S(2)}, u32[]{:S(2)}) collective-permute-start(f32[256,128]{1,0:T(8,128)S(1)} %shard_map.51), channel_id=1, source_target_pairs={{0,128},{32,160},{64,192},{96,224},{128,0},{160,32},{192,64},{224,... | collective-permute-start | bytes 393224 | tf_op jit(solution)/shard_map/ppermute | solution.py:401
  23.8 3.4 %collective-permute-start.7 = (f32[256,128]{1,0:T(8,128)S(1)}, f32[256,128]{1,0:T(8,128)S(1)}, u32[]{:S(2)}, u32[]{:S(2)}) collective-permute-start(f32[256,128]{1,0:T(8,128)S(1)} %shard_map.54), channel_id=1, source_target_pairs={{0,128},{32,160},{64,192},{96,224},{128,0},{160,32},{192,64},{224,... | collective-permute-start | bytes 393224 | tf_op jit(solution)/shard_map/ppermute | solution.py:401
  28.7 14.8 %collective-permute-start.10 = (f32[512,128]{1,0:T(8,128)S(1)}, f32[512,128]{1,0:T(8,128)S(1)}, u32[]{:S(2)}, u32[]{:S(2)}) collective-permute-start(f32[512,128]{1,0:T(8,128)S(1)} %shard_map.59), channel_id=1, source_target_pairs={{0,8},{1,9},{2,10},{3,11},{4,12},{5,13},{6,14},{7,15},{8,0},{9,1},... | collective-permute-start | bytes 786440 | tf_op jit(solution)/shard_map/ppermute | solution.py:401
  44.2 3.5 %collective-permute-start.8 = (f32[512,128]{1,0:T(8,128)S(1)}, f32[512,128]{1,0:T(8,128)S(1)}, u32[]{:S(2)}, u32[]{:S(2)}) collective-permute-start(f32[512,128]{1,0:T(8,128)S(1)} %shard_map.55), channel_id=1, source_target_pairs={{0,8},{1,9},{2,10},{3,11},{4,12},{5,13},{6,14},{7,15},{8,0},{9,1},... | collective-permute-start | bytes 786440 | tf_op jit(solution)/shard_map/ppermute | solution.py:401
  47.6 31.3 %conditional.1 = (f32[1024,128]{1,0:T(8,128)S(1)}) conditional(s32[]{:T(128)} %convert_element_type.3, () %tuple.24, (f32[2048,128]{1,0:T(8,128)S(1)}, f32[512,128]{1,0:T(8,128)S(1)}, bf16[8192,128]{1,0:T(8,128)(2,1)}) %tuple.34), branch_computations={%region_0.0_spmd, %region_1.0_spmd} | conditional | flops 20000000000 | bytes 41943196 | solution.py:519
  48.1 6.1 %collective-permute-start = (f32[512,128]{1,0:T(8,128)S(1)}, f32[512,128]{1,0:T(8,128)S(1)}, u32[]{:S(2)}, u32[]{:S(2)}) collective-permute-start(f32[512,128]{1,0:T(8,128)S(1)} %branch_1_fun.7), channel_id=1, source_target_pairs={{0,256},{32,288},{64,320},{96,352},{128,384},{160,416},{192,448},{... | collective-permute-start | bytes 786440 | tf_op jit(solution)/shard_map/cond/branch_1_fun/ppermute | solution.py:401
  54.3 4.2 %collective-permute-done.arr = f32[512,128]{1,0:T(8,128)S(1)} collective-permute-done((f32[512,128]{1,0:T(8,128)S(1)}, f32[512,128]{1,0:T(8,128)S(1)}, u32[]{:S(2)}, u32[]{:S(2)}) %collective-permute-start) | collective-permute-done | bytes 262176 | tf_op jit(solution)/shard_map/cond/branch_1_fun/ppermute | solution.py:401
  59.1 2.7 %collective-permute-start.1 = (f32[512,128]{1,0:T(8,128)S(1)}, f32[512,128]{1,0:T(8,128)S(1)}, u32[]{:S(2)}, u32[]{:S(2)}) collective-permute-start(f32[512,128]{1,0:T(8,128)S(1)} %branch_1_fun.10), channel_id=1, source_target_pairs={{0,16},{1,17},{2,18},{3,19},{4,20},{5,21},{6,22},{7,23},{8,24},{9,... | collective-permute-start | bytes 786440 | tf_op jit(solution)/shard_map/cond/branch_1_fun/ppermute | solution.py:401
  62.4 4.9 %collective-permute-done.1.arr = f32[512,128]{1,0:T(8,128)S(1)} collective-permute-done((f32[512,128]{1,0:T(8,128)S(1)}, f32[512,128]{1,0:T(8,128)S(1)}, u32[]{:S(2)}, u32[]{:S(2)}) %collective-permute-start.1) | collective-permute-done | bytes 262176 | tf_op jit(solution)/shard_map/cond/branch_1_fun/ppermute | solution.py:401
  68.0 2.9 %collective-permute-start.2 = (f32[512,128]{1,0:T(8,128)S(1)}, f32[512,128]{1,0:T(8,128)S(1)}, u32[]{:S(2)}, u32[]{:S(2)}) collective-permute-start(f32[512,128]{1,0:T(8,128)S(1)} %branch_1_fun.12), channel_id=1, source_target_pairs={{0,128},{32,160},{64,192},{96,224},{128,0},{160,32},{192,64},{224,... | collective-permute-start | bytes 786440 | tf_op jit(solution)/shard_map/cond/branch_1_fun/ppermute | solution.py:401
  71.5 6.2 %collective-permute-done.2.arr = f32[512,128]{1,0:T(8,128)S(1)} collective-permute-done((f32[512,128]{1,0:T(8,128)S(1)}, f32[512,128]{1,0:T(8,128)S(1)}, u32[]{:S(2)}, u32[]{:S(2)}) %collective-permute-start.2) | collective-permute-done | bytes 262176 | tf_op jit(solution)/shard_map/cond/branch_1_fun/ppermute | solution.py:401
  77.7 1.2 %branch_1_fun.13 = f32[1024,128]{1,0:T(8,128)S(1)} custom-call(f32[512,128]{1,0:T(8,128)S(1)} %branch_1_fun.11.own, f32[512,128]{1,0:T(8,128)S(1)} %collective-permute-done.2.arr, bf16[8192,128]{1,0:T(8,128)(2,1)S(1)} %copy-done.1, bf16[256,512]{1,0:T(8,128)(2,1)S(1)} %get-tuple-element.17.high, bf16[256,512]{1,0:T(8,128)(2,1)S(1)} %get-tuple-element.18.low), custom_call_target="tpu_custom_call" | custom-call | bytes 8388608 | tf_op jit(solution)/shard_map/cond/branch_1_fun/pallas_call | solution.py:235
  79.0 1.1 %shard_map.56.ang = bf16[2048,128]{1,0:T(8,128)(2,1)S(1)} custom-call(bf16[8192,128]{1,0:T(8,128)(2,1)} %bitcast.4), custom_call_target="tpu_custom_call" | custom-call | bytes 1048576 | tf_op jit(solution)/shard_map/pallas_call | solution.py:255
  80.0 1.2 %shard_map.57 = (f32[1024,128]{1,0:T(8,128)S(1)}, f32[1024,128]{1,0:T(8,128)S(1)}, f32[1024,128]{1,0:T(8,128)S(1)}) custom-call(f32[1024,128]{1,0:T(8,128)S(1)} %get-tuple-element.61.own, bf16[2048,128]{1,0:T(8,128)(2,1)S(1)} %shard_map.56.ang, bf16[128,256]{1,0:T(8,128)(2,1)S(1)} %get-tuple-element.54.high, bf16[128,256]{1,0:T(8,128)(2,1)S(1)} %get-tuple-element.55.low), custom_call_target="tpu_custom_call" | custom-call | bytes 4194304 | tf_op jit(solution)/shard_map/pallas_call | solution.py:342
  81.2 0.8 collective-permute-done.10.arr
  82.0 1.8 %shard_map.60.rest_0_ = f32[2048,128]{1,0:T(8,128)} custom-call(f32[1024,128]{1,0:T(8,128)S(1)} %get-tuple-element.61.own, f32[512,128]{1,0:T(8,128)S(1)} %collective-permute-done.10.arr, bf16[2048,128]{1,0:T(8,128)(2,1)S(1)} %shard_map.56.ang, bf16[256,512]{1,0:T(8,128)(2,1)S(1)} %get-tuple-element.49.high, bf16[256,512]{1,0:T(8,128)(2,1)S(1)} %get-tuple-element.50.low), custom_call_target="tpu_custom_call" | custom-call | bytes 4194304 | tf_op jit(solution)/shard_map/pallas_call | solution.py:289
  83.8 2.7 %collective-permute-done.8.arr = f32[512,128]{1,0:T(8,128)S(1)} collective-permute-done((f32[512,128]{1,0:T(8,128)S(1)}, f32[512,128]{1,0:T(8,128)S(1)}, u32[]{:S(2)}, u32[]{:S(2)}) %collective-permute-start.8) | collective-permute-done | bytes 262176 | tf_op jit(solution)/shard_map/ppermute | solution.py:401
  86.5 1.2 %shard_map.61 = f32[2048,128]{1,0:T(8,128)} custom-call(f32[512,128]{1,0:T(8,128)S(1)} %collective-permute-done.8.arr, f32[1024,128]{1,0:T(8,128)S(1)} %get-tuple-element.56.part, f32[1024,128]{1,0:T(8,128)S(1)} %get-tuple-element.57.cos_in, f32[1024,128]{1,0:T(8,128)S(1)} %get-tuple-element.58.sin_in, ...), custom_call_target="tpu_custom_call", output_to_operand_aliasing={{}: (6, {})} | custom-call | bytes 4194304 | tf_op jit(solution)/shard_map/pallas_call | solution.py:380
  (30 shorter events, 8.3 us)
Async XLA Ops:
  0.0 8.6 %copy-start = (bf16[4,1,1,2048,128]{4,3,2,1,0:T(8,128)(2,1)S(1)}, bf16[4,1,1,2048,128]{4,3,2,1,0:T(8,128)(2,1)}, u32[]{:S(2)}) copy-start(bf16[4,1,1,2048,128]{4,3,2,1,0:T(8,128)(2,1)} %param.7) | copy-start | bytes 6291460
  0.0 8.6 %copy-start.3 = (f32[512,128]{1,0:T(8,128)S(1)}, f32[512,128]{1,0:T(8,128)}, u32[]{:S(2)}) copy-start(f32[512,128]{1,0:T(8,128)} %constant.12.clone.blocks) | copy-start | bytes 786436
  1.1 8.9 %copy-start.2 = (f32[1,1,2048,128]{3,2,1,0:T(8,128)S(1)}, f32[1,1,2048,128]{3,2,1,0:T(8,128)}, u32[]{:S(2)}) copy-start(f32[1,1,2048,128]{3,2,1,0:T(8,128)} %param.6) | copy-start | bytes 3145732
  1.1 8.8 %collective-permute-start.4 = (f32[256,128]{1,0:T(8,128)S(1)}, f32[256,128]{1,0:T(8,128)S(1)}, u32[]{:S(2)}, u32[]{:S(2)}) collective-permute-start(f32[256,128]{1,0:T(8,128)S(1)} %get-tuple-element.42), channel_id=1, source_target_pairs={{0,256},{32,288},{64,320},{96,352},{128,384},{160,416},{192,448},{... | collective-permute-start | bytes 393224 | tf_op jit(solution)/shard_map/ppermute | solution.py:401
  6.4 8.4 %collective-permute-start.3 = (f32[256,128]{1,0:T(8,128)S(1)}, f32[256,128]{1,0:T(8,128)S(1)}, u32[]{:S(2)}, u32[]{:S(2)}) collective-permute-start(f32[256,128]{1,0:T(8,128)S(1)} %get-tuple-element.41), channel_id=1, source_target_pairs={{0,256},{32,288},{64,320},{96,352},{128,384},{160,416},{192,448},{... | collective-permute-start | bytes 393224 | tf_op jit(solution)/shard_map/ppermute | solution.py:401
  10.3 7.4 %collective-permute-start.5 = (f32[256,128]{1,0:T(8,128)S(1)}, f32[256,128]{1,0:T(8,128)S(1)}, u32[]{:S(2)}, u32[]{:S(2)}) collective-permute-start(f32[256,128]{1,0:T(8,128)S(1)} %shard_map.48), channel_id=1, source_target_pairs={{0,16},{1,17},{2,18},{3,19},{4,20},{5,21},{6,22},{7,23},{8,24},{9,... | collective-permute-start | bytes 393224 | tf_op jit(solution)/shard_map/ppermute | solution.py:401
  15.1 8.3 %collective-permute-start.6 = (f32[256,128]{1,0:T(8,128)S(1)}, f32[256,128]{1,0:T(8,128)S(1)}, u32[]{:S(2)}, u32[]{:S(2)}) collective-permute-start(f32[256,128]{1,0:T(8,128)S(1)} %shard_map.50), channel_id=1, source_target_pairs={{0,16},{1,17},{2,18},{3,19},{4,20},{5,21},{6,22},{7,23},{8,24},{9,... | collective-permute-start | bytes 393224 | tf_op jit(solution)/shard_map/ppermute | solution.py:401
  18.1 10.0 %collective-permute-start.9 = (f32[256,128]{1,0:T(8,128)S(1)}, f32[256,128]{1,0:T(8,128)S(1)}, u32[]{:S(2)}, u32[]{:S(2)}) collective-permute-start(f32[256,128]{1,0:T(8,128)S(1)} %shard_map.51), channel_id=1, source_target_pairs={{0,128},{32,160},{64,192},{96,224},{128,0},{160,32},{192,64},{224,... | collective-permute-start | bytes 393224 | tf_op jit(solution)/shard_map/ppermute | solution.py:401
  23.8 19.7 %collective-permute-start.7 = (f32[256,128]{1,0:T(8,128)S(1)}, f32[256,128]{1,0:T(8,128)S(1)}, u32[]{:S(2)}, u32[]{:S(2)}) collective-permute-start(f32[256,128]{1,0:T(8,128)S(1)} %shard_map.54), channel_id=1, source_target_pairs={{0,128},{32,160},{64,192},{96,224},{128,0},{160,32},{192,64},{224,... | collective-permute-start | bytes 393224 | tf_op jit(solution)/shard_map/ppermute | solution.py:401
  28.7 53.3 %collective-permute-start.10 = (f32[512,128]{1,0:T(8,128)S(1)}, f32[512,128]{1,0:T(8,128)S(1)}, u32[]{:S(2)}, u32[]{:S(2)}) collective-permute-start(f32[512,128]{1,0:T(8,128)S(1)} %shard_map.59), channel_id=1, source_target_pairs={{0,8},{1,9},{2,10},{3,11},{4,12},{5,13},{6,14},{7,15},{8,0},{9,1},... | collective-permute-start | bytes 786440 | tf_op jit(solution)/shard_map/ppermute | solution.py:401
  44.2 42.4 %collective-permute-start.8 = (f32[512,128]{1,0:T(8,128)S(1)}, f32[512,128]{1,0:T(8,128)S(1)}, u32[]{:S(2)}, u32[]{:S(2)}) collective-permute-start(f32[512,128]{1,0:T(8,128)S(1)} %shard_map.55), channel_id=1, source_target_pairs={{0,8},{1,9},{2,10},{3,11},{4,12},{5,13},{6,14},{7,15},{8,0},{9,1},... | collective-permute-start | bytes 786440 | tf_op jit(solution)/shard_map/ppermute | solution.py:401
  47.6 10.9 %copy-start.1 = (bf16[8192,128]{1,0:T(8,128)(2,1)S(1)}, bf16[8192,128]{1,0:T(8,128)(2,1)}, u32[]{:S(2)}) copy-start(bf16[8192,128]{1,0:T(8,128)(2,1)} %get-tuple-element.15.ang) | copy-start | bytes 6291460 | tf_op jit(solution)/shard_map/cond
  48.1 10.4 %collective-permute-start = (f32[512,128]{1,0:T(8,128)S(1)}, f32[512,128]{1,0:T(8,128)S(1)}, u32[]{:S(2)}, u32[]{:S(2)}) collective-permute-start(f32[512,128]{1,0:T(8,128)S(1)} %branch_1_fun.7), channel_id=1, source_target_pairs={{0,256},{32,288},{64,320},{96,352},{128,384},{160,416},{192,448},{... | collective-permute-start | bytes 786440 | tf_op jit(solution)/shard_map/cond/branch_1_fun/ppermute | solution.py:401
  59.1 8.3 %collective-permute-start.1 = (f32[512,128]{1,0:T(8,128)S(1)}, f32[512,128]{1,0:T(8,128)S(1)}, u32[]{:S(2)}, u32[]{:S(2)}) collective-permute-start(f32[512,128]{1,0:T(8,128)S(1)} %branch_1_fun.10), channel_id=1, source_target_pairs={{0,16},{1,17},{2,18},{3,19},{4,20},{5,21},{6,22},{7,23},{8,24},{9,... | collective-permute-start | bytes 786440 | tf_op jit(solution)/shard_map/cond/branch_1_fun/ppermute | solution.py:401
  68.0 9.8 %collective-permute-start.2 = (f32[512,128]{1,0:T(8,128)S(1)}, f32[512,128]{1,0:T(8,128)S(1)}, u32[]{:S(2)}, u32[]{:S(2)}) collective-permute-start(f32[512,128]{1,0:T(8,128)S(1)} %branch_1_fun.12), channel_id=1, source_target_pairs={{0,128},{32,160},{64,192},{96,224},{128,0},{160,32},{192,64},{224,... | collective-permute-start | bytes 786440 | tf_op jit(solution)/shard_map/cond/branch_1_fun/ppermute | solution.py:401

commit v6 on v5

--- a/solution.py
+++ b/solution.py
@@ -25,7 +25,6 @@
     return [float(v) for v in sine.coef], [float(v) for v in cosine.coef]
 
 
-AHEAD = 0
 SINE, COSINE = half_angle_polys()
 
 
@@ -139,31 +138,28 @@
     )(blocks)
 
 
-def take_kernel(rows, weights, *rest):
+def take_kernel(pick, chunks, weights, *rest):
     outs, sems = rest[:-1], rest[-1]
-    copies = []
-    for out, parts in zip(outs, rows()):
-        at = 0
-        for row, n in parts:
-            copies.append(
-                pltpu.make_async_copy(
-                    weights.at[pl.ds(row, n)], out.at[pl.ds(at, n)], sems.at[len(copies)]
-                )
-            )
-            at += n
+    t0, t3 = pick()
+    copies = [
+        pltpu.make_async_copy(weights.at[t0, :, t3, pl.ds(at, n), :], out, sems.at[i])
+        for i, ((at, n), out) in enumerate(zip(chunks, outs))
+    ]
     for copy in copies:
         copy.start()
     for copy in copies:
         copy.wait()
 
 
-def take(weights, rows, sizes, parts):
-    return pl.pallas_call(
-        functools.partial(take_kernel, rows),
-        out_shape=[jax.ShapeDtypeStruct((n, CH), jnp.float32) for n in sizes],
+def take(weights, pick, chunks):
+    return pl.pallas_call(
+        functools.partial(take_kernel, pick, chunks),
+        out_shape=[
+            jax.ShapeDtypeStruct((weights.shape[1], n, CH), jnp.float32) for _, n in chunks
+        ],
         in_specs=[HBM],
-        out_specs=[VMEM] * len(sizes),
-        scratch_shapes=[pltpu.SemaphoreType.DMA((parts,))],
+        out_specs=[VMEM] * len(chunks),
+        scratch_shapes=[pltpu.SemaphoreType.DMA((len(chunks),))],
         compiler_params=limits(),
         cost_estimate=pl.CostEstimate(
             flops=20_000_000_000, bytes_accessed=4 * 1024 * 1024, transcendentals=0
@@ -227,7 +223,7 @@
         pl.loop(0, n // tile)(step)
 
 
-def level_call(level, segments, own, arr, ang, table, rows, weight=0):
+def level_call(level, segments, own, arr, ang, table, rows):
     steps = -(-rows // 512)
     tile = rows // 2 // steps
     kernel = functools.partial(level_kernel, level, segments, tile)
@@ -240,7 +236,7 @@
         scratch_shapes=scratch,
         compiler_params=limits(),
         cost_estimate=pl.CostEstimate(
-            flops=weight * 1_000_000_000, bytes_accessed=rows * 8 * 1024, transcendentals=0
+            flops=0, bytes_accessed=rows * 8 * 1024, transcendentals=0
         ),
     )(own, arr, ang, *table)
 
@@ -422,17 +418,13 @@
         return 1 - own_bit(k) if other else own_bit(k)
 
     def first(chunks, given):
-        def rows():
-            low = [target(3, given) + 2 * t for t in range(4)]
-            return [
-                [(aligned(((1 - own_bit(0)) * 8 + k) * base + at), n) for k in low]
-                for at, n in chunks
-            ]
-
-        taken = take(far, rows, [4 * n for _, n in chunks], 4 * len(chunks))
-        return [from_partner(part, "gx", bits_x - 1) for part in taken]
-
-    def level0(chunk, given, arr, send, weight=0):
+        def pick():
+            return 1 - own_bit(0), target(3, given)
+
+        taken = take(far.reshape(2, 4, 2, base, CH), pick, chunks)
+        return [from_partner(part.reshape(-1, CH), "gx", bits_x - 1) for part in taken]
+
+    def level0(chunk, given, arr, send):
         at, n = chunk
 
         def segments():
@@ -451,9 +443,9 @@
                 )
             return parts
 
-        return level_call(0, segments, env[3], arr, env[0], env[1], 4 * n, weight)
-
-    def level1(chunk, given, own, arr, send, weight=0):
+        return level_call(0, segments, env[3], arr, env[0], env[1], 4 * n)
+
+    def level1(chunk, given, own, arr, send):
         at, n = chunk
 
         def segments():
@@ -461,16 +453,16 @@
             row = aligned(t2 * 2 * n)
             return [(row, row, aligned(boxes + (t2 * 2 + t3) * 4 * base + 4 * at), 0, 2 * n)]
 
-        return level_call(1, segments, own, arr, env[0], env[2], 4 * n, weight)
-
-    def level2(chunk, given, own, arr, weight=0):
+        return level_call(1, segments, own, arr, env[0], env[2], 4 * n)
+
+    def level2(chunk, given, own, arr):
         at, n = chunk
 
         def segments():
             t3 = target(3, given)
             return [(0, 0, aligned(2 * boxes + t3 * 8 * base + 8 * at), 0, 4 * n)]
 
-        return level_call(2, segments, own, arr, env[0], env[1], 8 * n, weight)
+        return level_call(2, segments, own, arr, env[0], env[1], 8 * n)
 
     def swap1(part):
         return from_partner(part, "gy", bits_y - 1)
@@ -484,21 +476,21 @@
     cut = base // 2
     a, b, k = (0, cut), (cut, base - cut), (0, base)
     arr_a, arr_b = first([a, b], True)
-    send_a = level0(a, True, arr_a, True, AHEAD)
+    send_a = level0(a, True, arr_a, True)
     arr1_a = swap1(send_a)
-    keep_a = level0(a, True, after(arr_a, send_a), False, AHEAD)
+    keep_a = level0(a, True, after(arr_a, send_a), False)
     send_b = level0(b, True, after(arr_b, keep_a), True)
     arr1_b = swap1(send_b)
-    send_a = level1(a, True, keep_a, after(arr1_a, send_b), True, AHEAD)
+    send_a = level1(a, True, keep_a, after(arr1_a, send_b), True)
     arr2_a = swap2(send_a)
     keep_b = level0(b, True, after(arr_b, send_a), False)
     send_b = level1(b, True, keep_b, arr1_b, True)
     arr2_b = swap2(send_b)
-    keep_b = level1(b, True, keep_b, arr1_b, False)
     keep_a = level1(a, True, keep_a, arr1_a, False)
     given_a = level2(a, True, keep_a, after(arr2_a, send_b))
     z_a = swap3(given_a)
 
+    keep_b = level1(b, True, keep_b, after(arr1_b, given_a), False)
     given_b = level2(b, True, keep_b, arr2_b)
     z_b = swap3(given_b)
 

time: 88.2 us -> 87.8 us (level)
  transfers between devices with their start and end apart: 11 -> 11, of which waited for: 7 -> 7; matrix products, arithmetic and copies ran while one was open for 0% -> 0% of each run, Pallas kernels for 15% -> 14%
where the time goes in v6:
time: 87.8 us; the launch traced here: 87.4 us
  starting transfers between devices  52.1 us (59%)
  waiting for transfers between devices  20 us (23%)
  Pallas kernels  15 us (17%)
    ppermute x11, starting transfers between devices, from_partner(): return lax.ppermute(block, axis, route)  52.1 us
    ppermute x11, waiting for transfers between devices, from_partner(): return lax.ppermute(block, axis, route)  20 us
    pallas_call x15, Pallas kernels, level_call(): pl.pallas_call(kernel, out_shape=jax.ShapeDtypeStruct((rows, CH), jnp.flo...  8.08 us
    pallas_call x1, Pallas kernels, direct_call(): pl.pallas_call(functools.partial(direct_kernel, row), out_shape=jax.Shape...  1.81 us
  transfers between devices with their start and end apart: 11, of which 7 were waited for; matrix products, arithmetic and copies ran while one was open for 0% of the time, Pallas kernels for 14%

profile of v6, /device:TPU:32, one launch (start us, length us, event | category | flops | bytes accessed | tf_op | source)
XLA Modules:
  0.0 87.4 jit_solution(15840098121293102449)
XLA Ops:
  0.0 1.1 %shard_map.46 = (f32[4,64,128]{2,1,0:T(8,128)S(1)}, f32[4,64,128]{2,1,0:T(8,128)S(1)}) custom-call(f32[2,4,2,128,128]{4,3,2,1,0:T(8,128)} %bitcast.14), custom_call_target="tpu_custom_call" | custom-call | flops 20000000000 | bytes 4194304 | tf_op jit(solution)/shard_map/pallas_call | solution.py:155
  1.2 5.2 %collective-permute-start.4 = (f32[256,128]{1,0:T(8,128)S(1)}, f32[256,128]{1,0:T(8,128)S(1)}, u32[]{:S(2)}, u32[]{:S(2)}) collective-permute-start(f32[256,128]{1,0:T(8,128)S(1)} %bitcast.10), channel_id=1, source_target_pairs={{0,256},{32,288},{64,320},{96,352},{128,384},{160,416},{192,448},{... | collective-permute-start | bytes 393224 | tf_op jit(solution)/shard_map/ppermute | solution.py:397
  6.4 2.2 %collective-permute-start.3 = (f32[256,128]{1,0:T(8,128)S(1)}, f32[256,128]{1,0:T(8,128)S(1)}, u32[]{:S(2)}, u32[]{:S(2)}) collective-permute-start(f32[256,128]{1,0:T(8,128)S(1)} %bitcast.9), channel_id=1, source_target_pairs={{0,256},{32,288},{64,320},{96,352},{128,384},{160,416},{192,448},{... | collective-permute-start | bytes 393224 | tf_op jit(solution)/shard_map/ppermute | solution.py:397
  9.0 1.0 %collective-permute-done.4.arr = f32[256,128]{1,0:T(8,128)S(1)} collective-permute-done((f32[256,128]{1,0:T(8,128)S(1)}, f32[256,128]{1,0:T(8,128)S(1)}, u32[]{:S(2)}, u32[]{:S(2)}) %collective-permute-start.4) | collective-permute-done | bytes 131104 | tf_op jit(solution)/shard_map/ppermute | solution.py:397
  10.4 3.4 %collective-permute-start.5 = (f32[256,128]{1,0:T(8,128)S(1)}, f32[256,128]{1,0:T(8,128)S(1)}, u32[]{:S(2)}, u32[]{:S(2)}) collective-permute-start(f32[256,128]{1,0:T(8,128)S(1)} %shard_map.48), channel_id=1, source_target_pairs={{0,16},{1,17},{2,18},{3,19},{4,20},{5,21},{6,22},{7,23},{8,24},{9,... | collective-permute-start | bytes 393224 | tf_op jit(solution)/shard_map/ppermute | solution.py:397
  15.2 2.6 %collective-permute-start.6 = (f32[256,128]{1,0:T(8,128)S(1)}, f32[256,128]{1,0:T(8,128)S(1)}, u32[]{:S(2)}, u32[]{:S(2)}) collective-permute-start(f32[256,128]{1,0:T(8,128)S(1)} %shard_map.50), channel_id=1, source_target_pairs={{0,16},{1,17},{2,18},{3,19},{4,20},{5,21},{6,22},{7,23},{8,24},{9,... | collective-permute-start | bytes 393224 | tf_op jit(solution)/shard_map/ppermute | solution.py:397
  18.2 4.9 %collective-permute-start.7 = (f32[256,128]{1,0:T(8,128)S(1)}, f32[256,128]{1,0:T(8,128)S(1)}, u32[]{:S(2)}, u32[]{:S(2)}) collective-permute-start(f32[256,128]{1,0:T(8,128)S(1)} %shard_map.51), channel_id=1, source_target_pairs={{0,128},{32,160},{64,192},{96,224},{128,0},{160,32},{192,64},{224,... | collective-permute-start | bytes 393224 | tf_op jit(solution)/shard_map/ppermute | solution.py:397
  23.9 3.5 %collective-permute-start.8 = (f32[256,128]{1,0:T(8,128)S(1)}, f32[256,128]{1,0:T(8,128)S(1)}, u32[]{:S(2)}, u32[]{:S(2)}) collective-permute-start(f32[256,128]{1,0:T(8,128)S(1)} %shard_map.54), channel_id=1, source_target_pairs={{0,128},{32,160},{64,192},{96,224},{128,0},{160,32},{192,64},{224,... | collective-permute-start | bytes 393224 | tf_op jit(solution)/shard_map/ppermute | solution.py:397
  28.4 14.8 %collective-permute-start.10 = (f32[512,128]{1,0:T(8,128)S(1)}, f32[512,128]{1,0:T(8,128)S(1)}, u32[]{:S(2)}, u32[]{:S(2)}) collective-permute-start(f32[512,128]{1,0:T(8,128)S(1)} %shard_map.55), channel_id=1, source_target_pairs={{0,8},{1,9},{2,10},{3,11},{4,12},{5,13},{6,14},{7,15},{8,0},{9,1},... | collective-permute-start | bytes 786440 | tf_op jit(solution)/shard_map/ppermute | solution.py:397
  44.2 3.5 %collective-permute-start.9 = (f32[512,128]{1,0:T(8,128)S(1)}, f32[512,128]{1,0:T(8,128)S(1)}, u32[]{:S(2)}, u32[]{:S(2)}) collective-permute-start(f32[512,128]{1,0:T(8,128)S(1)} %shard_map.57), channel_id=1, source_target_pairs={{0,8},{1,9},{2,10},{3,11},{4,12},{5,13},{6,14},{7,15},{8,0},{9,1},... | collective-permute-start | bytes 786440 | tf_op jit(solution)/shard_map/ppermute | solution.py:397
  47.7 31.0 %conditional.1 = (f32[1024,128]{1,0:T(8,128)S(1)}) conditional(s32[]{:T(128)} %convert_element_type.3, () %tuple.27, (f32[1,1,2048,128]{3,2,1,0:T(8,128)S(1)}, f32[512,128]{1,0:T(8,128)S(1)}, f32[2048,128]{1,0:T(8,128)S(1)}, bf16[8192,128]{1,0:T(8,128)(2,1)}) %tuple.37), branch_computations={%region_0.0_spmd, %region_1.0_spmd} | conditional | flops 20000000000 | bytes 41943196 | solution.py:511
  47.8 6.1 %collective-permute-start = (f32[512,128]{1,0:T(8,128)S(1)}, f32[512,128]{1,0:T(8,128)S(1)}, u32[]{:S(2)}, u32[]{:S(2)}) collective-permute-start(f32[512,128]{1,0:T(8,128)S(1)} %bitcast.8), channel_id=1, source_target_pairs={{0,256},{32,288},{64,320},{96,352},{128,384},{160,416},{192,448},{... | collective-permute-start | bytes 786440 | tf_op jit(solution)/shard_map/cond/branch_1_fun/ppermute | solution.py:397
  54.0 4.2 %collective-permute-done.arr = f32[512,128]{1,0:T(8,128)S(1)} collective-permute-done((f32[512,128]{1,0:T(8,128)S(1)}, f32[512,128]{1,0:T(8,128)S(1)}, u32[]{:S(2)}, u32[]{:S(2)}) %collective-permute-start) | collective-permute-done | bytes 262176 | tf_op jit(solution)/shard_map/cond/branch_1_fun/ppermute | solution.py:397
  58.8 2.7 %collective-permute-start.1 = (f32[512,128]{1,0:T(8,128)S(1)}, f32[512,128]{1,0:T(8,128)S(1)}, u32[]{:S(2)}, u32[]{:S(2)}) collective-permute-start(f32[512,128]{1,0:T(8,128)S(1)} %branch_1_fun.10), channel_id=1, source_target_pairs={{0,16},{1,17},{2,18},{3,19},{4,20},{5,21},{6,22},{7,23},{8,24},{9,... | collective-permute-start | bytes 786440 | tf_op jit(solution)/shard_map/cond/branch_1_fun/ppermute | solution.py:397
  62.1 4.9 %collective-permute-done.1.arr = f32[512,128]{1,0:T(8,128)S(1)} collective-permute-done((f32[512,128]{1,0:T(8,128)S(1)}, f32[512,128]{1,0:T(8,128)S(1)}, u32[]{:S(2)}, u32[]{:S(2)}) %collective-permute-start.1) | collective-permute-done | bytes 262176 | tf_op jit(solution)/shard_map/cond/branch_1_fun/ppermute | solution.py:397
  67.7 3.2 %collective-permute-start.2 = (f32[512,128]{1,0:T(8,128)S(1)}, f32[512,128]{1,0:T(8,128)S(1)}, u32[]{:S(2)}, u32[]{:S(2)}) collective-permute-start(f32[512,128]{1,0:T(8,128)S(1)} %branch_1_fun.12), channel_id=1, source_target_pairs={{0,128},{32,160},{64,192},{96,224},{128,0},{160,32},{192,64},{224,... | collective-permute-start | bytes 786440 | tf_op jit(solution)/shard_map/cond/branch_1_fun/ppermute | solution.py:397
  71.5 5.9 %collective-permute-done.2.arr = f32[512,128]{1,0:T(8,128)S(1)} collective-permute-done((f32[512,128]{1,0:T(8,128)S(1)}, f32[512,128]{1,0:T(8,128)S(1)}, u32[]{:S(2)}, u32[]{:S(2)}) %collective-permute-start.2) | collective-permute-done | bytes 262176 | tf_op jit(solution)/shard_map/cond/branch_1_fun/ppermute | solution.py:397
  77.4 1.2 %branch_1_fun.13 = f32[1024,128]{1,0:T(8,128)S(1)} custom-call(f32[512,128]{1,0:T(8,128)S(1)} %branch_1_fun.11.own, f32[512,128]{1,0:T(8,128)S(1)} %collective-permute-done.2.arr, bf16[8192,128]{1,0:T(8,128)(2,1)S(1)} %copy-done.1, bf16[256,512]{1,0:T(8,128)(2,1)S(1)} %get-tuple-element.20.high, bf16[256,512]{1,0:T(8,128)(2,1)S(1)} %get-tuple-element.21.low), custom_call_target="tpu_custom_call" | custom-call | bytes 8388608 | tf_op jit(solution)/shard_map/cond/branch_1_fun/pallas_call | solution.py:231
  78.7 1.1 %shard_map.58.ang = bf16[2048,128]{1,0:T(8,128)(2,1)S(1)} custom-call(bf16[8192,128]{1,0:T(8,128)(2,1)} %bitcast.12), custom_call_target="tpu_custom_call" | custom-call | bytes 1048576 | tf_op jit(solution)/shard_map/pallas_call | solution.py:251
  79.7 1.2 %shard_map.59 = (f32[1024,128]{1,0:T(8,128)S(1)}, f32[1024,128]{1,0:T(8,128)S(1)}, f32[1024,128]{1,0:T(8,128)S(1)}) custom-call(f32[1024,128]{1,0:T(8,128)S(1)} %get-tuple-element.66.own, bf16[2048,128]{1,0:T(8,128)(2,1)S(1)} %shard_map.58.ang, bf16[128,256]{1,0:T(8,128)(2,1)S(1)} %get-tuple-element.60.high, bf16[128,256]{1,0:T(8,128)(2,1)S(1)} %get-tuple-element.61.low), custom_call_target="tpu_custom_call" | custom-call | bytes 4194304 | tf_op jit(solution)/shard_map/pallas_call | solution.py:338
  80.9 0.7 collective-permute-done.10.arr
  81.6 1.8 %shard_map.60.rest_0_ = f32[2048,128]{1,0:T(8,128)} custom-call(f32[1024,128]{1,0:T(8,128)S(1)} %get-tuple-element.66.own, f32[512,128]{1,0:T(8,128)S(1)} %collective-permute-done.10.arr, bf16[2048,128]{1,0:T(8,128)(2,1)S(1)} %shard_map.58.ang, bf16[256,512]{1,0:T(8,128)(2,1)S(1)} %get-tuple-element.53.high, bf16[256,512]{1,0:T(8,128)(2,1)S(1)} %get-tuple-element.54.low), custom_call_target="tpu_custom_call" | custom-call | bytes 4194304 | tf_op jit(solution)/shard_map/pallas_call | solution.py:285
  83.4 2.7 %collective-permute-done.9.arr = f32[512,128]{1,0:T(8,128)S(1)} collective-permute-done((f32[512,128]{1,0:T(8,128)S(1)}, f32[512,128]{1,0:T(8,128)S(1)}, u32[]{:S(2)}, u32[]{:S(2)}) %collective-permute-start.9) | collective-permute-done | bytes 262176 | tf_op jit(solution)/shard_map/ppermute | solution.py:397
  86.1 1.2 %shard_map.61 = f32[2048,128]{1,0:T(8,128)} custom-call(f32[512,128]{1,0:T(8,128)S(1)} %collective-permute-done.9.arr, f32[1024,128]{1,0:T(8,128)S(1)} %get-tuple-element.62.part, f32[1024,128]{1,0:T(8,128)S(1)} %get-tuple-element.63.cos_in, f32[1024,128]{1,0:T(8,128)S(1)} %get-tuple-element.64.sin_in, ...), custom_call_target="tpu_custom_call", output_to_operand_aliasing={{}: (6, {})} | custom-call | bytes 4194304 | tf_op jit(solution)/shard_map/pallas_call | solution.py:376
  (30 shorter events, 7.9 us)
Async XLA Ops:
  0.0 8.7 %copy-start = (bf16[4,1,1,2048,128]{4,3,2,1,0:T(8,128)(2,1)S(1)}, bf16[4,1,1,2048,128]{4,3,2,1,0:T(8,128)(2,1)}, u32[]{:S(2)}) copy-start(bf16[4,1,1,2048,128]{4,3,2,1,0:T(8,128)(2,1)} %param.7) | copy-start | bytes 6291460
  0.0 8.7 %copy-start.3 = (f32[512,128]{1,0:T(8,128)S(1)}, f32[512,128]{1,0:T(8,128)}, u32[]{:S(2)}) copy-start(f32[512,128]{1,0:T(8,128)} %constant.12.clone.blocks) | copy-start | bytes 786436
  1.1 8.9 %copy-start.2 = (f32[1,1,2048,128]{3,2,1,0:T(8,128)S(1)}, f32[1,1,2048,128]{3,2,1,0:T(8,128)}, u32[]{:S(2)}) copy-start(f32[1,1,2048,128]{3,2,1,0:T(8,128)} %param.6) | copy-start | bytes 3145732
  1.2 8.8 %collective-permute-start.4 = (f32[256,128]{1,0:T(8,128)S(1)}, f32[256,128]{1,0:T(8,128)S(1)}, u32[]{:S(2)}, u32[]{:S(2)}) collective-permute-start(f32[256,128]{1,0:T(8,128)S(1)} %bitcast.10), channel_id=1, source_target_pairs={{0,256},{32,288},{64,320},{96,352},{128,384},{160,416},{192,448},{... | collective-permute-start | bytes 393224 | tf_op jit(solution)/shard_map/ppermute | solution.py:397
  6.4 8.4 %collective-permute-start.3 = (f32[256,128]{1,0:T(8,128)S(1)}, f32[256,128]{1,0:T(8,128)S(1)}, u32[]{:S(2)}, u32[]{:S(2)}) collective-permute-start(f32[256,128]{1,0:T(8,128)S(1)} %bitcast.9), channel_id=1, source_target_pairs={{0,256},{32,288},{64,320},{96,352},{128,384},{160,416},{192,448},{... | collective-permute-start | bytes 393224 | tf_op jit(solution)/shard_map/ppermute | solution.py:397
  10.4 7.4 %collective-permute-start.5 = (f32[256,128]{1,0:T(8,128)S(1)}, f32[256,128]{1,0:T(8,128)S(1)}, u32[]{:S(2)}, u32[]{:S(2)}) collective-permute-start(f32[256,128]{1,0:T(8,128)S(1)} %shard_map.48), channel_id=1, source_target_pairs={{0,16},{1,17},{2,18},{3,19},{4,20},{5,21},{6,22},{7,23},{8,24},{9,... | collective-permute-start | bytes 393224 | tf_op jit(solution)/shard_map/ppermute | solution.py:397
  15.2 8.3 %collective-permute-start.6 = (f32[256,128]{1,0:T(8,128)S(1)}, f32[256,128]{1,0:T(8,128)S(1)}, u32[]{:S(2)}, u32[]{:S(2)}) collective-permute-start(f32[256,128]{1,0:T(8,128)S(1)} %shard_map.50), channel_id=1, source_target_pairs={{0,16},{1,17},{2,18},{3,19},{4,20},{5,21},{6,22},{7,23},{8,24},{9,... | collective-permute-start | bytes 393224 | tf_op jit(solution)/shard_map/ppermute | solution.py:397
  18.2 9.6 %collective-permute-start.7 = (f32[256,128]{1,0:T(8,128)S(1)}, f32[256,128]{1,0:T(8,128)S(1)}, u32[]{:S(2)}, u32[]{:S(2)}) collective-permute-start(f32[256,128]{1,0:T(8,128)S(1)} %shard_map.51), channel_id=1, source_target_pairs={{0,128},{32,160},{64,192},{96,224},{128,0},{160,32},{192,64},{224,... | collective-permute-start | bytes 393224 | tf_op jit(solution)/shard_map/ppermute | solution.py:397
  23.9 19.7 %collective-permute-start.8 = (f32[256,128]{1,0:T(8,128)S(1)}, f32[256,128]{1,0:T(8,128)S(1)}, u32[]{:S(2)}, u32[]{:S(2)}) collective-permute-start(f32[256,128]{1,0:T(8,128)S(1)} %shard_map.54), channel_id=1, source_target_pairs={{0,128},{32,160},{64,192},{96,224},{128,0},{160,32},{192,64},{224,... | collective-permute-start | bytes 393224 | tf_op jit(solution)/shard_map/ppermute | solution.py:397
  28.4 53.2 %collective-permute-start.10 = (f32[512,128]{1,0:T(8,128)S(1)}, f32[512,128]{1,0:T(8,128)S(1)}, u32[]{:S(2)}, u32[]{:S(2)}) collective-permute-start(f32[512,128]{1,0:T(8,128)S(1)} %shard_map.55), channel_id=1, source_target_pairs={{0,8},{1,9},{2,10},{3,11},{4,12},{5,13},{6,14},{7,15},{8,0},{9,1},... | collective-permute-start | bytes 786440 | tf_op jit(solution)/shard_map/ppermute | solution.py:397
  44.2 41.9 %collective-permute-start.9 = (f32[512,128]{1,0:T(8,128)S(1)}, f32[512,128]{1,0:T(8,128)S(1)}, u32[]{:S(2)}, u32[]{:S(2)}) collective-permute-start(f32[512,128]{1,0:T(8,128)S(1)} %shard_map.57), channel_id=1, source_target_pairs={{0,8},{1,9},{2,10},{3,11},{4,12},{5,13},{6,14},{7,15},{8,0},{9,1},... | collective-permute-start | bytes 786440 | tf_op jit(solution)/shard_map/ppermute | solution.py:397
  47.7 10.5 %copy-start.1 = (bf16[8192,128]{1,0:T(8,128)(2,1)S(1)}, bf16[8192,128]{1,0:T(8,128)(2,1)}, u32[]{:S(2)}) copy-start(bf16[8192,128]{1,0:T(8,128)(2,1)} %get-tuple-element.18.ang) | copy-start | bytes 6291460 | tf_op jit(solution)/shard_map/cond
  47.8 10.4 %collective-permute-start = (f32[512,128]{1,0:T(8,128)S(1)}, f32[512,128]{1,0:T(8,128)S(1)}, u32[]{:S(2)}, u32[]{:S(2)}) collective-permute-start(f32[512,128]{1,0:T(8,128)S(1)} %bitcast.8), channel_id=1, source_target_pairs={{0,256},{32,288},{64,320},{96,352},{128,384},{160,416},{192,448},{... | collective-permute-start | bytes 786440 | tf_op jit(solution)/shard_map/cond/branch_1_fun/ppermute | solution.py:397
  58.8 8.3 %collective-permute-start.1 = (f32[512,128]{1,0:T(8,128)S(1)}, f32[512,128]{1,0:T(8,128)S(1)}, u32[]{:S(2)}, u32[]{:S(2)}) collective-permute-start(f32[512,128]{1,0:T(8,128)S(1)} %branch_1_fun.10), channel_id=1, source_target_pairs={{0,16},{1,17},{2,18},{3,19},{4,20},{5,21},{6,22},{7,23},{8,24},{9,... | collective-permute-start | bytes 786440 | tf_op jit(solution)/shard_map/cond/branch_1_fun/ppermute | solution.py:397
  67.7 9.8 %collective-permute-start.2 = (f32[512,128]{1,0:T(8,128)S(1)}, f32[512,128]{1,0:T(8,128)S(1)}, u32[]{:S(2)}, u32[]{:S(2)}) collective-permute-start(f32[512,128]{1,0:T(8,128)S(1)} %branch_1_fun.12), channel_id=1, source_target_pairs={{0,128},{32,160},{64,192},{96,224},{128,0},{160,32},{192,64},{224,... | collective-permute-start | bytes 786440 | tf_op jit(solution)/shard_map/cond/branch_1_fun/ppermute | solution.py:397

commit v7 on v6

--- a/solution.py
+++ b/solution.py
@@ -25,6 +25,7 @@
     return [float(v) for v in sine.coef], [float(v) for v in cosine.coef]
 
 
+AHEAD, LAST = 5_000_000_000, 1_500_000_000
 SINE, COSINE = half_angle_polys()
 
 
@@ -223,7 +224,7 @@
         pl.loop(0, n // tile)(step)
 
 
-def level_call(level, segments, own, arr, ang, table, rows):
+def level_call(level, segments, own, arr, ang, table, rows, weight=0):
     steps = -(-rows // 512)
     tile = rows // 2 // steps
     kernel = functools.partial(level_kernel, level, segments, tile)
@@ -236,7 +237,7 @@
         scratch_shapes=scratch,
         compiler_params=limits(),
         cost_estimate=pl.CostEstimate(
-            flops=0, bytes_accessed=rows * 8 * 1024, transcendentals=0
+            flops=weight, bytes_accessed=rows * 8 * 1024, transcendentals=0
         ),
     )(own, arr, ang, *table)
 
@@ -294,9 +295,13 @@
         ],
         compiler_params=limits(),
         cost_estimate=pl.CostEstimate(
-            flops=0, bytes_accessed=rows * 8 * 1024, transcendentals=0
+            flops=LAST, bytes_accessed=rows * 8 * 1024, transcendentals=0
         ),
     )(own, arr, ang, *table)
+
+
+def tile_of(rows):
+    return next(n for n in (128, 144, 112, 96) if rows % n == 0)
 
 
 def spread_last(x, high, low, scratch):
@@ -315,9 +320,9 @@
 
     def step(i):
         rows = pl.ds(pl.multiple_of(2 * i * tile, 2 * tile), 2 * tile)
-        near = pl.ds(pl.multiple_of(row + i * tile, tile), tile)
+        near = pl.ds(pl.multiple_of(row + i * tile, 16), tile)
         y = spread_last(own[near, :], high, low, scratch)
-        at = pl.ds(pl.multiple_of(2 * (row + i * tile), 2 * tile), 2 * tile)
+        at = pl.ds(pl.multiple_of(2 * (row + i * tile), 32), 2 * tile)
         c, s = cos_sin(ang[at, :].astype(jnp.float32))
         left = lax.broadcasted_iota(jnp.int32, c.shape, 1) < SQUARE
         c_far, s_far = pltpu.roll(c, SQUARE, 1), pltpu.roll(s, SQUARE, 1)
@@ -333,7 +338,7 @@
 
 
 def before_call(own, ang, table, row):
-    tile = 128
+    tile = tile_of(own.shape[0] - row)
     part = jax.ShapeDtypeStruct((2 * (own.shape[0] - row), CH), jnp.float32)
     return pl.pallas_call(
         functools.partial(before_kernel, row, tile),
@@ -370,7 +375,7 @@
 
 def last_call(arr, ready, table, row, earlier):
     rows = arr.shape[0]
-    tile = 128
+    tile = tile_of(rows)
     count = rows // tile
     operands = [arr, *ready, *table, earlier]
     return pl.pallas_call(
@@ -407,12 +412,10 @@
     boxes = weights.shape[2]
     base = boxes // 16
     far = weights.reshape(boxes, CH)
-    ang, *ready = load(angles.reshape(4 * boxes, CH))
     w2 = far
-    tab_x, tab_y, tab_last = ready[:2], ready[2:4], ready[4:]
-    env = [ang, tab_x, tab_y, w2]
+    env = [None] * 4
     ang_far = angles.reshape(4 * boxes, CH)
-    aligned = lambda row: pl.multiple_of(row, 16)
+    aligned = lambda row, by=16: pl.multiple_of(row, by)
 
     def target(k, other):
         return 1 - own_bit(k) if other else own_bit(k)
@@ -421,10 +424,14 @@
         def pick():
             return 1 - own_bit(0), target(3, given)
 
-        taken = take(far.reshape(2, 4, 2, base, CH), pick, chunks)
-        return [from_partner(part.reshape(-1, CH), "gx", bits_x - 1) for part in taken]
-
-    def level0(chunk, given, arr, send):
+        return [
+            part.reshape(-1, CH) for part in take(far.reshape(2, 4, 2, base, CH), pick, chunks)
+        ]
+
+    def swap0(part):
+        return from_partner(part, "gx", bits_x - 1)
+
+    def level0(chunk, given, arr, send, weight=0):
         at, n = chunk
 
         def segments():
@@ -434,8 +441,8 @@
                 low = (t1 * 2 + t2) * 2 + t3
                 parts.append(
                     (
-                        aligned((own_bit(0) * 8 + low) * base + at),
-                        aligned((t1 * 2 + t2) * n),
+                        aligned((own_bit(0) * 8 + low) * base + at, 8),
+                        aligned((t1 * 2 + t2) * n, 8),
                         aligned(low * 2 * base + 2 * at),
                         t2 * 2 * n,
                         n,
@@ -443,9 +450,9 @@
                 )
             return parts
 
-        return level_call(0, segments, env[3], arr, env[0], env[1], 4 * n)
-
-    def level1(chunk, given, own, arr, send):
+        return level_call(0, segments, env[3], arr, env[0], env[1], 4 * n, weight)
+
+    def level1(chunk, given, own, arr, send, weight=0):
         at, n = chunk
 
         def segments():
@@ -453,7 +460,7 @@
             row = aligned(t2 * 2 * n)
             return [(row, row, aligned(boxes + (t2 * 2 + t3) * 4 * base + 4 * at), 0, 2 * n)]
 
-        return level_call(1, segments, own, arr, env[0], env[2], 4 * n)
+        return level_call(1, segments, own, arr, env[0], env[2], 4 * n, weight)
 
     def level2(chunk, given, own, arr):
         at, n = chunk
@@ -473,15 +480,19 @@
     def swap3(part):
         return from_partner(part, "gy", bits_y - 2)
 
-    cut = base // 2
+    cut = 7 * base // 16
     a, b, k = (0, cut), (cut, base - cut), (0, base)
-    arr_a, arr_b = first([a, b], True)
-    send_a = level0(a, True, arr_a, True)
+    send_a, send_b = first([a, b], True)
+    arr_a, arr_b = swap0(send_a), swap0(send_b)
+    ang, *ready = load(after(ang_far, send_a))
+    tab_x, tab_y, tab_last = ready[:2], ready[2:4], ready[4:]
+    env[:] = [ang, tab_x, tab_y, after(w2, send_b)]
+    send_a = level0(a, True, arr_a, True, AHEAD)
     arr1_a = swap1(send_a)
-    keep_a = level0(a, True, after(arr_a, send_a), False)
+    keep_a = level0(a, True, after(arr_a, send_a), False, AHEAD)
     send_b = level0(b, True, after(arr_b, keep_a), True)
     arr1_b = swap1(send_b)
-    send_a = level1(a, True, keep_a, after(arr1_a, send_b), True)
+    send_a = level1(a, True, keep_a, after(arr1_a, send_b), True, AHEAD)
     arr2_a = swap2(send_a)
     keep_b = level0(b, True, after(arr_b, send_a), False)
     send_b = level1(b, True, keep_b, arr1_b, True)
@@ -501,7 +512,7 @@
         far = w2
         ready = make_tables(blocks)
         env[:] = [ang, ready[:2], ready[2:], w2]
-        (arr_k,) = first([k], False)
+        arr_k = swap0(first([k], False)[0])
         arr1_k = swap1(level0(k, False, arr_k, True))
         keep_k = level0(k, False, arr_k, False)
         arr2_k = swap2(level1(k, False, keep_k, arr1_k, True))

time: 87.8 us -> 87.7 us (level)
  transfers between devices with their start and end apart: 11 -> 11, of which waited for: 7 -> 6; matrix products, arithmetic and copies ran while one was open for 0% -> 0% of each run, Pallas kernels for 14% -> 15%
where the time goes in v7:
time: 87.7 us; the launch traced here: 87.3 us
  starting transfers between devices  51.5 us (59%)
  waiting for transfers between devices  20.3 us (23%)
  Pallas kernels  15.2 us (17%)
    ppermute x11, starting transfers between devices, from_partner(): return lax.ppermute(block, axis, route)  51.5 us
    ppermute x11, waiting for transfers between devices, from_partner(): return lax.ppermute(block, axis, route)  20.3 us
    pallas_call x15, Pallas kernels, level_call(): pl.pallas_call(kernel, out_shape=jax.ShapeDtypeStruct((rows, CH), jnp.flo...  8.33 us
  transfers between devices with their start and end apart: 11, of which 6 were waited for; matrix products, arithmetic and copies ran while one was open for 0% of the time, Pallas kernels for 15%

profile of v7, /device:TPU:32, one launch (start us, length us, event | category | flops | bytes accessed | tf_op | source)
XLA Modules:
  0.0 87.3 jit_solution(1064709421175992047)
XLA Ops:
  0.0 1.1 %shard_map.46 = (f32[4,56,128]{2,1,0:T(8,128)S(1)}, f32[4,72,128]{2,1,0:T(8,128)S(1)}) custom-call(f32[2,4,2,128,128]{4,3,2,1,0:T(8,128)} %bitcast.14), custom_call_target="tpu_custom_call" | custom-call | flops 20000000000 | bytes 4194304 | tf_op jit(solution)/shard_map/pallas_call | solution.py:156
  1.2 5.2 %collective-permute-start.4 = (f32[224,128]{1,0:T(8,128)S(1)}, f32[224,128]{1,0:T(8,128)S(1)}, u32[]{:S(2)}, u32[]{:S(2)}) collective-permute-start(f32[224,128]{1,0:T(8,128)S(1)} %bitcast.10), channel_id=1, source_target_pairs={{0,256},{32,288},{64,320},{96,352},{128,384},{160,416},{192,448},{... | collective-permute-start | bytes 344072 | tf_op jit(solution)/shard_map/ppermute | solution.py:402
  6.4 2.2 %collective-permute-start.3 = (f32[288,128]{1,0:T(8,128)S(1)}, f32[288,128]{1,0:T(8,128)S(1)}, u32[]{:S(2)}, u32[]{:S(2)}) collective-permute-start(f32[288,128]{1,0:T(8,128)S(1)} %bitcast.9), channel_id=1, source_target_pairs={{0,256},{32,288},{64,320},{96,352},{128,384},{160,416},{192,448},{... | collective-permute-start | bytes 442376 | tf_op jit(solution)/shard_map/ppermute | solution.py:402
  10.0 3.5 %collective-permute-start.5 = (f32[224,128]{1,0:T(8,128)S(1)}, f32[224,128]{1,0:T(8,128)S(1)}, u32[]{:S(2)}, u32[]{:S(2)}) collective-permute-start(f32[224,128]{1,0:T(8,128)S(1)} %shard_map.48), channel_id=1, source_target_pairs={{0,16},{1,17},{2,18},{3,19},{4,20},{5,21},{6,22},{7,23},{8,24},{9,... | collective-permute-start | bytes 344072 | tf_op jit(solution)/shard_map/ppermute | solution.py:402
  13.8 1.3 %collective-permute-done.3.arr = f32[288,128]{1,0:T(8,128)S(1)} collective-permute-done((f32[288,128]{1,0:T(8,128)S(1)}, f32[288,128]{1,0:T(8,128)S(1)}, u32[]{:S(2)}, u32[]{:S(2)}) %collective-permute-start.3) | collective-permute-done | bytes 147488 | tf_op jit(solution)/shard_map/ppermute | solution.py:402
  15.5 2.6 %collective-permute-start.6 = (f32[288,128]{1,0:T(8,128)S(1)}, f32[288,128]{1,0:T(8,128)S(1)}, u32[]{:S(2)}, u32[]{:S(2)}) collective-permute-start(f32[288,128]{1,0:T(8,128)S(1)} %shard_map.50), channel_id=1, source_target_pairs={{0,16},{1,17},{2,18},{3,19},{4,20},{5,21},{6,22},{7,23},{8,24},{9,... | collective-permute-start | bytes 442376 | tf_op jit(solution)/shard_map/ppermute | solution.py:402
  18.5 4.9 %collective-permute-start.7 = (f32[224,128]{1,0:T(8,128)S(1)}, f32[224,128]{1,0:T(8,128)S(1)}, u32[]{:S(2)}, u32[]{:S(2)}) collective-permute-start(f32[224,128]{1,0:T(8,128)S(1)} %shard_map.51), channel_id=1, source_target_pairs={{0,128},{32,160},{64,192},{96,224},{128,0},{160,32},{192,64},{224,... | collective-permute-start | bytes 344072 | tf_op jit(solution)/shard_map/ppermute | solution.py:402
  24.3 3.6 %collective-permute-start.8 = (f32[288,128]{1,0:T(8,128)S(1)}, f32[288,128]{1,0:T(8,128)S(1)}, u32[]{:S(2)}, u32[]{:S(2)}) collective-permute-start(f32[288,128]{1,0:T(8,128)S(1)} %shard_map.54), channel_id=1, source_target_pairs={{0,128},{32,160},{64,192},{96,224},{128,0},{160,32},{192,64},{224,... | collective-permute-start | bytes 442376 | tf_op jit(solution)/shard_map/ppermute | solution.py:402
  28.9 14.8 %collective-permute-start.10 = (f32[448,128]{1,0:T(8,128)S(1)}, f32[448,128]{1,0:T(8,128)S(1)}, u32[]{:S(2)}, u32[]{:S(2)}) collective-permute-start(f32[448,128]{1,0:T(8,128)S(1)} %shard_map.55), channel_id=1, source_target_pairs={{0,8},{1,9},{2,10},{3,11},{4,12},{5,13},{6,14},{7,15},{8,0},{9,1},... | collective-permute-start | bytes 688136 | tf_op jit(solution)/shard_map/ppermute | solution.py:402
  44.1 0.9 shard_map.57
  45.0 3.5 %collective-permute-start.9 = (f32[576,128]{1,0:T(8,128)S(1)}, f32[576,128]{1,0:T(8,128)S(1)}, u32[]{:S(2)}, u32[]{:S(2)}) collective-permute-start(f32[576,128]{1,0:T(8,128)S(1)} %shard_map.57), channel_id=1, source_target_pairs={{0,8},{1,9},{2,10},{3,11},{4,12},{5,13},{6,14},{7,15},{8,0},{9,1},... | collective-permute-start | bytes 884744 | tf_op jit(solution)/shard_map/ppermute | solution.py:402
  48.5 30.4 %conditional.1 = (f32[1024,128]{1,0:T(8,128)S(1)}) conditional(s32[]{:T(128)} %convert_element_type.3, () %tuple.31, (f32[1,1,2048,128]{3,2,1,0:T(8,128)S(1)}, f32[512,128]{1,0:T(8,128)S(1)}, f32[2048,128]{1,0:T(8,128)S(1)}, bf16[8192,128]{1,0:T(8,128)(2,1)}) %tuple.41), branch_computations={%region_0.0_spmd, %region_1.0_spmd} | conditional | flops 20000000000 | bytes 41943196 | solution.py:522
  48.6 4.3 %collective-permute-start = (f32[512,128]{1,0:T(8,128)S(1)}, f32[512,128]{1,0:T(8,128)S(1)}, u32[]{:S(2)}, u32[]{:S(2)}) collective-permute-start(f32[512,128]{1,0:T(8,128)S(1)} %bitcast.8), channel_id=1, source_target_pairs={{0,256},{32,288},{64,320},{96,352},{128,384},{160,416},{192,448},{... | collective-permute-start | bytes 786440 | tf_op jit(solution)/shard_map/cond/branch_1_fun/ppermute | solution.py:402
  53.0 5.5 %collective-permute-done.arr = f32[512,128]{1,0:T(8,128)S(1)} collective-permute-done((f32[512,128]{1,0:T(8,128)S(1)}, f32[512,128]{1,0:T(8,128)S(1)}, u32[]{:S(2)}, u32[]{:S(2)}) %collective-permute-start) | collective-permute-done | bytes 262176 | tf_op jit(solution)/shard_map/cond/branch_1_fun/ppermute | solution.py:402
  59.1 3.3 %collective-permute-start.1 = (f32[512,128]{1,0:T(8,128)S(1)}, f32[512,128]{1,0:T(8,128)S(1)}, u32[]{:S(2)}, u32[]{:S(2)}) collective-permute-start(f32[512,128]{1,0:T(8,128)S(1)} %branch_1_fun.10), channel_id=1, source_target_pairs={{0,16},{1,17},{2,18},{3,19},{4,20},{5,21},{6,22},{7,23},{8,24},{9,... | collective-permute-start | bytes 786440 | tf_op jit(solution)/shard_map/cond/branch_1_fun/ppermute | solution.py:402
  63.0 4.4 %collective-permute-done.1.arr = f32[512,128]{1,0:T(8,128)S(1)} collective-permute-done((f32[512,128]{1,0:T(8,128)S(1)}, f32[512,128]{1,0:T(8,128)S(1)}, u32[]{:S(2)}, u32[]{:S(2)}) %collective-permute-start.1) | collective-permute-done | bytes 262176 | tf_op jit(solution)/shard_map/cond/branch_1_fun/ppermute | solution.py:402
  68.0 3.6 %collective-permute-start.2 = (f32[512,128]{1,0:T(8,128)S(1)}, f32[512,128]{1,0:T(8,128)S(1)}, u32[]{:S(2)}, u32[]{:S(2)}) collective-permute-start(f32[512,128]{1,0:T(8,128)S(1)} %branch_1_fun.12), channel_id=1, source_target_pairs={{0,128},{32,160},{64,192},{96,224},{128,0},{160,32},{192,64},{224,... | collective-permute-start | bytes 786440 | tf_op jit(solution)/shard_map/cond/branch_1_fun/ppermute | solution.py:402
  72.2 5.5 %collective-permute-done.2.arr = f32[512,128]{1,0:T(8,128)S(1)} collective-permute-done((f32[512,128]{1,0:T(8,128)S(1)}, f32[512,128]{1,0:T(8,128)S(1)}, u32[]{:S(2)}, u32[]{:S(2)}) %collective-permute-start.2) | collective-permute-done | bytes 262176 | tf_op jit(solution)/shard_map/cond/branch_1_fun/ppermute | solution.py:402
  77.7 1.2 %branch_1_fun.13 = f32[1024,128]{1,0:T(8,128)S(1)} custom-call(f32[512,128]{1,0:T(8,128)S(1)} %branch_1_fun.11.own, f32[512,128]{1,0:T(8,128)S(1)} %collective-permute-done.2.arr, bf16[8192,128]{1,0:T(8,128)(2,1)S(1)} %copy-done.1, bf16[256,512]{1,0:T(8,128)(2,1)S(1)} %get-tuple-element.20.high, bf16[256,512]{1,0:T(8,128)(2,1)S(1)} %get-tuple-element.21.low), custom_call_target="tpu_custom_call" | custom-call | bytes 8388608 | tf_op jit(solution)/shard_map/cond/branch_1_fun/pallas_call | solution.py:232
  79.0 1.1 %shard_map.58.ang = bf16[2048,128]{1,0:T(8,128)(2,1)S(1)} custom-call(bf16[8192,128]{1,0:T(8,128)(2,1)} %bitcast.12), custom_call_target="tpu_custom_call" | custom-call | bytes 1048576 | tf_op jit(solution)/shard_map/pallas_call | solution.py:252
  80.0 1.3 %shard_map.59 = (f32[1152,128]{1,0:T(8,128)S(1)}, f32[1152,128]{1,0:T(8,128)S(1)}, f32[1152,128]{1,0:T(8,128)S(1)}) custom-call(f32[1024,128]{1,0:T(8,128)S(1)} %get-tuple-element.70.own, bf16[2048,128]{1,0:T(8,128)(2,1)S(1)} %shard_map.58.ang, bf16[128,256]{1,0:T(8,128)(2,1)S(1)} %get-tuple-element.64.high, bf16[128,256]{1,0:T(8,128)(2,1)S(1)} %get-tuple-element.65.low), custom_call_target="tpu_custom_call" | custom-call | bytes 4194304 | tf_op jit(solution)/shard_map/pallas_call | solution.py:343
  81.3 1.7 %shard_map.60.rest_0_ = f32[2048,128]{1,0:T(8,128)} custom-call(f32[1024,128]{1,0:T(8,128)S(1)} %get-tuple-element.70.own, f32[448,128]{1,0:T(8,128)S(1)} %collective-permute-done.10.arr, bf16[2048,128]{1,0:T(8,128)(2,1)S(1)} %shard_map.58.ang, bf16[256,512]{1,0:T(8,128)(2,1)S(1)} %get-tuple-element.57.high, bf16[256,512]{1,0:T(8,128)(2,1)S(1)} %get-tuple-element.58.low), custom_call_target="tpu_custom_call" | custom-call | flops 1500000000 | bytes 3670016 | tf_op jit(solution)/shard_map/pallas_call | solution.py:286
  83.0 3.0 %collective-permute-done.9.arr = f32[576,128]{1,0:T(8,128)S(1)} collective-permute-done((f32[576,128]{1,0:T(8,128)S(1)}, f32[576,128]{1,0:T(8,128)S(1)}, u32[]{:S(2)}, u32[]{:S(2)}) %collective-permute-start.9) | collective-permute-done | bytes 294944 | tf_op jit(solution)/shard_map/ppermute | solution.py:402
  86.0 1.3 %shard_map.61 = f32[2048,128]{1,0:T(8,128)} custom-call(f32[576,128]{1,0:T(8,128)S(1)} %collective-permute-done.9.arr, f32[1152,128]{1,0:T(8,128)S(1)} %get-tuple-element.66.part, f32[1152,128]{1,0:T(8,128)S(1)} %get-tuple-element.67.cos_in, f32[1152,128]{1,0:T(8,128)S(1)} %get-tuple-element.68.sin_in, ...), custom_call_target="tpu_custom_call", output_to_operand_aliasing={{}: (6, {})} | custom-call | bytes 4718592 | tf_op jit(solution)/shard_map/pallas_call | solution.py:381
  (30 shorter events, 7.3 us)
Async XLA Ops:
  0.0 8.7 %copy-start = (bf16[4,1,1,2048,128]{4,3,2,1,0:T(8,128)(2,1)S(1)}, bf16[4,1,1,2048,128]{4,3,2,1,0:T(8,128)(2,1)}, u32[]{:S(2)}) copy-start(bf16[4,1,1,2048,128]{4,3,2,1,0:T(8,128)(2,1)} %param.7) | copy-start | bytes 6291460
  0.0 8.7 %copy-start.3 = (f32[512,128]{1,0:T(8,128)S(1)}, f32[512,128]{1,0:T(8,128)}, u32[]{:S(2)}) copy-start(f32[512,128]{1,0:T(8,128)} %constant.12.clone.blocks) | copy-start | bytes 786436
  1.1 8.4 %copy-start.2 = (f32[1,1,2048,128]{3,2,1,0:T(8,128)S(1)}, f32[1,1,2048,128]{3,2,1,0:T(8,128)}, u32[]{:S(2)}) copy-start(f32[1,1,2048,128]{3,2,1,0:T(8,128)} %param.6) | copy-start | bytes 3145732
  1.2 8.4 %collective-permute-start.4 = (f32[224,128]{1,0:T(8,128)S(1)}, f32[224,128]{1,0:T(8,128)S(1)}, u32[]{:S(2)}, u32[]{:S(2)}) collective-permute-start(f32[224,128]{1,0:T(8,128)S(1)} %bitcast.10), channel_id=1, source_target_pairs={{0,256},{32,288},{64,320},{96,352},{128,384},{160,416},{192,448},{... | collective-permute-start | bytes 344072 | tf_op jit(solution)/shard_map/ppermute | solution.py:402
  6.4 8.7 %collective-permute-start.3 = (f32[288,128]{1,0:T(8,128)S(1)}, f32[288,128]{1,0:T(8,128)S(1)}, u32[]{:S(2)}, u32[]{:S(2)}) collective-permute-start(f32[288,128]{1,0:T(8,128)S(1)} %bitcast.9), channel_id=1, source_target_pairs={{0,256},{32,288},{64,320},{96,352},{128,384},{160,416},{192,448},{... | collective-permute-start | bytes 442376 | tf_op jit(solution)/shard_map/ppermute | solution.py:402
  10.0 8.2 %collective-permute-start.5 = (f32[224,128]{1,0:T(8,128)S(1)}, f32[224,128]{1,0:T(8,128)S(1)}, u32[]{:S(2)}, u32[]{:S(2)}) collective-permute-start(f32[224,128]{1,0:T(8,128)S(1)} %shard_map.48), channel_id=1, source_target_pairs={{0,16},{1,17},{2,18},{3,19},{4,20},{5,21},{6,22},{7,23},{8,24},{9,... | collective-permute-start | bytes 344072 | tf_op jit(solution)/shard_map/ppermute | solution.py:402
  15.5 8.3 %collective-permute-start.6 = (f32[288,128]{1,0:T(8,128)S(1)}, f32[288,128]{1,0:T(8,128)S(1)}, u32[]{:S(2)}, u32[]{:S(2)}) collective-permute-start(f32[288,128]{1,0:T(8,128)S(1)} %shard_map.50), channel_id=1, source_target_pairs={{0,16},{1,17},{2,18},{3,19},{4,20},{5,21},{6,22},{7,23},{8,24},{9,... | collective-permute-start | bytes 442376 | tf_op jit(solution)/shard_map/ppermute | solution.py:402
  18.5 9.8 %collective-permute-start.7 = (f32[224,128]{1,0:T(8,128)S(1)}, f32[224,128]{1,0:T(8,128)S(1)}, u32[]{:S(2)}, u32[]{:S(2)}) collective-permute-start(f32[224,128]{1,0:T(8,128)S(1)} %shard_map.51), channel_id=1, source_target_pairs={{0,128},{32,160},{64,192},{96,224},{128,0},{160,32},{192,64},{224,... | collective-permute-start | bytes 344072 | tf_op jit(solution)/shard_map/ppermute | solution.py:402
  24.3 19.8 %collective-permute-start.8 = (f32[288,128]{1,0:T(8,128)S(1)}, f32[288,128]{1,0:T(8,128)S(1)}, u32[]{:S(2)}, u32[]{:S(2)}) collective-permute-start(f32[288,128]{1,0:T(8,128)S(1)} %shard_map.54), channel_id=1, source_target_pairs={{0,128},{32,160},{64,192},{96,224},{128,0},{160,32},{192,64},{224,... | collective-permute-start | bytes 442376 | tf_op jit(solution)/shard_map/ppermute | solution.py:402
  28.9 52.4 %collective-permute-start.10 = (f32[448,128]{1,0:T(8,128)S(1)}, f32[448,128]{1,0:T(8,128)S(1)}, u32[]{:S(2)}, u32[]{:S(2)}) collective-permute-start(f32[448,128]{1,0:T(8,128)S(1)} %shard_map.55), channel_id=1, source_target_pairs={{0,8},{1,9},{2,10},{3,11},{4,12},{5,13},{6,14},{7,15},{8,0},{9,1},... | collective-permute-start | bytes 688136 | tf_op jit(solution)/shard_map/ppermute | solution.py:402
  45.0 41.0 %collective-permute-start.9 = (f32[576,128]{1,0:T(8,128)S(1)}, f32[576,128]{1,0:T(8,128)S(1)}, u32[]{:S(2)}, u32[]{:S(2)}) collective-permute-start(f32[576,128]{1,0:T(8,128)S(1)} %shard_map.57), channel_id=1, source_target_pairs={{0,8},{1,9},{2,10},{3,11},{4,12},{5,13},{6,14},{7,15},{8,0},{9,1},... | collective-permute-start | bytes 884744 | tf_op jit(solution)/shard_map/ppermute | solution.py:402
  48.5 10.0 %copy-start.1 = (bf16[8192,128]{1,0:T(8,128)(2,1)S(1)}, bf16[8192,128]{1,0:T(8,128)(2,1)}, u32[]{:S(2)}) copy-start(bf16[8192,128]{1,0:T(8,128)(2,1)} %get-tuple-element.18.ang) | copy-start | bytes 6291460 | tf_op jit(solution)/shard_map/cond
  48.6 9.9 %collective-permute-start = (f32[512,128]{1,0:T(8,128)S(1)}, f32[512,128]{1,0:T(8,128)S(1)}, u32[]{:S(2)}, u32[]{:S(2)}) collective-permute-start(f32[512,128]{1,0:T(8,128)S(1)} %bitcast.8), channel_id=1, source_target_pairs={{0,256},{32,288},{64,320},{96,352},{128,384},{160,416},{192,448},{... | collective-permute-start | bytes 786440 | tf_op jit(solution)/shard_map/cond/branch_1_fun/ppermute | solution.py:402
  59.1 8.3 %collective-permute-start.1 = (f32[512,128]{1,0:T(8,128)S(1)}, f32[512,128]{1,0:T(8,128)S(1)}, u32[]{:S(2)}, u32[]{:S(2)}) collective-permute-start(f32[512,128]{1,0:T(8,128)S(1)} %branch_1_fun.10), channel_id=1, source_target_pairs={{0,16},{1,17},{2,18},{3,19},{4,20},{5,21},{6,22},{7,23},{8,24},{9,... | collective-permute-start | bytes 786440 | tf_op jit(solution)/shard_map/cond/branch_1_fun/ppermute | solution.py:402
  68.0 9.8 %collective-permute-start.2 = (f32[512,128]{1,0:T(8,128)S(1)}, f32[512,128]{1,0:T(8,128)S(1)}, u32[]{:S(2)}, u32[]{:S(2)}) collective-permute-start(f32[512,128]{1,0:T(8,128)S(1)} %branch_1_fun.12), channel_id=1, source_target_pairs={{0,128},{32,160},{64,192},{96,224},{128,0},{160,32},{192,64},{224,... | collective-permute-start | bytes 786440 | tf_op jit(solution)/shard_map/cond/branch_1_fun/ppermute | solution.py:402

commit v8 on v7

--- a/solution.py
+++ b/solution.py
@@ -360,7 +360,7 @@
     copies = []
     for i in range(count):
         at = pl.ds(i * rows, rows)
-        y = spread_last(arr[pl.ds(i * tile, tile), :], high, low, scratch)
+        y = spread_last(arr[pl.ds(i * tile, tile), :], high, low, scratch.at[i])
         near_out[i] = (
             part[at, :] + cos_in[at, :] * y + sin_in[at, :] * pltpu.roll(y, SQUARE, 1)
         )
@@ -384,7 +384,7 @@
         in_specs=[VMEM] * 6 + [HBM],
         out_specs=HBM,
         scratch_shapes=[
-            pltpu.VMEM((2 * tile, CH), jnp.float32),
+            pltpu.VMEM((count, 2 * tile, CH), jnp.float32),
             pltpu.VMEM((count, 2 * tile, CH), jnp.float32),
             pltpu.SemaphoreType.DMA((count,)),
         ],

time: 87.7 us -> 87.7 us (level)
  no operation moved by 1% of the time
where the time goes in v8:
time: 87.7 us; the launch traced here: 87.3 us
  starting transfers between devices  51.5 us (59%)
  waiting for transfers between devices  20.3 us (23%)
  Pallas kernels  15.2 us (17%)
    ppermute x11, starting transfers between devices, from_partner(): return lax.ppermute(block, axis, route)  51.5 us
    ppermute x11, waiting for transfers between devices, from_partner(): return lax.ppermute(block, axis, route)  20.3 us
    pallas_call x15, Pallas kernels, level_call(): pl.pallas_call(kernel, out_shape=jax.ShapeDtypeStruct((rows, CH), jnp.flo...  8.33 us
  transfers between devices with their start and end apart: 11, of which 6 were waited for; matrix products, arithmetic and copies ran while one was open for 0% of the time, Pallas kernels for 15%

profile of v8, /device:TPU:32, one launch (start us, length us, event | category | flops | bytes accessed | tf_op | source)
XLA Modules:
  0.0 87.3 jit_solution(1546325449328595690)
XLA Ops:
  0.0 1.1 %shard_map.46 = (f32[4,56,128]{2,1,0:T(8,128)S(1)}, f32[4,72,128]{2,1,0:T(8,128)S(1)}) custom-call(f32[2,4,2,128,128]{4,3,2,1,0:T(8,128)} %bitcast.14), custom_call_target="tpu_custom_call" | custom-call | flops 20000000000 | bytes 4194304 | tf_op jit(solution)/shard_map/pallas_call | solution.py:156
  1.2 5.2 %collective-permute-start.4 = (f32[224,128]{1,0:T(8,128)S(1)}, f32[224,128]{1,0:T(8,128)S(1)}, u32[]{:S(2)}, u32[]{:S(2)}) collective-permute-start(f32[224,128]{1,0:T(8,128)S(1)} %bitcast.10), channel_id=1, source_target_pairs={{0,256},{32,288},{64,320},{96,352},{128,384},{160,416},{192,448},{... | collective-permute-start | bytes 344072 | tf_op jit(solution)/shard_map/ppermute | solution.py:402
  6.4 2.2 %collective-permute-start.3 = (f32[288,128]{1,0:T(8,128)S(1)}, f32[288,128]{1,0:T(8,128)S(1)}, u32[]{:S(2)}, u32[]{:S(2)}) collective-permute-start(f32[288,128]{1,0:T(8,128)S(1)} %bitcast.9), channel_id=1, source_target_pairs={{0,256},{32,288},{64,320},{96,352},{128,384},{160,416},{192,448},{... | collective-permute-start | bytes 442376 | tf_op jit(solution)/shard_map/ppermute | solution.py:402
  10.0 3.5 %collective-permute-start.5 = (f32[224,128]{1,0:T(8,128)S(1)}, f32[224,128]{1,0:T(8,128)S(1)}, u32[]{:S(2)}, u32[]{:S(2)}) collective-permute-start(f32[224,128]{1,0:T(8,128)S(1)} %shard_map.48), channel_id=1, source_target_pairs={{0,16},{1,17},{2,18},{3,19},{4,20},{5,21},{6,22},{7,23},{8,24},{9,... | collective-permute-start | bytes 344072 | tf_op jit(solution)/shard_map/ppermute | solution.py:402
  13.8 1.3 %collective-permute-done.3.arr = f32[288,128]{1,0:T(8,128)S(1)} collective-permute-done((f32[288,128]{1,0:T(8,128)S(1)}, f32[288,128]{1,0:T(8,128)S(1)}, u32[]{:S(2)}, u32[]{:S(2)}) %collective-permute-start.3) | collective-permute-done | bytes 147488 | tf_op jit(solution)/shard_map/ppermute | solution.py:402
  15.5 2.6 %collective-permute-start.6 = (f32[288,128]{1,0:T(8,128)S(1)}, f32[288,128]{1,0:T(8,128)S(1)}, u32[]{:S(2)}, u32[]{:S(2)}) collective-permute-start(f32[288,128]{1,0:T(8,128)S(1)} %shard_map.50), channel_id=1, source_target_pairs={{0,16},{1,17},{2,18},{3,19},{4,20},{5,21},{6,22},{7,23},{8,24},{9,... | collective-permute-start | bytes 442376 | tf_op jit(solution)/shard_map/ppermute | solution.py:402
  18.5 4.9 %collective-permute-start.7 = (f32[224,128]{1,0:T(8,128)S(1)}, f32[224,128]{1,0:T(8,128)S(1)}, u32[]{:S(2)}, u32[]{:S(2)}) collective-permute-start(f32[224,128]{1,0:T(8,128)S(1)} %shard_map.51), channel_id=1, source_target_pairs={{0,128},{32,160},{64,192},{96,224},{128,0},{160,32},{192,64},{224,... | collective-permute-start | bytes 344072 | tf_op jit(solution)/shard_map/ppermute | solution.py:402
  24.3 3.6 %collective-permute-start.8 = (f32[288,128]{1,0:T(8,128)S(1)}, f32[288,128]{1,0:T(8,128)S(1)}, u32[]{:S(2)}, u32[]{:S(2)}) collective-permute-start(f32[288,128]{1,0:T(8,128)S(1)} %shard_map.54), channel_id=1, source_target_pairs={{0,128},{32,160},{64,192},{96,224},{128,0},{160,32},{192,64},{224,... | collective-permute-start | bytes 442376 | tf_op jit(solution)/shard_map/ppermute | solution.py:402
  28.9 14.8 %collective-permute-start.10 = (f32[448,128]{1,0:T(8,128)S(1)}, f32[448,128]{1,0:T(8,128)S(1)}, u32[]{:S(2)}, u32[]{:S(2)}) collective-permute-start(f32[448,128]{1,0:T(8,128)S(1)} %shard_map.55), channel_id=1, source_target_pairs={{0,8},{1,9},{2,10},{3,11},{4,12},{5,13},{6,14},{7,15},{8,0},{9,1},... | collective-permute-start | bytes 688136 | tf_op jit(solution)/shard_map/ppermute | solution.py:402
  44.1 0.9 shard_map.57
  45.0 3.5 %collective-permute-start.9 = (f32[576,128]{1,0:T(8,128)S(1)}, f32[576,128]{1,0:T(8,128)S(1)}, u32[]{:S(2)}, u32[]{:S(2)}) collective-permute-start(f32[576,128]{1,0:T(8,128)S(1)} %shard_map.57), channel_id=1, source_target_pairs={{0,8},{1,9},{2,10},{3,11},{4,12},{5,13},{6,14},{7,15},{8,0},{9,1},... | collective-permute-start | bytes 884744 | tf_op jit(solution)/shard_map/ppermute | solution.py:402
  48.5 30.4 %conditional.1 = (f32[1024,128]{1,0:T(8,128)S(1)}) conditional(s32[]{:T(128)} %convert_element_type.3, () %tuple.31, (f32[1,1,2048,128]{3,2,1,0:T(8,128)S(1)}, f32[512,128]{1,0:T(8,128)S(1)}, f32[2048,128]{1,0:T(8,128)S(1)}, bf16[8192,128]{1,0:T(8,128)(2,1)}) %tuple.41), branch_computations={%region_0.0_spmd, %region_1.0_spmd} | conditional | flops 20000000000 | bytes 41943196 | solution.py:522
  48.6 4.3 %collective-permute-start = (f32[512,128]{1,0:T(8,128)S(1)}, f32[512,128]{1,0:T(8,128)S(1)}, u32[]{:S(2)}, u32[]{:S(2)}) collective-permute-start(f32[512,128]{1,0:T(8,128)S(1)} %bitcast.8), channel_id=1, source_target_pairs={{0,256},{32,288},{64,320},{96,352},{128,384},{160,416},{192,448},{... | collective-permute-start | bytes 786440 | tf_op jit(solution)/shard_map/cond/branch_1_fun/ppermute | solution.py:402
  53.0 5.5 %collective-permute-done.arr = f32[512,128]{1,0:T(8,128)S(1)} collective-permute-done((f32[512,128]{1,0:T(8,128)S(1)}, f32[512,128]{1,0:T(8,128)S(1)}, u32[]{:S(2)}, u32[]{:S(2)}) %collective-permute-start) | collective-permute-done | bytes 262176 | tf_op jit(solution)/shard_map/cond/branch_1_fun/ppermute | solution.py:402
  59.1 3.3 %collective-permute-start.1 = (f32[512,128]{1,0:T(8,128)S(1)}, f32[512,128]{1,0:T(8,128)S(1)}, u32[]{:S(2)}, u32[]{:S(2)}) collective-permute-start(f32[512,128]{1,0:T(8,128)S(1)} %branch_1_fun.10), channel_id=1, source_target_pairs={{0,16},{1,17},{2,18},{3,19},{4,20},{5,21},{6,22},{7,23},{8,24},{9,... | collective-permute-start | bytes 786440 | tf_op jit(solution)/shard_map/cond/branch_1_fun/ppermute | solution.py:402
  63.0 4.4 %collective-permute-done.1.arr = f32[512,128]{1,0:T(8,128)S(1)} collective-permute-done((f32[512,128]{1,0:T(8,128)S(1)}, f32[512,128]{1,0:T(8,128)S(1)}, u32[]{:S(2)}, u32[]{:S(2)}) %collective-permute-start.1) | collective-permute-done | bytes 262176 | tf_op jit(solution)/shard_map/cond/branch_1_fun/ppermute | solution.py:402
  68.0 3.6 %collective-permute-start.2 = (f32[512,128]{1,0:T(8,128)S(1)}, f32[512,128]{1,0:T(8,128)S(1)}, u32[]{:S(2)}, u32[]{:S(2)}) collective-permute-start(f32[512,128]{1,0:T(8,128)S(1)} %branch_1_fun.12), channel_id=1, source_target_pairs={{0,128},{32,160},{64,192},{96,224},{128,0},{160,32},{192,64},{224,... | collective-permute-start | bytes 786440 | tf_op jit(solution)/shard_map/cond/branch_1_fun/ppermute | solution.py:402
  72.2 5.5 %collective-permute-done.2.arr = f32[512,128]{1,0:T(8,128)S(1)} collective-permute-done((f32[512,128]{1,0:T(8,128)S(1)}, f32[512,128]{1,0:T(8,128)S(1)}, u32[]{:S(2)}, u32[]{:S(2)}) %collective-permute-start.2) | collective-permute-done | bytes 262176 | tf_op jit(solution)/shard_map/cond/branch_1_fun/ppermute | solution.py:402
  77.7 1.2 %branch_1_fun.13 = f32[1024,128]{1,0:T(8,128)S(1)} custom-call(f32[512,128]{1,0:T(8,128)S(1)} %branch_1_fun.11.own, f32[512,128]{1,0:T(8,128)S(1)} %collective-permute-done.2.arr, bf16[8192,128]{1,0:T(8,128)(2,1)S(1)} %copy-done.1, bf16[256,512]{1,0:T(8,128)(2,1)S(1)} %get-tuple-element.20.high, bf16[256,512]{1,0:T(8,128)(2,1)S(1)} %get-tuple-element.21.low), custom_call_target="tpu_custom_call" | custom-call | bytes 8388608 | tf_op jit(solution)/shard_map/cond/branch_1_fun/pallas_call | solution.py:232
  79.0 1.1 %shard_map.58.ang = bf16[2048,128]{1,0:T(8,128)(2,1)S(1)} custom-call(bf16[8192,128]{1,0:T(8,128)(2,1)} %bitcast.12), custom_call_target="tpu_custom_call" | custom-call | bytes 1048576 | tf_op jit(solution)/shard_map/pallas_call | solution.py:252
  80.0 1.3 %shard_map.59 = (f32[1152,128]{1,0:T(8,128)S(1)}, f32[1152,128]{1,0:T(8,128)S(1)}, f32[1152,128]{1,0:T(8,128)S(1)}) custom-call(f32[1024,128]{1,0:T(8,128)S(1)} %get-tuple-element.70.own, bf16[2048,128]{1,0:T(8,128)(2,1)S(1)} %shard_map.58.ang, bf16[128,256]{1,0:T(8,128)(2,1)S(1)} %get-tuple-element.64.high, bf16[128,256]{1,0:T(8,128)(2,1)S(1)} %get-tuple-element.65.low), custom_call_target="tpu_custom_call" | custom-call | bytes 4194304 | tf_op jit(solution)/shard_map/pallas_call | solution.py:343
  81.3 1.7 %shard_map.60.rest_0_ = f32[2048,128]{1,0:T(8,128)} custom-call(f32[1024,128]{1,0:T(8,128)S(1)} %get-tuple-element.70.own, f32[448,128]{1,0:T(8,128)S(1)} %collective-permute-done.10.arr, bf16[2048,128]{1,0:T(8,128)(2,1)S(1)} %shard_map.58.ang, bf16[256,512]{1,0:T(8,128)(2,1)S(1)} %get-tuple-element.57.high, bf16[256,512]{1,0:T(8,128)(2,1)S(1)} %get-tuple-element.58.low), custom_call_target="tpu_custom_call" | custom-call | flops 1500000000 | bytes 3670016 | tf_op jit(solution)/shard_map/pallas_call | solution.py:286
  83.0 3.0 %collective-permute-done.9.arr = f32[576,128]{1,0:T(8,128)S(1)} collective-permute-done((f32[576,128]{1,0:T(8,128)S(1)}, f32[576,128]{1,0:T(8,128)S(1)}, u32[]{:S(2)}, u32[]{:S(2)}) %collective-permute-start.9) | collective-permute-done | bytes 294944 | tf_op jit(solution)/shard_map/ppermute | solution.py:402
  86.0 1.3 %shard_map.61 = f32[2048,128]{1,0:T(8,128)} custom-call(f32[576,128]{1,0:T(8,128)S(1)} %collective-permute-done.9.arr, f32[1152,128]{1,0:T(8,128)S(1)} %get-tuple-element.66.part, f32[1152,128]{1,0:T(8,128)S(1)} %get-tuple-element.67.cos_in, f32[1152,128]{1,0:T(8,128)S(1)} %get-tuple-element.68.sin_in, ...), custom_call_target="tpu_custom_call", output_to_operand_aliasing={{}: (6, {})} | custom-call | bytes 4718592 | tf_op jit(solution)/shard_map/pallas_call | solution.py:381
  (30 shorter events, 7.3 us)
Async XLA Ops:
  0.0 8.7 %copy-start = (bf16[4,1,1,2048,128]{4,3,2,1,0:T(8,128)(2,1)S(1)}, bf16[4,1,1,2048,128]{4,3,2,1,0:T(8,128)(2,1)}, u32[]{:S(2)}) copy-start(bf16[4,1,1,2048,128]{4,3,2,1,0:T(8,128)(2,1)} %param.7) | copy-start | bytes 6291460
  0.0 8.7 %copy-start.3 = (f32[512,128]{1,0:T(8,128)S(1)}, f32[512,128]{1,0:T(8,128)}, u32[]{:S(2)}) copy-start(f32[512,128]{1,0:T(8,128)} %constant.12.clone.blocks) | copy-start | bytes 786436
  1.1 8.4 %copy-start.2 = (f32[1,1,2048,128]{3,2,1,0:T(8,128)S(1)}, f32[1,1,2048,128]{3,2,1,0:T(8,128)}, u32[]{:S(2)}) copy-start(f32[1,1,2048,128]{3,2,1,0:T(8,128)} %param.6) | copy-start | bytes 3145732
  1.2 8.4 %collective-permute-start.4 = (f32[224,128]{1,0:T(8,128)S(1)}, f32[224,128]{1,0:T(8,128)S(1)}, u32[]{:S(2)}, u32[]{:S(2)}) collective-permute-start(f32[224,128]{1,0:T(8,128)S(1)} %bitcast.10), channel_id=1, source_target_pairs={{0,256},{32,288},{64,320},{96,352},{128,384},{160,416},{192,448},{... | collective-permute-start | bytes 344072 | tf_op jit(solution)/shard_map/ppermute | solution.py:402
  6.4 8.7 %collective-permute-start.3 = (f32[288,128]{1,0:T(8,128)S(1)}, f32[288,128]{1,0:T(8,128)S(1)}, u32[]{:S(2)}, u32[]{:S(2)}) collective-permute-start(f32[288,128]{1,0:T(8,128)S(1)} %bitcast.9), channel_id=1, source_target_pairs={{0,256},{32,288},{64,320},{96,352},{128,384},{160,416},{192,448},{... | collective-permute-start | bytes 442376 | tf_op jit(solution)/shard_map/ppermute | solution.py:402
  10.0 8.2 %collective-permute-start.5 = (f32[224,128]{1,0:T(8,128)S(1)}, f32[224,128]{1,0:T(8,128)S(1)}, u32[]{:S(2)}, u32[]{:S(2)}) collective-permute-start(f32[224,128]{1,0:T(8,128)S(1)} %shard_map.48), channel_id=1, source_target_pairs={{0,16},{1,17},{2,18},{3,19},{4,20},{5,21},{6,22},{7,23},{8,24},{9,... | collective-permute-start | bytes 344072 | tf_op jit(solution)/shard_map/ppermute | solution.py:402
  15.5 8.3 %collective-permute-start.6 = (f32[288,128]{1,0:T(8,128)S(1)}, f32[288,128]{1,0:T(8,128)S(1)}, u32[]{:S(2)}, u32[]{:S(2)}) collective-permute-start(f32[288,128]{1,0:T(8,128)S(1)} %shard_map.50), channel_id=1, source_target_pairs={{0,16},{1,17},{2,18},{3,19},{4,20},{5,21},{6,22},{7,23},{8,24},{9,... | collective-permute-start | bytes 442376 | tf_op jit(solution)/shard_map/ppermute | solution.py:402
  18.5 9.8 %collective-permute-start.7 = (f32[224,128]{1,0:T(8,128)S(1)}, f32[224,128]{1,0:T(8,128)S(1)}, u32[]{:S(2)}, u32[]{:S(2)}) collective-permute-start(f32[224,128]{1,0:T(8,128)S(1)} %shard_map.51), channel_id=1, source_target_pairs={{0,128},{32,160},{64,192},{96,224},{128,0},{160,32},{192,64},{224,... | collective-permute-start | bytes 344072 | tf_op jit(solution)/shard_map/ppermute | solution.py:402
  24.3 19.8 %collective-permute-start.8 = (f32[288,128]{1,0:T(8,128)S(1)}, f32[288,128]{1,0:T(8,128)S(1)}, u32[]{:S(2)}, u32[]{:S(2)}) collective-permute-start(f32[288,128]{1,0:T(8,128)S(1)} %shard_map.54), channel_id=1, source_target_pairs={{0,128},{32,160},{64,192},{96,224},{128,0},{160,32},{192,64},{224,... | collective-permute-start | bytes 442376 | tf_op jit(solution)/shard_map/ppermute | solution.py:402
  28.9 52.4 %collective-permute-start.10 = (f32[448,128]{1,0:T(8,128)S(1)}, f32[448,128]{1,0:T(8,128)S(1)}, u32[]{:S(2)}, u32[]{:S(2)}) collective-permute-start(f32[448,128]{1,0:T(8,128)S(1)} %shard_map.55), channel_id=1, source_target_pairs={{0,8},{1,9},{2,10},{3,11},{4,12},{5,13},{6,14},{7,15},{8,0},{9,1},... | collective-permute-start | bytes 688136 | tf_op jit(solution)/shard_map/ppermute | solution.py:402
  45.0 41.0 %collective-permute-start.9 = (f32[576,128]{1,0:T(8,128)S(1)}, f32[576,128]{1,0:T(8,128)S(1)}, u32[]{:S(2)}, u32[]{:S(2)}) collective-permute-start(f32[576,128]{1,0:T(8,128)S(1)} %shard_map.57), channel_id=1, source_target_pairs={{0,8},{1,9},{2,10},{3,11},{4,12},{5,13},{6,14},{7,15},{8,0},{9,1},... | collective-permute-start | bytes 884744 | tf_op jit(solution)/shard_map/ppermute | solution.py:402
  48.5 10.0 %copy-start.1 = (bf16[8192,128]{1,0:T(8,128)(2,1)S(1)}, bf16[8192,128]{1,0:T(8,128)(2,1)}, u32[]{:S(2)}) copy-start(bf16[8192,128]{1,0:T(8,128)(2,1)} %get-tuple-element.18.ang) | copy-start | bytes 6291460 | tf_op jit(solution)/shard_map/cond
  48.6 9.9 %collective-permute-start = (f32[512,128]{1,0:T(8,128)S(1)}, f32[512,128]{1,0:T(8,128)S(1)}, u32[]{:S(2)}, u32[]{:S(2)}) collective-permute-start(f32[512,128]{1,0:T(8,128)S(1)} %bitcast.8), channel_id=1, source_target_pairs={{0,256},{32,288},{64,320},{96,352},{128,384},{160,416},{192,448},{... | collective-permute-start | bytes 786440 | tf_op jit(solution)/shard_map/cond/branch_1_fun/ppermute | solution.py:402
  59.1 8.3 %collective-permute-start.1 = (f32[512,128]{1,0:T(8,128)S(1)}, f32[512,128]{1,0:T(8,128)S(1)}, u32[]{:S(2)}, u32[]{:S(2)}) collective-permute-start(f32[512,128]{1,0:T(8,128)S(1)} %branch_1_fun.10), channel_id=1, source_target_pairs={{0,16},{1,17},{2,18},{3,19},{4,20},{5,21},{6,22},{7,23},{8,24},{9,... | collective-permute-start | bytes 786440 | tf_op jit(solution)/shard_map/cond/branch_1_fun/ppermute | solution.py:402
  68.0 9.8 %collective-permute-start.2 = (f32[512,128]{1,0:T(8,128)S(1)}, f32[512,128]{1,0:T(8,128)S(1)}, u32[]{:S(2)}, u32[]{:S(2)}) collective-permute-start(f32[512,128]{1,0:T(8,128)S(1)} %branch_1_fun.12), channel_id=1, source_target_pairs={{0,128},{32,160},{64,192},{96,224},{128,0},{160,32},{192,64},{224,... | collective-permute-start | bytes 786440 | tf_op jit(solution)/shard_map/cond/branch_1_fun/ppermute | solution.py:402

commit v9 on v8

--- a/solution.py
+++ b/solution.py
@@ -375,7 +375,7 @@
 
 def last_call(arr, ready, table, row, earlier):
     rows = arr.shape[0]
-    tile = tile_of(rows)
+    tile = 96 if rows % 96 == 0 else tile_of(rows)
     count = rows // tile
     operands = [arr, *ready, *table, earlier]
     return pl.pallas_call(

time: 87.7 us -> 87.7 us (level)
  no operation moved by 1% of the time
where the time goes in v9:
time: 87.7 us; the launch traced here: 87.2 us
  starting transfers between devices  51.5 us (59%)
  waiting for transfers between devices  20.3 us (23%)
  Pallas kernels  15.2 us (17%)
    ppermute x11, starting transfers between devices, from_partner(): return lax.ppermute(block, axis, route)  51.5 us
    ppermute x11, waiting for transfers between devices, from_partner(): return lax.ppermute(block, axis, route)  20.3 us
    pallas_call x15, Pallas kernels, level_call(): pl.pallas_call(kernel, out_shape=jax.ShapeDtypeStruct((rows, CH), jnp.flo...  8.33 us
  transfers between devices with their start and end apart: 11, of which 6 were waited for; matrix products, arithmetic and copies ran while one was open for 0% of the time, Pallas kernels for 15%

profile of v9, /device:TPU:32, one launch (start us, length us, event | category | flops | bytes accessed | tf_op | source)
XLA Modules:
  0.0 87.2 jit_solution(8024285204706577219)
XLA Ops:
  0.0 1.1 %shard_map.46 = (f32[4,56,128]{2,1,0:T(8,128)S(1)}, f32[4,72,128]{2,1,0:T(8,128)S(1)}) custom-call(f32[2,4,2,128,128]{4,3,2,1,0:T(8,128)} %bitcast.14), custom_call_target="tpu_custom_call" | custom-call | flops 20000000000 | bytes 4194304 | tf_op jit(solution)/shard_map/pallas_call | solution.py:156
  1.2 5.2 %collective-permute-start.4 = (f32[224,128]{1,0:T(8,128)S(1)}, f32[224,128]{1,0:T(8,128)S(1)}, u32[]{:S(2)}, u32[]{:S(2)}) collective-permute-start(f32[224,128]{1,0:T(8,128)S(1)} %bitcast.10), channel_id=1, source_target_pairs={{0,256},{32,288},{64,320},{96,352},{128,384},{160,416},{192,448},{... | collective-permute-start | bytes 344072 | tf_op jit(solution)/shard_map/ppermute | solution.py:402
  6.4 2.2 %collective-permute-start.3 = (f32[288,128]{1,0:T(8,128)S(1)}, f32[288,128]{1,0:T(8,128)S(1)}, u32[]{:S(2)}, u32[]{:S(2)}) collective-permute-start(f32[288,128]{1,0:T(8,128)S(1)} %bitcast.9), channel_id=1, source_target_pairs={{0,256},{32,288},{64,320},{96,352},{128,384},{160,416},{192,448},{... | collective-permute-start | bytes 442376 | tf_op jit(solution)/shard_map/ppermute | solution.py:402
  10.0 3.5 %collective-permute-start.5 = (f32[224,128]{1,0:T(8,128)S(1)}, f32[224,128]{1,0:T(8,128)S(1)}, u32[]{:S(2)}, u32[]{:S(2)}) collective-permute-start(f32[224,128]{1,0:T(8,128)S(1)} %shard_map.48), channel_id=1, source_target_pairs={{0,16},{1,17},{2,18},{3,19},{4,20},{5,21},{6,22},{7,23},{8,24},{9,... | collective-permute-start | bytes 344072 | tf_op jit(solution)/shard_map/ppermute | solution.py:402
  13.8 1.3 %collective-permute-done.3.arr = f32[288,128]{1,0:T(8,128)S(1)} collective-permute-done((f32[288,128]{1,0:T(8,128)S(1)}, f32[288,128]{1,0:T(8,128)S(1)}, u32[]{:S(2)}, u32[]{:S(2)}) %collective-permute-start.3) | collective-permute-done | bytes 147488 | tf_op jit(solution)/shard_map/ppermute | solution.py:402
  15.5 2.6 %collective-permute-start.6 = (f32[288,128]{1,0:T(8,128)S(1)}, f32[288,128]{1,0:T(8,128)S(1)}, u32[]{:S(2)}, u32[]{:S(2)}) collective-permute-start(f32[288,128]{1,0:T(8,128)S(1)} %shard_map.50), channel_id=1, source_target_pairs={{0,16},{1,17},{2,18},{3,19},{4,20},{5,21},{6,22},{7,23},{8,24},{9,... | collective-permute-start | bytes 442376 | tf_op jit(solution)/shard_map/ppermute | solution.py:402
  18.5 4.9 %collective-permute-start.7 = (f32[224,128]{1,0:T(8,128)S(1)}, f32[224,128]{1,0:T(8,128)S(1)}, u32[]{:S(2)}, u32[]{:S(2)}) collective-permute-start(f32[224,128]{1,0:T(8,128)S(1)} %shard_map.51), channel_id=1, source_target_pairs={{0,128},{32,160},{64,192},{96,224},{128,0},{160,32},{192,64},{224,... | collective-permute-start | bytes 344072 | tf_op jit(solution)/shard_map/ppermute | solution.py:402
  24.3 3.6 %collective-permute-start.8 = (f32[288,128]{1,0:T(8,128)S(1)}, f32[288,128]{1,0:T(8,128)S(1)}, u32[]{:S(2)}, u32[]{:S(2)}) collective-permute-start(f32[288,128]{1,0:T(8,128)S(1)} %shard_map.54), channel_id=1, source_target_pairs={{0,128},{32,160},{64,192},{96,224},{128,0},{160,32},{192,64},{224,... | collective-permute-start | bytes 442376 | tf_op jit(solution)/shard_map/ppermute | solution.py:402
  28.9 14.8 %collective-permute-start.10 = (f32[448,128]{1,0:T(8,128)S(1)}, f32[448,128]{1,0:T(8,128)S(1)}, u32[]{:S(2)}, u32[]{:S(2)}) collective-permute-start(f32[448,128]{1,0:T(8,128)S(1)} %shard_map.55), channel_id=1, source_target_pairs={{0,8},{1,9},{2,10},{3,11},{4,12},{5,13},{6,14},{7,15},{8,0},{9,1},... | collective-permute-start | bytes 688136 | tf_op jit(solution)/shard_map/ppermute | solution.py:402
  44.1 0.9 shard_map.57
  45.0 3.5 %collective-permute-start.9 = (f32[576,128]{1,0:T(8,128)S(1)}, f32[576,128]{1,0:T(8,128)S(1)}, u32[]{:S(2)}, u32[]{:S(2)}) collective-permute-start(f32[576,128]{1,0:T(8,128)S(1)} %shard_map.57), channel_id=1, source_target_pairs={{0,8},{1,9},{2,10},{3,11},{4,12},{5,13},{6,14},{7,15},{8,0},{9,1},... | collective-permute-start | bytes 884744 | tf_op jit(solution)/shard_map/ppermute | solution.py:402
  48.5 30.4 %conditional.1 = (f32[1024,128]{1,0:T(8,128)S(1)}) conditional(s32[]{:T(128)} %convert_element_type.3, () %tuple.31, (f32[1,1,2048,128]{3,2,1,0:T(8,128)S(1)}, f32[512,128]{1,0:T(8,128)S(1)}, f32[2048,128]{1,0:T(8,128)S(1)}, bf16[8192,128]{1,0:T(8,128)(2,1)}) %tuple.41), branch_computations={%region_0.0_spmd, %region_1.0_spmd} | conditional | flops 20000000000 | bytes 41943196 | solution.py:522
  48.6 4.3 %collective-permute-start = (f32[512,128]{1,0:T(8,128)S(1)}, f32[512,128]{1,0:T(8,128)S(1)}, u32[]{:S(2)}, u32[]{:S(2)}) collective-permute-start(f32[512,128]{1,0:T(8,128)S(1)} %bitcast.8), channel_id=1, source_target_pairs={{0,256},{32,288},{64,320},{96,352},{128,384},{160,416},{192,448},{... | collective-permute-start | bytes 786440 | tf_op jit(solution)/shard_map/cond/branch_1_fun/ppermute | solution.py:402
  53.0 5.5 %collective-permute-done.arr = f32[512,128]{1,0:T(8,128)S(1)} collective-permute-done((f32[512,128]{1,0:T(8,128)S(1)}, f32[512,128]{1,0:T(8,128)S(1)}, u32[]{:S(2)}, u32[]{:S(2)}) %collective-permute-start) | collective-permute-done | bytes 262176 | tf_op jit(solution)/shard_map/cond/branch_1_fun/ppermute | solution.py:402
  59.1 3.3 %collective-permute-start.1 = (f32[512,128]{1,0:T(8,128)S(1)}, f32[512,128]{1,0:T(8,128)S(1)}, u32[]{:S(2)}, u32[]{:S(2)}) collective-permute-start(f32[512,128]{1,0:T(8,128)S(1)} %branch_1_fun.10), channel_id=1, source_target_pairs={{0,16},{1,17},{2,18},{3,19},{4,20},{5,21},{6,22},{7,23},{8,24},{9,... | collective-permute-start | bytes 786440 | tf_op jit(solution)/shard_map/cond/branch_1_fun/ppermute | solution.py:402
  63.0 4.4 %collective-permute-done.1.arr = f32[512,128]{1,0:T(8,128)S(1)} collective-permute-done((f32[512,128]{1,0:T(8,128)S(1)}, f32[512,128]{1,0:T(8,128)S(1)}, u32[]{:S(2)}, u32[]{:S(2)}) %collective-permute-start.1) | collective-permute-done | bytes 262176 | tf_op jit(solution)/shard_map/cond/branch_1_fun/ppermute | solution.py:402
  68.0 3.6 %collective-permute-start.2 = (f32[512,128]{1,0:T(8,128)S(1)}, f32[512,128]{1,0:T(8,128)S(1)}, u32[]{:S(2)}, u32[]{:S(2)}) collective-permute-start(f32[512,128]{1,0:T(8,128)S(1)} %branch_1_fun.12), channel_id=1, source_target_pairs={{0,128},{32,160},{64,192},{96,224},{128,0},{160,32},{192,64},{224,... | collective-permute-start | bytes 786440 | tf_op jit(solution)/shard_map/cond/branch_1_fun/ppermute | solution.py:402
  72.2 5.5 %collective-permute-done.2.arr = f32[512,128]{1,0:T(8,128)S(1)} collective-permute-done((f32[512,128]{1,0:T(8,128)S(1)}, f32[512,128]{1,0:T(8,128)S(1)}, u32[]{:S(2)}, u32[]{:S(2)}) %collective-permute-start.2) | collective-permute-done | bytes 262176 | tf_op jit(solution)/shard_map/cond/branch_1_fun/ppermute | solution.py:402
  77.7 1.2 %branch_1_fun.13 = f32[1024,128]{1,0:T(8,128)S(1)} custom-call(f32[512,128]{1,0:T(8,128)S(1)} %branch_1_fun.11.own, f32[512,128]{1,0:T(8,128)S(1)} %collective-permute-done.2.arr, bf16[8192,128]{1,0:T(8,128)(2,1)S(1)} %copy-done.1, bf16[256,512]{1,0:T(8,128)(2,1)S(1)} %get-tuple-element.20.high, bf16[256,512]{1,0:T(8,128)(2,1)S(1)} %get-tuple-element.21.low), custom_call_target="tpu_custom_call" | custom-call | bytes 8388608 | tf_op jit(solution)/shard_map/cond/branch_1_fun/pallas_call | solution.py:232
  79.0 1.1 %shard_map.58.ang = bf16[2048,128]{1,0:T(8,128)(2,1)S(1)} custom-call(bf16[8192,128]{1,0:T(8,128)(2,1)} %bitcast.12), custom_call_target="tpu_custom_call" | custom-call | bytes 1048576 | tf_op jit(solution)/shard_map/pallas_call | solution.py:252
  80.0 1.3 %shard_map.59 = (f32[1152,128]{1,0:T(8,128)S(1)}, f32[1152,128]{1,0:T(8,128)S(1)}, f32[1152,128]{1,0:T(8,128)S(1)}) custom-call(f32[1024,128]{1,0:T(8,128)S(1)} %get-tuple-element.70.own, bf16[2048,128]{1,0:T(8,128)(2,1)S(1)} %shard_map.58.ang, bf16[128,256]{1,0:T(8,128)(2,1)S(1)} %get-tuple-element.64.high, bf16[128,256]{1,0:T(8,128)(2,1)S(1)} %get-tuple-element.65.low), custom_call_target="tpu_custom_call" | custom-call | bytes 4194304 | tf_op jit(solution)/shard_map/pallas_call | solution.py:343
  81.3 1.7 %shard_map.60.rest_0_ = f32[2048,128]{1,0:T(8,128)} custom-call(f32[1024,128]{1,0:T(8,128)S(1)} %get-tuple-element.70.own, f32[448,128]{1,0:T(8,128)S(1)} %collective-permute-done.10.arr, bf16[2048,128]{1,0:T(8,128)(2,1)S(1)} %shard_map.58.ang, bf16[256,512]{1,0:T(8,128)(2,1)S(1)} %get-tuple-element.57.high, bf16[256,512]{1,0:T(8,128)(2,1)S(1)} %get-tuple-element.58.low), custom_call_target="tpu_custom_call" | custom-call | flops 1500000000 | bytes 3670016 | tf_op jit(solution)/shard_map/pallas_call | solution.py:286
  83.0 3.0 %collective-permute-done.9.arr = f32[576,128]{1,0:T(8,128)S(1)} collective-permute-done((f32[576,128]{1,0:T(8,128)S(1)}, f32[576,128]{1,0:T(8,128)S(1)}, u32[]{:S(2)}, u32[]{:S(2)}) %collective-permute-start.9) | collective-permute-done | bytes 294944 | tf_op jit(solution)/shard_map/ppermute | solution.py:402
  86.0 1.2 %shard_map.61 = f32[2048,128]{1,0:T(8,128)} custom-call(f32[576,128]{1,0:T(8,128)S(1)} %collective-permute-done.9.arr, f32[1152,128]{1,0:T(8,128)S(1)} %get-tuple-element.66.part, f32[1152,128]{1,0:T(8,128)S(1)} %get-tuple-element.67.cos_in, f32[1152,128]{1,0:T(8,128)S(1)} %get-tuple-element.68.sin_in, ...), custom_call_target="tpu_custom_call", output_to_operand_aliasing={{}: (6, {})} | custom-call | bytes 4718592 | tf_op jit(solution)/shard_map/pallas_call | solution.py:381
  (30 shorter events, 7.3 us)
Async XLA Ops:
  0.0 8.7 %copy-start = (bf16[4,1,1,2048,128]{4,3,2,1,0:T(8,128)(2,1)S(1)}, bf16[4,1,1,2048,128]{4,3,2,1,0:T(8,128)(2,1)}, u32[]{:S(2)}) copy-start(bf16[4,1,1,2048,128]{4,3,2,1,0:T(8,128)(2,1)} %param.7) | copy-start | bytes 6291460
  0.0 8.7 %copy-start.3 = (f32[512,128]{1,0:T(8,128)S(1)}, f32[512,128]{1,0:T(8,128)}, u32[]{:S(2)}) copy-start(f32[512,128]{1,0:T(8,128)} %constant.12.clone.blocks) | copy-start | bytes 786436
  1.1 8.4 %copy-start.2 = (f32[1,1,2048,128]{3,2,1,0:T(8,128)S(1)}, f32[1,1,2048,128]{3,2,1,0:T(8,128)}, u32[]{:S(2)}) copy-start(f32[1,1,2048,128]{3,2,1,0:T(8,128)} %param.6) | copy-start | bytes 3145732
  1.2 8.4 %collective-permute-start.4 = (f32[224,128]{1,0:T(8,128)S(1)}, f32[224,128]{1,0:T(8,128)S(1)}, u32[]{:S(2)}, u32[]{:S(2)}) collective-permute-start(f32[224,128]{1,0:T(8,128)S(1)} %bitcast.10), channel_id=1, source_target_pairs={{0,256},{32,288},{64,320},{96,352},{128,384},{160,416},{192,448},{... | collective-permute-start | bytes 344072 | tf_op jit(solution)/shard_map/ppermute | solution.py:402
  6.4 8.7 %collective-permute-start.3 = (f32[288,128]{1,0:T(8,128)S(1)}, f32[288,128]{1,0:T(8,128)S(1)}, u32[]{:S(2)}, u32[]{:S(2)}) collective-permute-start(f32[288,128]{1,0:T(8,128)S(1)} %bitcast.9), channel_id=1, source_target_pairs={{0,256},{32,288},{64,320},{96,352},{128,384},{160,416},{192,448},{... | collective-permute-start | bytes 442376 | tf_op jit(solution)/shard_map/ppermute | solution.py:402
  10.0 8.2 %collective-permute-start.5 = (f32[224,128]{1,0:T(8,128)S(1)}, f32[224,128]{1,0:T(8,128)S(1)}, u32[]{:S(2)}, u32[]{:S(2)}) collective-permute-start(f32[224,128]{1,0:T(8,128)S(1)} %shard_map.48), channel_id=1, source_target_pairs={{0,16},{1,17},{2,18},{3,19},{4,20},{5,21},{6,22},{7,23},{8,24},{9,... | collective-permute-start | bytes 344072 | tf_op jit(solution)/shard_map/ppermute | solution.py:402
  15.5 8.3 %collective-permute-start.6 = (f32[288,128]{1,0:T(8,128)S(1)}, f32[288,128]{1,0:T(8,128)S(1)}, u32[]{:S(2)}, u32[]{:S(2)}) collective-permute-start(f32[288,128]{1,0:T(8,128)S(1)} %shard_map.50), channel_id=1, source_target_pairs={{0,16},{1,17},{2,18},{3,19},{4,20},{5,21},{6,22},{7,23},{8,24},{9,... | collective-permute-start | bytes 442376 | tf_op jit(solution)/shard_map/ppermute | solution.py:402
  18.5 9.8 %collective-permute-start.7 = (f32[224,128]{1,0:T(8,128)S(1)}, f32[224,128]{1,0:T(8,128)S(1)}, u32[]{:S(2)}, u32[]{:S(2)}) collective-permute-start(f32[224,128]{1,0:T(8,128)S(1)} %shard_map.51), channel_id=1, source_target_pairs={{0,128},{32,160},{64,192},{96,224},{128,0},{160,32},{192,64},{224,... | collective-permute-start | bytes 344072 | tf_op jit(solution)/shard_map/ppermute | solution.py:402
  24.3 19.8 %collective-permute-start.8 = (f32[288,128]{1,0:T(8,128)S(1)}, f32[288,128]{1,0:T(8,128)S(1)}, u32[]{:S(2)}, u32[]{:S(2)}) collective-permute-start(f32[288,128]{1,0:T(8,128)S(1)} %shard_map.54), channel_id=1, source_target_pairs={{0,128},{32,160},{64,192},{96,224},{128,0},{160,32},{192,64},{224,... | collective-permute-start | bytes 442376 | tf_op jit(solution)/shard_map/ppermute | solution.py:402
  28.9 52.4 %collective-permute-start.10 = (f32[448,128]{1,0:T(8,128)S(1)}, f32[448,128]{1,0:T(8,128)S(1)}, u32[]{:S(2)}, u32[]{:S(2)}) collective-permute-start(f32[448,128]{1,0:T(8,128)S(1)} %shard_map.55), channel_id=1, source_target_pairs={{0,8},{1,9},{2,10},{3,11},{4,12},{5,13},{6,14},{7,15},{8,0},{9,1},... | collective-permute-start | bytes 688136 | tf_op jit(solution)/shard_map/ppermute | solution.py:402
  45.0 41.0 %collective-permute-start.9 = (f32[576,128]{1,0:T(8,128)S(1)}, f32[576,128]{1,0:T(8,128)S(1)}, u32[]{:S(2)}, u32[]{:S(2)}) collective-permute-start(f32[576,128]{1,0:T(8,128)S(1)} %shard_map.57), channel_id=1, source_target_pairs={{0,8},{1,9},{2,10},{3,11},{4,12},{5,13},{6,14},{7,15},{8,0},{9,1},... | collective-permute-start | bytes 884744 | tf_op jit(solution)/shard_map/ppermute | solution.py:402
  48.5 10.0 %copy-start.1 = (bf16[8192,128]{1,0:T(8,128)(2,1)S(1)}, bf16[8192,128]{1,0:T(8,128)(2,1)}, u32[]{:S(2)}) copy-start(bf16[8192,128]{1,0:T(8,128)(2,1)} %get-tuple-element.18.ang) | copy-start | bytes 6291460 | tf_op jit(solution)/shard_map/cond
  48.6 9.9 %collective-permute-start = (f32[512,128]{1,0:T(8,128)S(1)}, f32[512,128]{1,0:T(8,128)S(1)}, u32[]{:S(2)}, u32[]{:S(2)}) collective-permute-start(f32[512,128]{1,0:T(8,128)S(1)} %bitcast.8), channel_id=1, source_target_pairs={{0,256},{32,288},{64,320},{96,352},{128,384},{160,416},{192,448},{... | collective-permute-start | bytes 786440 | tf_op jit(solution)/shard_map/cond/branch_1_fun/ppermute | solution.py:402
  59.1 8.3 %collective-permute-start.1 = (f32[512,128]{1,0:T(8,128)S(1)}, f32[512,128]{1,0:T(8,128)S(1)}, u32[]{:S(2)}, u32[]{:S(2)}) collective-permute-start(f32[512,128]{1,0:T(8,128)S(1)} %branch_1_fun.10), channel_id=1, source_target_pairs={{0,16},{1,17},{2,18},{3,19},{4,20},{5,21},{6,22},{7,23},{8,24},{9,... | collective-permute-start | bytes 786440 | tf_op jit(solution)/shard_map/cond/branch_1_fun/ppermute | solution.py:402
  68.0 9.8 %collective-permute-start.2 = (f32[512,128]{1,0:T(8,128)S(1)}, f32[512,128]{1,0:T(8,128)S(1)}, u32[]{:S(2)}, u32[]{:S(2)}) collective-permute-start(f32[512,128]{1,0:T(8,128)S(1)} %branch_1_fun.12), channel_id=1, source_target_pairs={{0,128},{32,160},{64,192},{96,224},{128,0},{160,32},{192,64},{224,... | collective-permute-start | bytes 786440 | tf_op jit(solution)/shard_map/cond/branch_1_fun/ppermute | solution.py:402
